TPU v7x, 32 devices: a whole 2x2x4 slice. The times are simulated.
32 devices in a mesh: dp: 16 (over z, x, core), blk: 2 (over y).
Axes of the slice: x: 2, y: 2, z: 4, core: 2. Of those that a mesh axis runs over, the one named last changes fastest.
Arguments:
- tokens: bfloat16 [4, 16, 1024, 768], P(None, 'dp', 'blk'), may hold values from -6 to 6
- lengths: int32 [4, 16], P(None, 'dp'), may hold values from 50 to 1024, as said below
- norm1_gain: bfloat16 [768], P(('dp', 'blk')), may hold values from 0.25 to 1.75
- w_query: bfloat16 [768, 768], P(('dp', 'blk')), may hold values from -0.21875 to 0.21875
- w_key: bfloat16 [768, 768], P(('dp', 'blk')), may hold values from -0.21875 to 0.21875
- w_value: bfloat16 [768, 768], P(('dp', 'blk')), may hold values from -0.21875 to 0.21875
- w_out: bfloat16 [768, 768], P(('dp', 'blk')), may hold values from -2.5 to 2.5
- rel_table: float32 [32, 12], replicated, may hold values from -3 to 3
- norm2_gain: bfloat16 [768], P(('dp', 'blk')), may hold values from 0.25 to 1.75
- w_in: bfloat16 [768, 3072], P(('dp', 'blk')), may hold values from -0.21875 to 0.21875
- w_down: bfloat16 [768, 3072], P(('dp', 'blk')), may hold values from -0.109375 to 0.109375
- cotangent: bfloat16 [4, 16, 1024, 768], P(None, 'dp', 'blk'), may hold values from -6 to 6
Outputs:
- mixed: bfloat16 [4, 16, 1024, 768], P(None, 'dp', 'blk')
- grad_tokens: bfloat16 [4, 16, 1024, 768], P(None, 'dp', 'blk')
- grad_norm1: float32 [768], P(('dp', 'blk'))
- grad_query: float32 [768, 768], P(('dp', 'blk'))
- grad_key: float32 [768, 768], P(('dp', 'blk'))
- grad_value: float32 [768, 768], P(('dp', 'blk'))
- grad_out: float32 [768, 768], P(('dp', 'blk'))
- grad_table: float32 [32, 12], replicated
- grad_norm2: float32 [768], P(('dp', 'blk'))
- grad_in: float32 [768, 3072], P(('dp', 'blk'))
- grad_down: float32 [768, 3072], P(('dp', 'blk'))
Inputs may be any that keep to these rules, and one draw needn't show every extreme that they name: `lengths`: in each index of dp, at least one of its 4 documents has length 1024; which one is drawn.
All inputs are finite; a program needn't handle non-finite values.
Results may differ from a plain program's by a relative error of at most 0.035.
Values may be sent and summed in bfloat16 or wider, within the bound.
A program may use at most 448 MiB of HBM per device.

v0:
```python
import jax
import jax.numpy as jnp
from jax import lax
from jax.sharding import PartitionSpec as P

EPS = 1e-06
NEG = -1e30
HIGH = lax.Precision.HIGHEST
LIMITS = (12, 16, 23, 32, 46, 64, 91)


def bucket_of(relative):
    distance = jnp.abs(relative)
    far_bucket = 8 + sum(((distance >= border).astype(jnp.int32) for border in LIMITS))
    bucket = jnp.where(distance < 8, distance, far_bucket)
    return bucket + 16 * (relative > 0).astype(jnp.int32)


def far_label(bucket_count, query_place, key_place):
    after = key_place[0] > query_place[0]
    spacing = jnp.where(after, key_place[0] - query_place[-1], query_place[0] - key_place[-1])
    distant = spacing > LIMITS[-1]
    label = jnp.where(after, 31, 15)
    selector = (jnp.arange(bucket_count, dtype=jnp.int32) == label).astype(jnp.float32)
    return (distant, selector)


def near_onehot(bucket_count, query_place, key_place):
    labels = bucket_of(key_place[None, :] - query_place[:, None])
    return (labels[:, :, None] == jnp.arange(bucket_count, dtype=jnp.int32)).astype(jnp.float32)


def bias_block(bias_table, query_place, key_place):
    bucket_count, head_count = bias_table.shape
    distant, selector = far_label(bucket_count, query_place, key_place)

    def far_bias():
        head_bias = jnp.sum(selector[:, None] * bias_table, 0)
        return jnp.broadcast_to(
            head_bias[:, None, None], (head_count, query_place.shape[0], key_place.shape[0])
        )

    def near_bias():
        onehot = near_onehot(bucket_count, query_place, key_place)
        return jnp.einsum("qkn,nh->hqk", onehot, bias_table, precision=HIGH)

    return lax.cond(distant, far_bias, near_bias)


def table_grad(score_grad, bias_table, query_place, key_place):
    bucket_count = bias_table.shape[0]
    distant, selector = far_label(bucket_count, query_place, key_place)

    def far_grad():
        return selector[:, None] * jnp.sum(score_grad, (0, 2, 3))[None, :]

    def near_grad():
        onehot = near_onehot(bucket_count, query_place, key_place)
        return jnp.einsum("bhqk,qkn->nh", score_grad, onehot, precision=HIGH)

    return lax.cond(distant, far_grad, near_grad)


def norm_rows(vector):
    inverse = lax.rsqrt(jnp.mean(vector * vector, -1, keepdims=True) + EPS)
    return (vector * inverse, inverse)


def norm_back(gradient, normed, inverse, gain_row):
    scaled = gradient * gain_row
    inner_mean = jnp.mean(scaled * normed, -1, keepdims=True)
    return (inverse * (scaled - normed * inner_mean), jnp.sum(gradient * normed, (0, 1)))


def project(left_side, weight):
    return jnp.einsum("bsd,de->bse", left_side, weight, preferred_element_type=jnp.float32)


def project_back(left_side, weight):
    return jnp.einsum("bse,de->bsd", left_side, weight, preferred_element_type=jnp.float32)


def outer_sum(left_side, right_side):
    return jnp.einsum("bsd,bse->de", left_side, right_side, preferred_element_type=jnp.float32)


def split_heads(tensor, head_count):
    return tensor.reshape(tensor.shape[0], tensor.shape[1], head_count, -1)


def masked_scores(
    query_heads, key_heads, bias_table, query_place, key_place, doc_length, score_scale
):
    pos_bias = bias_block(bias_table, query_place, key_place)
    raw_score = jnp.einsum(
        "bqhd,bkhd->bhqk", query_heads, key_heads, preferred_element_type=jnp.float32
    )
    key_live = key_place[None, :] < doc_length[:, None]
    return jnp.where(key_live[:, None, None, :], raw_score * score_scale + pos_bias[None], NEG)


def block_grads(
    query_heads,
    grad_heads,
    log_total,
    row_delta,
    query_place,
    key_heads,
    value_heads,
    key_place,
    bias_table,
    doc_length,
    score_scale,
):
    scores = masked_scores(
        query_heads, key_heads, bias_table, query_place, key_place, doc_length, score_scale
    )
    probability = jnp.exp(scores - log_total[..., None])
    prob_grad = jnp.einsum(
        "bqhd,bkhd->bhqk", grad_heads, value_heads, preferred_element_type=jnp.float32
    )
    score_grad = probability * (prob_grad - row_delta[..., None])
    raw_grad = (score_grad * score_scale).astype(jnp.bfloat16)
    dquery = jnp.einsum("bhqk,bkhd->bqhd", raw_grad, key_heads, preferred_element_type=jnp.float32)
    key_grad = jnp.einsum(
        "bhqk,bqhd->bkhd", raw_grad, query_heads, preferred_element_type=jnp.float32
    )
    dvalue = jnp.einsum(
        "bhqk,bqhd->bkhd",
        probability.astype(jnp.bfloat16),
        grad_heads,
        preferred_element_type=jnp.float32,
    )
    dtable = table_grad(score_grad, bias_table, query_place, key_place)
    return (dquery, key_grad, dvalue, dtable)


def body(
    tokens,
    lengths,
    norm1_gain,
    w_query,
    w_key,
    w_value,
    w_out,
    rel_table,
    norm2_gain,
    w_in,
    w_down,
    cotangent,
):
    micro_count, doc_count, block_rows, model_width = tokens.shape
    seq_count = micro_count * doc_count
    head_count = rel_table.shape[1]
    head_width = model_width // head_count
    score_scale = head_width ** (-0.5)
    gathered = (
        lax.all_gather(norm1_gain, ("dp", "blk"), axis=0, tiled=True),
        lax.all_gather(w_query, ("dp", "blk"), axis=0, tiled=True),
        lax.all_gather(w_key, ("dp", "blk"), axis=0, tiled=True),
        lax.all_gather(w_value, ("dp", "blk"), axis=0, tiled=True),
        lax.all_gather(w_out, ("dp", "blk"), axis=0, tiled=True),
        lax.all_gather(norm2_gain, ("dp", "blk"), axis=0, tiled=True),
        lax.all_gather(w_in, ("dp", "blk"), axis=0, tiled=True),
        lax.all_gather(w_down, ("dp", "blk"), axis=0, tiled=True),
    )
    gain_first = gathered[0].astype(jnp.float32)
    query_full, key_full, value_full, out_full = (
        gathered[1],
        gathered[2],
        gathered[3],
        gathered[4],
    )
    gain_second = gathered[5].astype(jnp.float32)
    in_full, down_full = (gathered[6], gathered[7])
    inputs = tokens.reshape(seq_count, block_rows, model_width).astype(jnp.float32)
    doc_length = lengths.reshape(seq_count)
    query_place = lax.axis_index("blk") * block_rows + jnp.arange(block_rows, dtype=jnp.int32)
    row_valid = (query_place[None, :] < doc_length[:, None]).astype(jnp.bfloat16)
    normed_in, inverse_in = norm_rows(inputs)
    normed_low = (normed_in * gain_first).astype(jnp.bfloat16)
    query_rows = project(normed_low, query_full).astype(jnp.bfloat16)
    key_rows = project(normed_low, key_full).astype(jnp.bfloat16)
    value_rows = project(normed_low, value_full).astype(jnp.bfloat16)
    query_heads = split_heads(query_rows, head_count)
    position = jnp.int32(0)
    row_max = jnp.full((seq_count, head_count, block_rows), NEG, jnp.float32)
    row_total = jnp.zeros((seq_count, head_count, block_rows), jnp.float32)
    weighted = jnp.zeros((seq_count, head_count, block_rows, head_width), jnp.float32)
    key_part = lax.all_gather(key_rows, "blk", axis=1, tiled=True)
    value_part = lax.all_gather(value_rows, "blk", axis=1, tiled=True)
    for block_index in range(key_part.shape[1] // block_rows):
        offset = block_index * block_rows
        key_block = split_heads(key_part[:, offset : offset + block_rows], head_count)
        value_block = split_heads(value_part[:, offset : offset + block_rows], head_count)
        key_place = position + offset + jnp.arange(block_rows, dtype=jnp.int32)
        scores = masked_scores(
            query_heads, key_block, rel_table, query_place, key_place, doc_length, score_scale
        )
        new_max = jnp.maximum(row_max, jnp.max(scores, -1))
        factor = jnp.exp(row_max - new_max)
        weight = jnp.exp(scores - new_max[..., None])
        row_total = row_total * factor + jnp.sum(weight, -1)
        weighted = weighted * factor[..., None] + jnp.einsum(
            "bhqk,bkhd->bhqd",
            weight.astype(jnp.bfloat16),
            value_block,
            preferred_element_type=jnp.float32,
        )
        row_max = new_max
    row_max, row_total, weighted = (row_max, row_total, weighted)
    log_total = row_max + jnp.log(row_total)
    attended = jnp.transpose(weighted / row_total[..., None], (0, 2, 1, 3))
    heads_out = attended.reshape(seq_count, block_rows, model_width).astype(jnp.bfloat16)
    residual_mid = inputs + project(heads_out, out_full)
    normed_mid, inverse_mid = norm_rows(residual_mid)
    mid_low = (normed_mid * gain_second).astype(jnp.bfloat16)
    up_proj = project(mid_low, in_full)
    activated = jax.nn.gelu(up_proj).astype(jnp.bfloat16)
    final_rows = residual_mid + jnp.einsum(
        "bsf,df->bsd", activated, down_full, preferred_element_type=jnp.float32
    )
    mixed = final_rows.astype(jnp.bfloat16).reshape(tokens.shape)
    out_grad = cotangent.reshape(seq_count, block_rows, model_width) * row_valid[:, :, None]
    grad_down = jnp.einsum("bsd,bsf->df", out_grad, activated, preferred_element_type=jnp.float32)
    act_grad = jnp.einsum("bsd,df->bsf", out_grad, down_full, preferred_element_type=jnp.float32)
    _, gelu_back = jax.vjp(jax.nn.gelu, up_proj)
    up_grad = gelu_back(act_grad)[0].astype(jnp.bfloat16)
    grad_in = outer_sum(mid_low, up_grad)
    mid_grad_n = jnp.einsum("bsf,df->bsd", up_grad, in_full, preferred_element_type=jnp.float32)
    mid_norm_grad, grad_second = norm_back(mid_grad_n, normed_mid, inverse_mid, gain_second)
    mid_grad = out_grad.astype(jnp.float32) + mid_norm_grad
    mid_grad_low = mid_grad.astype(jnp.bfloat16)
    grad_outw = outer_sum(heads_out, mid_grad_low)
    heads_grad = project_back(mid_grad_low, out_full).astype(jnp.bfloat16)
    grad_heads = split_heads(heads_grad, head_count)
    row_delta = jnp.sum(grad_heads.astype(jnp.float32) * attended, -1)
    delta_heads = jnp.transpose(row_delta, (0, 2, 1))
    cycle_rows = block_rows * lax.axis_size("blk")
    position = jnp.int32(0)
    query_acc = jnp.zeros((seq_count, block_rows, head_count, head_width), jnp.float32)
    key_all = jnp.zeros((seq_count, cycle_rows, model_width), jnp.float32)
    value_all = jnp.zeros((seq_count, cycle_rows, model_width), jnp.float32)
    table_acc = jnp.zeros(rel_table.shape, jnp.float32)
    key_part = lax.all_gather(key_rows, "blk", axis=1, tiled=True)
    value_part = lax.all_gather(value_rows, "blk", axis=1, tiled=True)
    for block_index in range(key_part.shape[1] // block_rows):
        offset = block_index * block_rows
        key_block = split_heads(key_part[:, offset : offset + block_rows], head_count)
        value_block = split_heads(value_part[:, offset : offset + block_rows], head_count)
        key_place = position + offset + jnp.arange(block_rows, dtype=jnp.int32)
        dquery, key_grad, dvalue, dtable = block_grads(
            query_heads,
            grad_heads,
            log_total,
            delta_heads,
            query_place,
            key_block,
            value_block,
            key_place,
            rel_table,
            doc_length,
            score_scale,
        )
        row_start = position + offset
        key_now = lax.dynamic_slice_in_dim(key_all, row_start, block_rows, 1)
        key_all = lax.dynamic_update_slice_in_dim(
            key_all, key_now + key_grad.reshape(seq_count, block_rows, model_width), row_start, 1
        )
        value_now = lax.dynamic_slice_in_dim(value_all, row_start, block_rows, 1)
        value_all = lax.dynamic_update_slice_in_dim(
            value_all, value_now + dvalue.reshape(seq_count, block_rows, model_width), row_start, 1
        )
        query_acc = query_acc + dquery
        table_acc = table_acc + dtable
    query_acc, key_all, value_all, table_acc = (query_acc, key_all, value_all, table_acc)
    key_sum, value_sum = (
        lax.psum_scatter(
            key_all.astype(jnp.bfloat16), "blk", scatter_dimension=1, tiled=True
        ).astype(jnp.float32),
        lax.psum_scatter(
            value_all.astype(jnp.bfloat16), "blk", scatter_dimension=1, tiled=True
        ).astype(jnp.float32),
    )
    query_grad_rows = query_acc.reshape(seq_count, block_rows, model_width)
    query_low = query_grad_rows.astype(jnp.bfloat16)
    key_low = key_sum.astype(jnp.bfloat16)
    value_low = value_sum.astype(jnp.bfloat16)
    grad_q = outer_sum(normed_low, query_low)
    grad_k = outer_sum(normed_low, key_low)
    grad_v = outer_sum(normed_low, value_low)
    in_grad_n = (
        project_back(query_low, query_full)
        + project_back(key_low, key_full)
        + project_back(value_low, value_full)
    )
    input_norm_grad, grad_first = norm_back(in_grad_n, normed_in, inverse_in, gain_first)
    grad_tokens = (mid_grad + input_norm_grad).astype(jnp.bfloat16).reshape(tokens.shape)
    reduced = (
        lax.psum_scatter(grad_first, ("dp", "blk"), scatter_dimension=0, tiled=True),
        lax.psum_scatter(grad_q, ("dp", "blk"), scatter_dimension=0, tiled=True),
        lax.psum_scatter(grad_k, ("dp", "blk"), scatter_dimension=0, tiled=True),
        lax.psum_scatter(grad_v, ("dp", "blk"), scatter_dimension=0, tiled=True),
        lax.psum_scatter(grad_outw, ("dp", "blk"), scatter_dimension=0, tiled=True),
        lax.psum_scatter(grad_second, ("dp", "blk"), scatter_dimension=0, tiled=True),
        lax.psum_scatter(grad_in, ("dp", "blk"), scatter_dimension=0, tiled=True),
        lax.psum_scatter(grad_down, ("dp", "blk"), scatter_dimension=0, tiled=True),
    )
    grad_table = lax.psum(table_acc, ("dp", "blk"))
    return (
        mixed,
        grad_tokens,
        reduced[0],
        reduced[1],
        reduced[2],
        reduced[3],
        reduced[4],
        grad_table,
        reduced[5],
        reduced[6],
        reduced[7],
    )


def solution(mesh):
    placed = (
        P(None, "dp", "blk", None),
        P(None, "dp"),
        P(("dp", "blk")),
        P(("dp", "blk"), None),
        P(("dp", "blk"), None),
        P(("dp", "blk"), None),
        P(("dp", "blk"), None),
        P(),
        P(("dp", "blk")),
        P(("dp", "blk"), None),
        P(("dp", "blk"), None),
        P(None, "dp", "blk", None),
    )
    return jax.shard_map(
        body,
        mesh=mesh,
        in_specs=placed,
        out_specs=(
            P(None, "dp", "blk", None),
            P(None, "dp", "blk", None),
            P(("dp", "blk")),
            P(("dp", "blk"), None),
            P(("dp", "blk"), None),
            P(("dp", "blk"), None),
            P(("dp", "blk"), None),
            P(),
            P(("dp", "blk")),
            P(("dp", "blk"), None),
            P(("dp", "blk"), None),
        ),
        check_vma=False,
    )
```

profile of v0, /device:TPU:0, one launch (start us, length us, event | category | flops | bytes accessed | tf_op | source)
XLA Modules:
  0.0 1582.1 jit_solution(17091688883945063884)
XLA Ops:
  11.1 42.1 %all-reduce.5 = (bf16[768]{0:T(1024)(128)(2,1)S(1)}, bf16[768]{0:T(1024)(128)(2,1)S(1)}) all-reduce(bf16[768]{0:T(1024)(128)(2,1)S(1)} %dynamic-update-slice, bf16[768]{0:T(1024)(128)(2,1)S(1)} %dynamic-update-slice.1), channel_id=1, replica_groups=mesh['dp'=16,'blk'=2] {'dp','blk'}, use_global_device_ids=true, to_apply=%add | all-reduce | flops 1536 | bytes 6144
  74.5 49.4 %all-gather.15.cloned.1.call-done = bf16[768,768]{1,0:T(8,128)(2,1)} async-done(((bf16[24,768]{1,0:T(8,128)(2,1)}), bf16[768,768]{1,0:T(8,128)(2,1)}) %all-gather.15.cloned.1.call-update) | async-done | bytes 1179664 | tf_op jit(solution)/shard_map/all_gather | solution.py:161
  216.9 44.3 %all-gather.13.cloned.1.call-done = bf16[4,1024,768]{2,1,0:T(8,128)(2,1)} async-done(((bf16[4,512,768]{2,1,0:T(8,128)(2,1)}), bf16[4,1024,768]{2,1,0:T(8,128)(2,1)}) %all-gather.13.cloned.1.call-update) | async-done | bytes 6291472 | tf_op jit(solution)/shard_map/all_gather | solution.py:190
  276.9 25.0 %fusion.166 = (f32[4,12,512]{2,1,0:T(8,128)S(1)}, f32[4,12,512,512]{2,3,1,0:T(8,128)}) fusion(f32[12,512,512]{1,2,0:T(8,128)} %copy.152, bf16[4,512,12,64]{1,3,2,0:T(8,128)(2,1)S(1)} %bitcast.234, bf16[4,512,12,64]{1,3,2,0:T(8,128)(2,1)} %bitcast.244, pred[4,512]{1,0:T(4,128)(4,1)S(1)} %get-tuple-element.202), kind=kOutput, calls=%fused_computation.215 | convolution fusion | flops 1660919808 | bytes 69306368 | tf_op jit(solution)/shard_map/bqhd,bkhd->bhqk/dot_general | solution.py:95
  301.9 24.7 %fusion.165 = (f32[4,12,512]{2,1,0:T(8,128)S(1)}, f32[4,12,512,512]{2,3,1,0:T(8,128)}) fusion(f32[12,512,512]{1,2,0:T(8,128)} %copy.148, bf16[4,512,12,64]{1,3,2,0:T(8,128)(2,1)S(1)} %bitcast.235, bf16[4,512,12,64]{1,3,2,0:T(8,128)(2,1)} %bitcast.242, pred[4,512]{1,0:T(4,128)(4,1)S(1)} %get-tuple-element.203), kind=kOutput, calls=%fused_computation.214 | convolution fusion | flops 1660919808 | bytes 69306368 | tf_op jit(solution)/shard_map/bqhd,bkhd->bhqk/dot_general | solution.py:95
  326.6 19.9 %fusion.52 = f32[4,12,512]{2,1,0:T(8,128)} fusion(f32[4,12,512,512]{2,3,1,0:T(8,128)} %get-tuple-element.205, f32[4,12,512]{2,1,0:T(8,128)S(1)} %get-tuple-element.195), kind=kLoop, calls=%fused_computation.78 | loop fusion | flops 25141248 | bytes 50528256 | tf_op jit(solution)/shard_map/reduce_sum | solution.py:203
  346.5 19.9 %fusion.54 = f32[4,12,512]{2,1,0:T(8,128)} fusion(f32[4,12,512,512]{2,3,1,0:T(8,128)} %get-tuple-element.207, f32[4,12,512]{2,1,0:T(8,128)S(1)} %get-tuple-element.196), kind=kLoop, calls=%fused_computation.80 | loop fusion | flops 25141248 | bytes 50528256 | tf_op jit(solution)/shard_map/reduce_sum | solution.py:203
  378.7 21.6 %fusion.69 = f32[4,12,512,64]{2,3,1,0:T(8,128)} fusion(bf16[4,512,12,64]{1,3,2,0:T(8,128)(2,1)S(1)} %bitcast.240, f32[4,12,512,512]{2,3,1,0:T(8,128)} %get-tuple-element.207, f32[4,12,512]{2,1,0:T(8,128)} %copy-done.11), kind=kOutput, calls=%fused_computation.95 | convolution fusion | flops 1635778560 | bytes 59867136 | tf_op jit(solution)/shard_map/bhqk,bkhd->bhqd/dot_general | solution.py:204
  400.3 24.5 %fusion.167 = (bf16[4,512,12,64]{1,3,2,0:T(8,128)(2,1)}, f32[4,512,12,64]{1,3,2,0:T(8,128)}) fusion(f32[4,512,12]{1,2,0:T(8,128)S(1)} %get-tuple-element.193, f32[4,12,512,64]{2,3,1,0:T(8,128)} %fusion.69, f32[4,512,12]{1,2,0:T(8,128)S(1)} %get-tuple-element.192, bf16[4,512,12,64]{1,3,2,0:T(8,128)(2,1)S(1)} %bitcast.239, ...), kind=kOutput, calls=%fused_computation.216 | convolution fusion | flops 1643642880 | bytes 69599232 | tf_op jit(solution)/shard_map/bhqk,bkhd->bhqd/dot_general | solution.py:204
  432.6 32.9 %all-gather.21.cloned.1.call-done = bf16[768,3072]{1,0:T(8,128)(2,1)} async-done(((bf16[24,3072]{1,0:T(8,128)(2,1)}), bf16[768,3072]{1,0:T(8,128)(2,1)}) %all-gather.21.cloned.1.call-update) | async-done | bytes 4718608 | tf_op jit(solution)/shard_map/all_gather | solution.py:164
  483.7 47.2 %all-gather.23.cloned.1.call-done = bf16[768,3072]{1,0:T(8,128)(2,1)} async-done(((bf16[24,3072]{1,0:T(8,128)(2,1)}), bf16[768,3072]{1,0:T(8,128)(2,1)}) %all-gather.23.cloned.1.call-update) | async-done | bytes 4718608 | tf_op jit(solution)/shard_map/all_gather | solution.py:165
  531.0 29.6 %fusion.64 = bf16[4,512,3072]{2,1,0:T(8,128)(2,1)} fusion(f32[4,512,3072]{2,1,0:T(8,128)} %fusion.108, bf16[768,3072]{1,0:T(8,128)(2,1)} %all-gather.23.cloned.1.call-done, bf16[4,1,512,768]{3,2,1,0:T(8,128)(2,1)} %param.31, bf16[4,512]{1,0:T(4,128)(2,1)S(1)} %copy-done.26), kind=kOutput, calls=%fused_computation.92 | convolution fusion | flops 9791078400 | bytes 45617152 | tf_op jit(solution)/shard_map/bsd,df->bsf/dot_general | solution.py:226
  594.1 33.9 %subtract_multiply_fusion = f32[4,12,512,512]{2,3,1,0:T(8,128)} fusion(f32[4,12,512,512]{2,3,1,0:T(8,128)} %get-tuple-element.207, f32[4,12,512]{2,1,0:T(8,128)S(1)} %bitcast.256, f32[4,12,512]{2,1,0:T(8,128)S(1)} %log_add_fusion, bf16[4,512,12,64]{1,3,2,0:T(8,128)(2,1)S(1)} %bitcast.230, bf16[4,512,12,64]{1,3,2,0:T(8,128)(2,1)} %bitcast.241), kind=kOutput, calls=%fused_computation.69 | convolution fusion | flops 1648361472 | bytes 107151360 | tf_op jit(solution)/shard_map/bqhd,bkhd->bhqk/dot_general | solution.py:119
  628.1 33.6 %subtract_multiply_fusion.1 = f32[4,12,512,512]{2,3,1,0:T(8,128)} fusion(f32[4,12,512,512]{2,3,1,0:T(8,128)} %get-tuple-element.205, f32[4,12,512]{2,1,0:T(8,128)S(1)} %bitcast.257, f32[4,12,512]{2,1,0:T(8,128)S(1)} %log_add_fusion, bf16[4,512,12,64]{1,3,2,0:T(8,128)(2,1)S(1)} %bitcast.231, bf16[4,512,12,64]{1,3,2,0:T(8,128)(2,1)} %bitcast.238), kind=kOutput, calls=%fused_computation.72 | convolution fusion | flops 1648361472 | bytes 107151360 | tf_op jit(solution)/shard_map/bqhd,bkhd->bhqk/dot_general | solution.py:119
  661.7 20.9 %fusion.122 = bf16[4,12,64,512]{3,2,1,0:T(8,128)(2,1)} fusion(bf16[4,512,12,64]{1,3,2,0:T(8,128)(2,1)} %bitcast.236, f32[4,12,512,512]{2,3,1,0:T(8,128)} %subtract_multiply_fusion), kind=kOutput, calls=%fused_computation.158 | convolution fusion | flops 1637351424 | bytes 56623104 | tf_op jit(solution)/shard_map/bhqk,bqhd->bkhd/dot_general | solution.py:125
  687.2 21.3 %fusion.123 = bf16[4,12,64,512]{3,2,1,0:T(8,128)(2,1)} fusion(bf16[4,512,12,64]{1,3,2,0:T(8,128)(2,1)} %bitcast.237, f32[4,12,512,512]{2,3,1,0:T(8,128)} %subtract_multiply_fusion.1), kind=kOutput, calls=%fused_computation.159 | convolution fusion | flops 1637351424 | bytes 56623104 | tf_op jit(solution)/shard_map/bhqk,bqhd->bkhd/dot_general | solution.py:125
  719.1 20.9 %fusion.127 = bf16[4,12,64,512]{3,2,1,0:T(8,128)(2,1)} fusion(bf16[4,512,12,64]{1,3,2,0:T(8,128)(2,1)S(1)} %bitcast.232, f32[4,12,512,512]{2,3,1,0:T(8,128)} %get-tuple-element.207, f32[4,12,512]{2,1,0:T(8,128)S(1)} %log_add_fusion), kind=kOutput, calls=%fused_computation.161 | convolution fusion | flops 1637351424 | bytes 56721408 | tf_op jit(solution)/shard_map/bhqk,bqhd->bkhd/dot_general | solution.py:128
  744.6 20.4 %fusion.124 = bf16[4,12,64,512]{3,2,1,0:T(8,128)(2,1)} fusion(bf16[4,512,12,64]{1,3,2,0:T(8,128)(2,1)S(1)} %bitcast.233, f32[4,12,512,512]{2,3,1,0:T(8,128)} %get-tuple-element.205, f32[4,12,512]{2,1,0:T(8,128)S(1)} %log_add_fusion), kind=kOutput, calls=%fused_computation.160 | convolution fusion | flops 1637351424 | bytes 56721408 | tf_op jit(solution)/shard_map/bhqk,bqhd->bkhd/dot_general | solution.py:128
  782.9 20.3 %fusion.78 = f32[4,12,64,512]{3,2,1,0:T(8,128)} fusion(bf16[4,512,12,64]{1,3,2,0:T(8,128)(2,1)S(1)} %bitcast.243, f32[4,12,512,512]{2,3,1,0:T(8,128)} %subtract_multiply_fusion.1), kind=kOutput, calls=%fused_computation.103 | convolution fusion | flops 1635778560 | bytes 59768832 | tf_op jit(solution)/shard_map/bhqk,bkhd->bqhd/dot_general | solution.py:124
  803.3 22.9 %add_convert_fusion = bf16[4,12,64,512]{3,2,1,0:T(8,128)(2,1)} fusion(f32[4,12,64,512]{3,2,1,0:T(8,128)} %fusion.78, bf16[4,512,12,64]{1,3,2,0:T(8,128)(2,1)} %bitcast.245, f32[4,12,512,512]{2,3,1,0:T(8,128)} %subtract_multiply_fusion), kind=kOutput, calls=%fused_computation.133 | convolution fusion | flops 1638924288 | bytes 62914560 | tf_op jit(solution)/shard_map/bhqk,bkhd->bqhd/dot_general | solution.py:124
  875.7 35.5 %fusion.110 = bf16[4,1,512,768]{3,2,1,0:T(8,128)(2,1)} fusion(f32[4,512,768]{2,1,0:T(8,128)} %get-tuple-element.211, bf16[768,3072]{1,0:T(8,128)(2,1)} %all-gather.23.cloned.1.call-done, f32[4,512,3072]{2,1,0:T(8,128)} %fusion.108), kind=kOutput, calls=%fused_computation.150 | convolution fusion | flops 9723445248 | bytes 39321600 | tf_op jit(solution)/shard_map/bsf,df->bsd/dot_general | solution.py:220
  925.1 50.6 %conditional.7 = (f32[32,12]{0,1:T(8,128)S(1)}) conditional(s32[]{:T(128)} %bitcast.20, (s32[512]{0:T(512)S(1)}, s32[512]{0:T(512)S(1)}, f32[4,12,512,512]{2,3,1,0:T(8,128)}) %tuple.130, (f32[32]{0:T(128)S(1)}, f32[4,12,512,512]{2,3,1,0:T(8,128)}) %tuple.132), branch_computations={%region_27.29_spmd, %region_29.31_spmd} | conditional | flops 1233125376 | bytes 77600264 | solution.py:61
  925.1 24.6 %reduce_sum.107 = f32[12,512,512]{1,2,0:T(8,128)} reduce(f32[4,12,512,512]{2,3,1,0:T(8,128)} %get-tuple-element.165, f32[]{:T(128)} %constant.81.clone), dimensions={0}, to_apply=%region_28.28 | reduce | flops 9437184 | bytes 62914564 | tf_op jit(solution)/shard_map/cond/branch_0_fun/bhqk,qkn->nh/reduce_sum | solution.py:59
  950.8 24.4 %fusion.48 = f32[32,12]{0,1:T(8,128)S(1)} fusion(f32[12,512,512]{1,2,0:T(8,128)} %reduce_sum.107, s32[512,512]{0,1:T(8,128)S(1)} %fusion.51), kind=kOutput, calls=%fused_computation.65 | convolution fusion | flops 1216348160 | bytes 13633024 | tf_op jit(solution)/shard_map/cond/branch_0_fun/bhqk,qkn->nh/dot_general | solution.py:59
  975.6 50.1 %conditional.6 = (f32[32,12]{0,1:T(8,128)S(1)}) conditional(s32[]{:T(128)} %bitcast.13, (s32[512]{0:T(512)S(1)}, s32[512]{0:T(512)S(1)}, f32[4,12,512,512]{2,3,1,0:T(8,128)}) %tuple.129, (f32[32]{0:T(128)S(1)}, f32[4,12,512,512]{2,3,1,0:T(8,128)}) %tuple.131), branch_computations={%region_23.25_spmd, %region_25.27_spmd} | conditional | flops 1233125376 | bytes 77600264 | solution.py:61
  975.7 24.4 %reduce_sum.99 = f32[12,512,512]{1,2,0:T(8,128)} reduce(f32[4,12,512,512]{2,3,1,0:T(8,128)} %get-tuple-element.160, f32[]{:T(128)} %constant.49.clone), dimensions={0}, to_apply=%region_24.24 | reduce | flops 9437184 | bytes 62914564 | tf_op jit(solution)/shard_map/cond/branch_0_fun/bhqk,qkn->nh/reduce_sum | solution.py:59
  1001.1 24.5 %fusion.34 = f32[32,12]{0,1:T(8,128)S(1)} fusion(f32[12,512,512]{1,2,0:T(8,128)} %reduce_sum.99, s32[512,512]{0,1:T(8,128)S(1)} %fusion.37), kind=kOutput, calls=%fused_computation.48 | convolution fusion | flops 1216348160 | bytes 13633024 | tf_op jit(solution)/shard_map/cond/branch_0_fun/bhqk,qkn->nh/dot_general | solution.py:59
  1036.5 40.4 %all-reduce.4 = (f32[768]{0:T(1024)S(1)}, f32[32,12]{0,1:T(8,128)}, f32[768]{0:T(1024)S(1)}) all-reduce(f32[768]{0:T(1024)S(1)} %get-tuple-element.181, f32[32,12]{0,1:T(8,128)S(1)} %add.432, f32[768]{0:T(1024)S(1)} %copy-done.30), channel_id=4, replica_groups=mesh['dp'=16,'blk'=2] {'dp','blk'}, use_global_device_ids=true, to_apply=%region_18.19.clone | all-reduce | flops 1920 | bytes 15360
  1084.8 140.2 %reduce-scatter.23.cloned.1.call-done = f32[24,3072]{1,0:T(8,128)} async-done(((f32[768,3072]{1,0:T(8,128)}), f32[24,3072]{1,0:T(8,128)}) %reduce-scatter.23.cloned.1.call-update) | async-done | bytes 294928 | tf_op jit(solution)/shard_map/reduce_scatter | solution.py:307
  1225.0 141.9 %reduce-scatter.21.cloned.1.call-done = f32[24,3072]{1,0:T(8,128)} async-done(((f32[768,3072]{1,0:T(8,128)}), f32[24,3072]{1,0:T(8,128)}) %reduce-scatter.21.cloned.1.call-update) | async-done | bytes 294928 | tf_op jit(solution)/shard_map/reduce_scatter | solution.py:306
  1367.0 103.8 %reduce-scatter.15.cloned.1.call-done = f32[24,768]{1,0:T(8,128)} async-done(((f32[768,768]{1,0:T(8,128)}), f32[24,768]{1,0:T(8,128)}) %reduce-scatter.15.cloned.1.call-update) | async-done | bytes 73744 | tf_op jit(solution)/shard_map/reduce_scatter | solution.py:302
  1470.8 104.6 %reduce-scatter.17.cloned.1.call-done = f32[24,768]{1,0:T(8,128)} async-done(((f32[768,768]{1,0:T(8,128)}), f32[24,768]{1,0:T(8,128)}) %reduce-scatter.17.cloned.1.call-update) | async-done | bytes 73744 | tf_op jit(solution)/shard_map/reduce_scatter | solution.py:303
  (191 shorter events, 349.3 us)
Async XLA Ops:
  7.2 60.6 %all-gather.11.cloned.1.call-start = ((), (), s32[]{:S(2)}) async-start(), calls=%async_computation.9 | async-start | bytes 1216512 | tf_op jit(solution)/shard_map/all_gather | solution.py:160
  7.9 115.9 %all-gather.15.cloned.1.call-start = ((), (), s32[]{:S(2)}) async-start(), calls=%async_computation.11 | async-start | bytes 1216512 | tf_op jit(solution)/shard_map/all_gather | solution.py:161
  8.7 199.7 %all-gather.9.cloned.1.call-start = ((), (), s32[]{:S(2)}) async-start(), calls=%async_computation.8 | async-start | bytes 1216512 | tf_op jit(solution)/shard_map/all_gather | solution.py:159
  9.4 251.8 %all-gather.13.cloned.1.call-start = ((), (), s32[]{:S(2)}) async-start(), calls=%async_computation.10 | async-start | bytes 9437184 | tf_op jit(solution)/shard_map/all_gather | solution.py:190
  53.2 155.1 %copy-start.20 = (f32[768]{0:T(1024)}, f32[768]{0:T(1024)S(1)}, u32[]{:S(2)}) copy-start(f32[768]{0:T(1024)S(1)} %convert_element_type.357) | copy-start | bytes 9220
  56.0 152.4 %copy-start.15 = (f32[4,512]{1,0:T(4,128)}, f32[4,512]{1,0:T(4,128)S(1)}, u32[]{:S(2)}) copy-start(f32[4,512]{1,0:T(4,128)S(1)} %add_rsqrt_fusion.1) | copy-start | bytes 24580
  56.0 67.8 %copy-start.1 = (bf16[4,1,512,768]{3,2,1,0:T(8,128)(2,1)S(1)}, bf16[4,1,512,768]{3,2,1,0:T(8,128)(2,1)}, u32[]{:S(2)}) copy-start(bf16[4,1,512,768]{3,2,1,0:T(8,128)(2,1)} %param.20) | copy-start | bytes 9437188
  74.4 67.1 %copy-start.35 = (s32[4,1]{0,1:T(1,128)S(1)}, s32[4,1]{0,1:T(1,128)}, u32[]{:S(2)}) copy-start(s32[4,1]{0,1:T(1,128)} %param.21) | copy-start | bytes 52
  74.4 67.8 %copy-start.17 = (f32[32,12]{0,1:T(8,128)S(1)}, f32[32,12]{0,1:T(8,128)}, u32[]{:S(2)}) copy-start(f32[32,12]{0,1:T(8,128)} %param.27) | copy-start | bytes 4612
  74.4 292.0 %all-gather.17.cloned.1.call-start = ((), (), s32[]{:S(2)}) async-start(), calls=%async_computation.12 | async-start | bytes 9437184 | tf_op jit(solution)/shard_map/all_gather | solution.py:191
  129.2 295.5 %all-gather.19.cloned.1.call-start = ((), (), s32[]{:S(2)}) async-start(), calls=%async_computation.13 | async-start | bytes 1216512 | tf_op jit(solution)/shard_map/all_gather | solution.py:162
  129.8 335.8 %all-gather.21.cloned.1.call-start = ((), (), s32[]{:S(2)}) async-start(), calls=%async_computation.14 | async-start | bytes 4866048 | tf_op jit(solution)/shard_map/all_gather | solution.py:164
  130.5 400.4 %all-gather.23.cloned.1.call-start = ((), (), s32[]{:S(2)}) async-start(), calls=%async_computation.15 | async-start | bytes 4866048 | tf_op jit(solution)/shard_map/all_gather | solution.py:165
  131.3 738.2 %reduce-scatter.9.cloned.1.call-start = ((), (), s32[]{:S(2)}) async-start(), calls=%async_computation.16 | async-start | bytes 9437184 | tf_op jit(solution)/shard_map/reduce_scatter | solution.py:278
  131.4 43.6 %copy-start.22 = (s32[512]{0:T(512)}, s32[512]{0:T(512)S(1)}, u32[]{:S(2)}) copy-start(s32[512]{0:T(512)S(1)} %iota_add_fusion) | copy-start | bytes 6148
  131.4 43.5 %copy-start.18 = (s32[512]{0:T(512)}, s32[512]{0:T(512)S(1)}, u32[]{:S(2)}) copy-start(s32[512]{0:T(512)S(1)} %iota_add_fusion.1) | copy-start | bytes 6148
  140.9 34.0 %copy-start.33 = (f32[32]{0:T(128)}, f32[32]{0:T(128)S(1)}, u32[]{:S(2)}) copy-start(f32[32]{0:T(128)S(1)} %compare_convert_fusion.1) | copy-start | bytes 388
  216.9 85.0 %copy-start = (bf16[4,512,768]{1,2,0:T(8,128)(2,1)}, bf16[4,512,768]{1,2,0:T(8,128)(2,1)S(1)}, u32[]{:S(2)}) copy-start(bf16[4,512,768]{1,2,0:T(8,128)(2,1)S(1)} %copy.146) | copy-start | bytes 9437188
  400.3 24.5 %copy-start.2 = (bf16[4,1,512,768]{3,2,1,0:T(8,128)(2,1)S(1)}, bf16[4,1,512,768]{3,2,1,0:T(8,128)(2,1)}, u32[]{:S(2)}) copy-start(bf16[4,1,512,768]{3,2,1,0:T(8,128)(2,1)} %param.20) | copy-start | bytes 9437188
  424.8 40.8 %copy-start.28 = (f32[768]{0:T(1024)S(1)}, f32[768]{0:T(1024)}, u32[]{:S(2)}) copy-start(f32[768]{0:T(1024)} %convert_element_type.372) | copy-start | bytes 9220
  432.5 143.5 %copy-start.24 = (f32[4,512]{1,0:T(4,128)}, f32[4,512]{1,0:T(4,128)S(1)}, u32[]{:S(2)}) copy-start(f32[4,512]{1,0:T(4,128)S(1)} %add_rsqrt_fusion) | copy-start | bytes 24580
  465.6 65.4 %copy-start.26 = (bf16[4,512]{1,0:T(4,128)(2,1)S(1)}, bf16[4,512]{1,0:T(4,128)(2,1)}, u32[]{:S(2)}) copy-start(bf16[4,512]{1,0:T(4,128)(2,1)} %get-tuple-element.201) | copy-start | bytes 12292
  465.6 95.0 %slice-start = ((s8[6291456]{0:T(1024)(128)(4,1)}), s8[2097152]{0:T(1024)(128)(4,1)S(1)}, s32[]{:S(2)}) async-start(s8[6291456]{0:T(1024)(128)(4,1)} %bitcast.250), calls=%async_computation.24 | async-start | bytes 4194304
  531.0 29.6 %slice-start.1 = ((s8[6291456]{0:T(1024)(128)(4,1)}), s8[4194304]{0:T(1024)(128)(4,1)S(1)}, s32[]{:S(2)}) async-start(s8[6291456]{0:T(1024)(128)(4,1)} %bitcast.250), calls=%async_computation.25 | async-start | bytes 8388608
  719.0 192.2 %reduce-scatter.11.cloned.1.call-start = ((), (), s32[]{:S(2)}) async-start(), calls=%async_computation.17 | async-start | bytes 9437184 | tf_op jit(solution)/shard_map/reduce_scatter | solution.py:281
  774.8 310.1 %reduce-scatter.19.cloned.1.call-start = ((), (), s32[]{:S(2)}) async-start(), calls=%async_computation.21 | async-start | bytes 2433024 | tf_op jit(solution)/shard_map/reduce_scatter | solution.py:304
  803.2 281.6 %reduce-scatter.13.cloned.1.call-start = ((), (), s32[]{:S(2)}) async-start(), calls=%async_computation.18 | async-start | bytes 2433024 | tf_op jit(solution)/shard_map/reduce_scatter | solution.py:301
  832.5 392.5 %reduce-scatter.23.cloned.1.call-start = ((), (), s32[]{:S(2)}) async-start(), calls=%async_computation.23 | async-start | bytes 9732096 | tf_op jit(solution)/shard_map/reduce_scatter | solution.py:307
  851.2 515.8 %reduce-scatter.21.cloned.1.call-start = ((), (), s32[]{:S(2)}) async-start(), calls=%async_computation.22 | async-start | bytes 9732096 | tf_op jit(solution)/shard_map/reduce_scatter | solution.py:306
  869.4 601.4 %reduce-scatter.15.cloned.1.call-start = ((), (), s32[]{:S(2)}) async-start(), calls=%async_computation.19 | async-start | bytes 2433024 | tf_op jit(solution)/shard_map/reduce_scatter | solution.py:302
  875.7 699.8 %reduce-scatter.17.cloned.1.call-start = ((), (), s32[]{:S(2)}) async-start(), calls=%async_computation.20 | async-start | bytes 2433024 | tf_op jit(solution)/shard_map/reduce_scatter | solution.py:303
  925.0 50.6 %copy-start.32 = (f32[32]{0:T(128)S(1)}, f32[32]{0:T(128)}, u32[]{:S(2)}) copy-start(f32[32]{0:T(128)} %copy-done.31) | copy-start | bytes 388
  (23 other events, 223.5 us)
Sparse Core Ops, SparseCore 0:
  10.9 56.8 all-gather.10
  70.7 53.0 all-gather.14
  126.8 53.0 all-gather.8
  181.8 79.3 all-gather.12
  262.6 80.3 all-gather.16
  345.8 54.1 all-gather.18
  402.9 62.6 all-gather.20
  468.5 62.4 all-gather.22
  719.2 75.8 reduce-scatter.8
  797.3 77.0 reduce-scatter.10
  880.3 98.9 reduce-scatter.18
  985.8 98.1 reduce-scatter.12
  1090.5 134.4 reduce-scatter.22
  1232.4 134.5 reduce-scatter.20
  1372.7 98.0 reduce-scatter.14
  1477.4 98.0 reduce-scatter.16
where the time goes:
time: 1590 us; the launch traced here: 1580 us
  waiting for transfers between devices  680 us (43%)
  matrix products  575 us (36%)
  other arithmetic  124 us (8%)
  local copies, waits for them, and re-layouts  95.9 us (6%)
  blocking collectives  82.5 us (5%)
  between operations  22.5 us (1%)
    reduce_scatter x1, waiting for transfers between devices, body(): lax.psum_scatter(grad_in, ('dp', 'blk'), scatter_dimension=0, tiled=True)  142 us
    reduce_scatter x1, waiting for transfers between devices, body(): lax.psum_scatter(grad_down, ('dp', 'blk'), scatter_dimension=0, tiled=True)  140 us
    reduce_scatter x1, waiting for transfers between devices, body(): lax.psum_scatter(grad_v, ('dp', 'blk'), scatter_dimension=0, tiled=True)  105 us
    reduce_scatter x1, waiting for transfers between devices, body(): lax.psum_scatter(grad_k, ('dp', 'blk'), scatter_dimension=0, tiled=True)  104 us
    unnamed x2, blocking collectives  82.5 us
    dot_general x2, matrix products, block_grads(): jnp.einsum('bqhd,bkhd->bhqk', grad_heads, value_heads, preferred_element_...  67.6 us
    dot_general x2, matrix products, masked_scores(): jnp.einsum('bqhd,bkhd->bhqk', query_heads, key_heads, preferred_element_t...  49.7 us
    all_gather x1, waiting for transfers between devices, body(): lax.all_gather(w_value, ('dp', 'blk'), axis=0, tiled=True)  49.4 us
  transfers between devices with their start and end apart: 16, of which 9 were waited for; matrix products, arithmetic and copies ran while one was open for 38% of the time, Pallas kernels for 0%

commit v1 on v0

v1 whole, which is shorter than its diff:
```python
import functools

import jax
import jax.numpy as jnp
from jax import lax
from jax.experimental import pallas as pl
from jax.experimental.pallas import tpu as pltpu
from jax.sharding import PartitionSpec as P

EPS = 1e-06
NEG = -1e30
LIMITS = (12, 16, 23, 32, 46, 64, 91)
SUB = 128
LOG2E = 1.4426950408889634
GELU_A = 0.7978845608028654
GELU_B = 0.044715
VMEM = 62 * 2**20
NN = (((1,), (0,)), ((), ()))
NT = (((1,), (1,)), ((), ()))
TN = (((0,), (0,)), ((), ()))
low_type = jnp.bfloat16
f32 = jnp.float32


def dot(left, right, dims=NN):
    return lax.dot_general(left, right, dims, preferred_element_type=f32)


def bucket_of(relative):
    distance = jnp.abs(relative)
    far_bucket = 8 + sum(((distance >= border).astype(jnp.int32) for border in LIMITS))
    bucket = jnp.where(distance < 8, distance, far_bucket)
    return bucket + 16 * (relative > 0).astype(jnp.int32)


def norm_rows(rows):
    inverse = lax.rsqrt(jnp.mean(rows * rows, -1, keepdims=True) + EPS)
    return rows * inverse, inverse


def whole(shape):
    return pl.BlockSpec(shape, lambda *_: (0,) * len(shape), pipeline_mode=pl.Buffered(1))


def params():
    return pltpu.CompilerParams(vmem_limit_bytes=VMEM)


def struct(shape, dtype=low_type):
    return jax.ShapeDtypeStruct(shape, dtype)


SMEM = pl.BlockSpec(memory_space=pltpu.SMEM)


def qkv_kernel(x_ref, gain_ref, w_ref, q_ref, k_ref, v_ref):
    width = q_ref.shape[1]
    normed, _ = norm_rows(x_ref[...].astype(f32))
    low = (normed * gain_ref[...]).astype(low_type)
    q_ref[...] = (dot(low, w_ref[:, :width]) * (0.125 * LOG2E)).astype(low_type)
    k_ref[...] = dot(low, w_ref[:, width : 2 * width]).astype(low_type)
    v_ref[...] = dot(low, w_ref[:, 2 * width : 3 * width]).astype(low_type)


def qkv_call(x, gain, w_first, heads_width, rows=512):
    total, width = x.shape
    row = pl.BlockSpec((rows, width), lambda i: (i, 0))
    return pl.pallas_call(
        qkv_kernel,
        grid=(total // rows,),
        in_specs=[row, whole((1, width)), whole(w_first.shape)],
        out_specs=[pl.BlockSpec((rows, heads_width), lambda i: (i, 0))] * 3,
        out_shape=[struct((total, heads_width))] * 3,
        compiler_params=params(),
        name="qkv",
    )(x, gain, w_first)


def attend_kernel(
    len_ref, far_ref, q_ref, k_ref, v_ref, near_ref, o_ref, lse_ref, *, rows
):
    pair, doc = pl.program_id(0), pl.program_id(1)
    seq = q_ref.shape[0]
    subs = seq // SUB
    first = lax.broadcasted_iota(jnp.int32, (1, 128), 1) < 64
    live = lax.broadcasted_iota(jnp.int32, (1, seq), 1) < len_ref[doc]
    one = jnp.ones((), low_type)
    k, v = k_ref[...], v_ref[...]
    v_ones = (jnp.where(first, v, one), jnp.where(first, one, v))
    for block in range(seq // rows):
        span = slice(block * rows, (block + 1) * rows)
        q = q_ref[span, :]
        outs, tops = [], []
        for h in range(2):
            q_one = jnp.where(first == (h == 0), q, jnp.zeros((), low_type))
            raw = dot(q_one, k, NT)
            strips = []
            for a in range(rows // SUB):
                at = block * (rows // SUB) + a
                strip = raw[a * SUB : (a + 1) * SUB]
                low, high = max(at - 1, 0), min(at + 2, subs)
                parts = []
                if low > 0:
                    parts.append(strip[:, : low * SUB] + far_ref[2 * pair + h, 0])
                for b in range(low, high):
                    parts.append(strip[:, b * SUB : (b + 1) * SUB] + near_ref[h, b - at + 1])
                if high < subs:
                    parts.append(strip[:, high * SUB :] + far_ref[2 * pair + h, 1])
                strips.append(jnp.concatenate(parts, 1))
            scores = jnp.where(live, jnp.concatenate(strips, 0), NEG)
            top = jnp.max(scores, 1, keepdims=True)
            outs.append(dot(jnp.exp2(scores - top).astype(low_type), v_ones[h]))
            tops.append(top)
        total = jnp.where(first, pltpu.roll(outs[0], 64, 1), pltpu.roll(outs[1], 64, 1))
        o_ref[span, :] = (jnp.where(first, outs[0], outs[1]) / total).astype(low_type)
        log_total = (jnp.where(first, tops[0], tops[1]) + jnp.log2(total)).T
        lse_ref[0, 0, 0:1, span] = log_total[0:1]
        lse_ref[0, 0, 1:2, span] = log_total[64:65]


def attend_call(lengths, far, q, k, v, near, rows=512):
    docs, (total, width) = lengths.shape[0], q.shape
    seq, pairs = total // docs, width // 128
    slab = pl.BlockSpec((seq, 128), lambda p, d: (d, p))
    return pl.pallas_call(
        functools.partial(attend_kernel, rows=rows),
        grid=(pairs, docs),
        in_specs=[
            SMEM,
            SMEM,
            slab,
            slab,
            slab,
            pl.BlockSpec((2, 3, SUB, SUB), lambda p, d: (p, 0, 0, 0)),
        ],
        out_specs=[slab, pl.BlockSpec((1, 1, 2, seq), lambda p, d: (d, p, 0, 0))],
        out_shape=[struct((total, width)), struct((docs, pairs, 2, seq), f32)],
        compiler_params=params(),
        name="attend",
    )(lengths, far, q, k, v, near)


def middle_kernel(
    len_ref,
    x_ref,
    heads_ref,
    cot_ref,
    gain_ref,
    w_ref,
    mixed_ref,
    hgrad_ref,
    mid_ref,
    gw_ref,
    gn_ref,
    acc,
    acc_gain,
    *,
    seq,
    chunk,
):
    step = pl.program_id(0)
    rows, width = x_ref.shape
    hidden = (w_ref.shape[1] - width) // 2

    @pl.when(step == 0)
    def _():
        acc[...] = jnp.zeros_like(acc)
        acc_gain[...] = jnp.zeros_like(acc_gain)

    per = seq // rows
    place = (step % per) * rows + lax.broadcasted_iota(jnp.int32, (rows, 1), 0)
    heads, gain = heads_ref[...], gain_ref[...]
    residual = x_ref[...].astype(f32) + dot(heads, w_ref[:, :width])
    normed, inverse = norm_rows(residual)
    low = (normed * gain).astype(low_type)
    out_grad = jnp.where(place < len_ref[step // per], cot_ref[...], jnp.zeros((), low_type))
    mixed, normed_grad = residual, jnp.zeros((rows, width), f32)
    for at in range(0, hidden, chunk):
        up = slice(width + at, width + at + chunk)
        down = slice(width + hidden + at, width + hidden + at + chunk)
        u = dot(low, w_ref[:, up])
        square = u * u
        bend = jnp.tanh(u * (GELU_A + GELU_A * GELU_B * square))
        half = 0.5 + 0.5 * bend
        act = (u * half).astype(low_type)
        slope = half + (0.5 * u) * (1 - bend * bend) * (GELU_A + 3 * GELU_A * GELU_B * square)
        up_grad = (dot(out_grad, w_ref[:, down]) * slope).astype(low_type)
        mixed = mixed + dot(act, w_ref[:, down], NT)
        normed_grad = normed_grad + dot(up_grad, w_ref[:, up], NT)
        acc[:, down] += dot(out_grad, act, TN)
        acc[:, up] += dot(low, up_grad, TN)
    mixed_ref[...] = mixed.astype(low_type)
    scaled = normed_grad * gain
    inner = jnp.mean(scaled * normed, -1, keepdims=True)
    mid = (out_grad.astype(f32) + inverse * (scaled - normed * inner)).astype(low_type)
    acc_gain[...] += jnp.sum((normed_grad * normed).reshape(rows // 8, 8, width), 0)
    mid_ref[...] = mid
    acc[:, :width] += dot(heads, mid, TN)
    hgrad_ref[...] = dot(mid, w_ref[:, :width], NT).astype(low_type)

    @pl.when(step == pl.num_programs(0) - 1)
    def _():
        gw_ref[...] = acc[...].astype(low_type)
        gn_ref[...] = jnp.sum(acc_gain[...], 0, keepdims=True)


def middle_call(lengths, x, heads, cot, gain, w_second, rows=256, chunk=1024):
    total, width = x.shape
    row = pl.BlockSpec((rows, width), lambda i: (i, 0))
    return pl.pallas_call(
        functools.partial(middle_kernel, seq=total // lengths.shape[0], chunk=chunk),
        grid=(total // rows,),
        in_specs=[SMEM, row, row, row, whole((1, width)), whole(w_second.shape)],
        out_specs=[row, row, row, whole(w_second.shape), whole((1, width))],
        out_shape=[struct((total, width))] * 3 + [struct(w_second.shape), struct((1, width), f32)],
        scratch_shapes=[pltpu.VMEM(w_second.shape, f32), pltpu.VMEM((8, width), f32)],
        compiler_params=params(),
        name="middle",
    )(lengths, x, heads, cot, gain, w_second)


def attend_back_kernel(
    len_ref,
    far_ref,
    q_ref,
    k_ref,
    v_ref,
    grad_ref,
    o_ref,
    lse_ref,
    near_ref,
    dq_ref,
    dk_ref,
    dv_ref,
    near_sum,
    far_sum,
    acc,
    *,
    keys,
    queries,
):
    pair, doc = pl.program_id(0), pl.program_id(1)
    seq = q_ref.shape[0]
    first = lax.broadcasted_iota(jnp.int32, (1, 128), 1) < 64
    zero = jnp.zeros((), low_type)

    def halves(x):
        return jnp.where(first, x, zero), jnp.where(first, zero, x)

    grad = grad_ref[...]
    q_one, g_one = halves(q_ref[...]), halves(grad)
    product = grad.astype(f32) * o_ref[...].astype(f32)
    upper = product.astype(low_type)
    lower = (product - upper.astype(f32)).astype(low_type)
    row = lax.broadcasted_iota(jnp.int32, (16, 128), 0)
    column = lax.broadcasted_iota(jnp.int32, (16, 128), 1)
    member = (row == column // 64).astype(f32).astype(low_type)
    delta = dot(member, upper, NT) + dot(member, lower, NT)

    @pl.when(doc == 0)
    def _():
        near_sum[...] = jnp.zeros_like(near_sum)
        far_sum[...] = jnp.zeros_like(far_sum)

    acc[...] = jnp.zeros_like(acc)
    for kb in range(seq // keys):
        held = slice(kb * keys, (kb + 1) * keys)
        k, v = k_ref[held, :], v_ref[held, :]
        k_one = halves(k)
        live = (kb * keys + lax.broadcasted_iota(jnp.int32, (keys, 1), 0)) < len_ref[doc]
        dk = jnp.zeros((keys, 128), f32)
        dv = jnp.zeros((keys, 128), f32)
        for qb in range(seq // queries):
            span = slice(qb * queries, (qb + 1) * queries)
            dq = None
            for h in range(2):
                scores = dot(k, q_one[h][span], NT)
                prob_grad = dot(v, g_one[h][span], NT)
                lse = lse_ref[0, 0, h : h + 1, span]
                lse_side = (lse - far_ref[2 * pair + h, 0], lse - far_ref[2 * pair + h, 1])
                row_delta = delta[h : h + 1, span]
                prob_rows, grad_rows = [], []
                for a in range(keys // SUB):
                    down = slice(a * SUB, (a + 1) * SUB)
                    probs, grads = [], []
                    for b in range(queries // SUB):
                        across = slice(b * SUB, (b + 1) * SUB)
                        apart = kb * (keys // SUB) + a - qb * (queries // SUB) - b
                        tile = scores[down, across]
                        if abs(apart) <= 1:
                            tile = tile + near_ref[h, apart + 1] - lse[:, across]
                        else:
                            tile = tile - lse_side[int(apart > 0)][:, across]
                        prob = jnp.where(live[down], jnp.exp2(tile), 0.0)
                        score_grad = prob * (prob_grad[down, across] - row_delta[:, across])
                        if abs(apart) <= 1:
                            near_sum[h, apart + 1] += score_grad
                        else:
                            far_sum[h, int(apart > 0)] += jnp.sum(
                                score_grad.reshape(SUB // 8, 8, SUB), 0
                            )
                        probs.append(prob.astype(low_type))
                        grads.append(score_grad.astype(low_type))
                    prob_rows.append(jnp.concatenate(probs, 1))
                    grad_rows.append(jnp.concatenate(grads, 1))
                prob_low = jnp.concatenate(prob_rows, 0)
                grad_low = jnp.concatenate(grad_rows, 0)
                dv = dv + dot(prob_low, g_one[h][span])
                dk = dk + dot(grad_low, q_one[h][span])
                part = dot(grad_low, k_one[h], TN)
                dq = part if dq is None else dq + part
            acc[span, :] += dq
        dv_ref[held, :] = dv.astype(low_type)
        dk_ref[held, :] = (dk * (1 / LOG2E)).astype(low_type)
    dq_ref[...] = (acc[...] * 0.125).astype(low_type)


def attend_back_call(lengths, far, q, k, v, grad, o, lse, near, keys=256, queries=1024):
    docs, (total, width) = lengths.shape[0], q.shape
    seq, pairs = total // docs, width // 128
    queries = min(queries, seq)
    slab = pl.BlockSpec((seq, 128), lambda p, d: (d, p))
    tiles = pl.BlockSpec((2, 3, SUB, SUB), lambda p, d: (p, 0, 0, 0))
    return pl.pallas_call(
        functools.partial(attend_back_kernel, keys=keys, queries=queries),
        grid=(pairs, docs),
        in_specs=[
            SMEM,
            SMEM,
            slab,
            slab,
            slab,
            slab,
            slab,
            pl.BlockSpec((1, 1, 2, seq), lambda p, d: (d, p, 0, 0)),
            tiles,
        ],
        out_specs=[
            slab,
            slab,
            slab,
            tiles,
            pl.BlockSpec((2, 2, 8, SUB), lambda p, d: (p, 0, 0, 0)),
        ],
        out_shape=[struct((total, width))] * 3
        + [struct((2 * pairs, 3, SUB, SUB), f32), struct((2 * pairs, 2, 8, SUB), f32)],
        scratch_shapes=[pltpu.VMEM((seq, 128), f32)],
        compiler_params=params(),
        name="attend_back",
    )(lengths, far, q, k, v, grad, o, lse, near)


def last_kernel(
    x_ref,
    dq_ref,
    dk_ref,
    dv_ref,
    mid_ref,
    gain_ref,
    w_ref,
    gn_second_ref,
    gt_ref,
    gw_ref,
    acc,
    acc_gain,
):
    step = pl.program_id(0)
    rows, width = x_ref.shape

    @pl.when(step == 0)
    def _():
        acc[...] = jnp.zeros_like(acc)
        acc_gain[...] = jnp.zeros_like(acc_gain)

    gain = gain_ref[...]
    normed, inverse = norm_rows(x_ref[...].astype(f32))
    low = (normed * gain).astype(low_type)
    normed_grad = None
    for index, ref in enumerate((dq_ref, dk_ref, dv_ref)):
        part = slice(index * width, (index + 1) * width)
        grad = ref[...]
        acc[:, part] += dot(low, grad, TN)
        back = dot(grad, w_ref[:, part], NT)
        normed_grad = back if normed_grad is None else normed_grad + back
    acc_gain[...] += jnp.sum((normed_grad * normed).reshape(rows // 8, 8, width), 0)
    scaled = normed_grad * gain
    inner = jnp.mean(scaled * normed, -1, keepdims=True)
    gt_ref[...] = (mid_ref[...].astype(f32) + inverse * (scaled - normed * inner)).astype(low_type)

    @pl.when(step == pl.num_programs(0) - 1)
    def _():
        gw_ref[:, : 3 * width] = acc[...].astype(low_type)
        pick = lax.broadcasted_iota(jnp.int32, (128, 1), 0)
        gains = jnp.where(
            pick == 0,
            jnp.sum(acc_gain[...], 0, keepdims=True),
            jnp.where(pick == 1, gn_second_ref[...], 0.0),
        )
        gw_ref[:, 3 * width :] = gains.T.astype(low_type)


def last_call(x, dq, dk, dv, mid, gain, w_first, gn_second, rows=512):
    total, width = x.shape
    row = pl.BlockSpec((rows, width), lambda i: (i, 0))
    return pl.pallas_call(
        last_kernel,
        grid=(total // rows,),
        in_specs=[row] * 5 + [whole((1, width)), whole(w_first.shape), whole((1, width))],
        out_specs=[row, whole(w_first.shape)],
        out_shape=[struct((total, width)), struct(w_first.shape)],
        scratch_shapes=[pltpu.VMEM((width, 3 * width), f32), pltpu.VMEM((8, width), f32)],
        compiler_params=params(),
        name="last",
    )(x, dq, dk, dv, mid, gain, w_first, gn_second)


def sharing(count):
    ways = lax.axis_size("blk")
    return max(1, count // ways), max(1, ways // count)


def to_documents(x):
    count, rows, width = x.shape
    ways, me = lax.axis_size("blk"), lax.axis_index("blk")
    per, share = sharing(count)
    if share > 1:
        everything = lax.all_gather(x, "blk", axis=1, tiled=True)
        return lax.dynamic_index_in_dim(everything, me // share, 0, keepdims=False)
    out = jnp.zeros((per, ways * rows, width), x.dtype)
    for hop in range(ways):
        piece = lax.dynamic_slice_in_dim(x, lax.rem(me + hop, ways) * per, per, 0)
        if hop:
            piece = lax.ppermute(piece, "blk", [(i, (i + hop) % ways) for i in range(ways)])
        source = lax.rem(me - hop + ways, ways)
        out = lax.dynamic_update_slice_in_dim(out, piece, source * rows, 1)
    return out.reshape(per * ways * rows, width)


def from_documents(y, count):
    ways, me = lax.axis_size("blk"), lax.axis_index("blk")
    per, share = sharing(count)
    width = y.shape[1]
    if share > 1:
        everything = lax.all_gather(y, "blk", axis=0, tiled=True).reshape(count, -1, width)
        rows = everything.shape[1] // ways
        return lax.dynamic_slice_in_dim(everything, me * rows, rows, 1)
    y = y.reshape(per, -1, width)
    rows = y.shape[1] // ways
    out = jnp.zeros((count, rows, width), y.dtype)
    for hop in range(ways):
        piece = lax.dynamic_slice_in_dim(y, lax.rem(me + hop, ways) * rows, rows, 1)
        if hop:
            piece = lax.ppermute(piece, "blk", [(i, (i + hop) % ways) for i in range(ways)])
        source = lax.rem(me - hop + ways, ways)
        out = lax.dynamic_update_slice_in_dim(out, piece, source * per, 0)
    return out


def among(y, share, split, concat):
    if share == 1:
        return y
    ways = lax.axis_size("blk")
    groups = [list(range(at, at + share)) for at in range(0, ways, share)]
    return lax.all_to_all(
        y, "blk", split, concat, axis_index_groups=groups, tiled=True
    )


def my_share(y, share, axis):
    if share == 1:
        return y
    size = y.shape[axis] // share
    at = lax.rem(lax.axis_index("blk"), share) * size
    return lax.dynamic_slice_in_dim(y, at, size, axis)


def bias_tiles(table):
    offset = jnp.arange(SUB)[None, :] - jnp.arange(SUB)[:, None]
    buckets = bucket_of(offset[None] + SUB * jnp.arange(-1, 2)[:, None, None])
    tiles = jnp.zeros((table.shape[1],) + buckets.shape, f32)
    for b in range(table.shape[0]):
        tiles = jnp.where(buckets == b, table[b][:, None, None, None], tiles)
    return tiles, buckets


def body(
    tokens,
    lengths,
    norm1_gain,
    w_query,
    w_key,
    w_value,
    w_out,
    rel_table,
    norm2_gain,
    w_in,
    w_down,
    cotangent,
):
    micro, docs, rows, width = tokens.shape
    count = micro * docs
    per, share = sharing(count)
    both = ("dp", "blk")
    gains = jnp.pad(jnp.stack([norm1_gain, norm2_gain], 1), ((0, 0), (0, 126)))
    w_first = lax.all_gather(
        jnp.concatenate([w_query, w_key, w_value, gains], 1), both, axis=0, tiled=True
    )
    w_second = lax.all_gather(
        jnp.concatenate([w_out, w_in, w_down], 1), both, axis=0, tiled=True
    )
    gain_rows = w_first[:, 3 * width : 3 * width + 2].astype(f32).T
    gain_first, gain_second = gain_rows[:1], gain_rows[1:]
    own = lax.dynamic_slice_in_dim(
        lengths.reshape(count), lax.axis_index("blk") // share * per, per, 0
    )
    x = to_documents(tokens.reshape(count, rows, width))
    cot = to_documents(cotangent.reshape(count, rows, width))
    x_rows, cot_rows = my_share(x, share, 0), my_share(cot, share, 0)
    own_rows, w_heads = own, w_first
    if share > 1:
        own_rows = own - lax.rem(lax.axis_index("blk"), share) * x_rows.shape[0]
        w_heads = jnp.concatenate(
            [my_share(w_first[:, i * width : (i + 1) * width], share, 1) for i in range(3)], 1
        )

    table = rel_table * LOG2E
    near, buckets = bias_tiles(my_share(table, share, 1))
    far = my_share(jnp.stack([table[15], table[31]], 1), share, 0)

    q, k, v = qkv_call(x, gain_first, w_heads, width // share)
    heads, lse = attend_call(own, far, q, k, v, near)
    mixed, heads_grad, mid, g_second, gn_second = middle_call(
        own_rows, x_rows, among(heads, share, 0, 1), cot_rows, gain_second, w_second
    )
    dq, dk, dv, near_sum, far_sum = attend_back_call(
        own, far, q, k, v, among(heads_grad, share, 1, 0), heads, lse, jnp.swapaxes(near, 2, 3)
    )
    dq, dk, dv = (among(grad, share, 0, 1) for grad in (dq, dk, dv))
    grad_tokens, g_first = last_call(x_rows, dq, dk, dv, mid, gain_first, w_first, gn_second)

    flipped = jnp.swapaxes(buckets, 1, 2)
    rows_of = []
    for b in range(rel_table.shape[0]):
        rows_of.append(jnp.sum(jnp.where(flipped == b, near_sum, 0.0), (1, 2, 3)))
    table_sum = jnp.stack(rows_of)
    far_total = jnp.sum(far_sum, (2, 3))
    table_sum = table_sum.at[15].add(far_total[:, 0]).at[31].add(far_total[:, 1])
    if share > 1:
        at = lax.rem(lax.axis_index("blk"), share) * table_sum.shape[1]
        table_sum = lax.dynamic_update_slice_in_dim(
            jnp.zeros(rel_table.shape, f32), table_sum, at, 1
        )
    grad_table = lax.psum(table_sum, both)

    g_first = lax.psum_scatter(g_first, both, scatter_dimension=0, tiled=True).astype(f32)
    g_second = lax.psum_scatter(g_second, both, scatter_dimension=0, tiled=True).astype(f32)
    hidden = w_in.shape[1]
    return (
        from_documents(mixed, count).reshape(tokens.shape),
        from_documents(grad_tokens, count).reshape(tokens.shape),
        g_first[:, 3 * width],
        g_first[:, :width],
        g_first[:, width : 2 * width],
        g_first[:, 2 * width : 3 * width],
        g_second[:, :width],
        grad_table,
        g_first[:, 3 * width + 1],
        g_second[:, width : width + hidden],
        g_second[:, width + hidden :],
    )


def solution(mesh):
    rows = P(None, "dp", "blk", None)
    weight = P(("dp", "blk"), None)
    gain = P(("dp", "blk"))
    return jax.shard_map(
        body,
        mesh=mesh,
        in_specs=(
            rows,
            P(None, "dp"),
            gain,
            weight,
            weight,
            weight,
            weight,
            P(),
            gain,
            weight,
            weight,
            rows,
        ),
        out_specs=(rows, rows, gain, weight, weight, weight, weight, P(), gain, weight, weight),
        check_vma=False,
    )
```

time: 1590 us -> 631 us (0.40)
  matrix products: 575 us -> 0 us
  waiting for transfers between devices: 680 us -> 159 us
  Pallas kernels: 0 us -> 243 us
  other arithmetic: 124 us -> 54.7 us
  local copies, waits for them, and re-layouts: 95.9 us -> 45.3 us
  blocking collectives: 82.5 us -> 99.1 us
    dot_general x34 -> x0, matrix products: 575 us -> none  [the longest x2 67.6 us: block_grads(): jnp.einsum('bqhd,bkhd->bhqk', grad_heads, value_heads, preferred_element_...]
    reduce_scatter x8 -> x1, waiting for transfers between devices: 491 us -> 120 us  [body(): lax.psum_scatter(g_second, both, scatter_dimension=0, tiled=True)]
    pallas_call x0 -> x5, Pallas kernels: none -> 243 us  [the longest x1 84 us: middle_call(): pl.pallas_call(functools.partial(middle_kernel, seq=total // lengths.shap...]
    all_gather x8 -> x2, waiting for transfers between devices: 186 us -> 11.5 us  [the longest x1 11.5 us: body(): lax.all_gather(jnp.concatenate([w_out, w_in, w_down], 1), both, axis=0, t...]
    psum x0 -> x1, blocking collectives: none -> 99.1 us  [body(): grad_table = lax.psum(table_sum, both)]
    reduce_sum x6 -> x3, other arithmetic: 95.5 us -> 10.1 us  [the longest x2 9.96 us: body(): rows_of.append(jnp.sum(jnp.where(flipped == b, near_sum, 0.0), (1, 2, 3)))]
    unnamed x2 -> x0, blocking collectives: 82.5 us -> none
    cond x2 -> x0, local copies, waits for them, and re-layouts: 35.8 us -> none  [bias_block(): return lax.cond(distant, far_bias, near_bias)]
  transfers between devices with their start and end apart: 16 -> 8, of which waited for: 9 -> 3; matrix products, arithmetic and copies ran while one was open for 38% -> 15% of each run, Pallas kernels for 0% -> 9%
where the time goes in v1:
time: 631 us; the launch traced here: 622 us
  Pallas kernels  243 us (39%)
  waiting for transfers between devices  159 us (25%)
  blocking collectives  99.1 us (16%)
  other arithmetic  54.7 us (9%)
  local copies, waits for them, and re-layouts  45.3 us (7%)
  between operations  15.9 us (3%)
    reduce_scatter x1, waiting for transfers between devices, body(): lax.psum_scatter(g_second, both, scatter_dimension=0, tiled=True)  120 us
    psum x1, blocking collectives, body(): grad_table = lax.psum(table_sum, both)  99.1 us
    pallas_call x1, Pallas kernels, middle_call(): pl.pallas_call(functools.partial(middle_kernel, seq=total // lengths.shap...  84 us
    pallas_call x1, Pallas kernels, attend_back_call(): pl.pallas_call(functools.partial(attend_back_kernel, keys=keys, queries=q...  78.2 us
    pallas_call x1, Pallas kernels, attend_call(): pl.pallas_call(functools.partial(attend_kernel, rows=rows), grid=(pairs,...  45.1 us
    select_n x2, other arithmetic, bias_tiles(): tiles = jnp.where(buckets == b, table[b][:, None, None, None], tiles)  35.2 us
    ppermute x2, waiting for transfers between devices, to_documents(): lax.ppermute(piece, 'blk', [(i, (i + hop) % ways) for i in range(ways)])  26.5 us
    pallas_call x1, Pallas kernels, last_call(): pl.pallas_call(last_kernel, grid=(total // rows,), in_specs=[row] * 5 + [...  24.2 us
  transfers between devices with their start and end apart: 8, of which 3 were waited for; matrix products, arithmetic and copies ran while one was open for 15% of the time, Pallas kernels for 9%

profile of v1, /device:TPU:0, one launch (start us, length us, event | category | flops | bytes accessed | tf_op | source)
XLA Modules:
  0.0 622.1 jit_solution(12074246318989296621)
XLA Ops:
  8.2 1.5 fusion.17
  9.7 1.7 pad_maximum_fusion
  11.6 2.7 dynamic-slice_bitcast_fusion.1
  14.2 3.0 collective-permute-start
  20.5 3.5 broadcast_compare_fusion.52
  24.6 11.6 %select_select_fusion.near_ref = f32[12,3,128,128]{3,2,1,0:T(8,128)} fusion(f32[12]{0:T(128)} %get-tuple-element.150, f32[12]{0:T(128)} %get-tuple-element.151, f32[12]{0:T(128)} %get-tuple-element.152, f32[12]{0:T(128)} %get-tuple-element.153, f32[12]{0:T(128)} %get-tuple-element.154, f32[12]{0:T(128)} %get-tuple-element.155, f32[12]{0:T(128)} %get-tuple-element.156, ...), kind=kLoop, calls=%fused_computation.32 | loop fusion | flops 18874368 | bytes 3933696 | tf_op jit(solution)/shard_map/jit(_where)/select_n | solution.py:482
  38.1 1.6 bitcast_dynamic-update-slice_fusion.5
  39.7 1.9 broadcast.611.clone.1
  44.6 23.6 %select_select_fusion.1.near_ref = f32[12,3,128,128]{3,2,1,0:T(8,128)} fusion(f32[12]{0:T(128)} %get-tuple-element.150, f32[12]{0:T(128)} %get-tuple-element.151, f32[12]{0:T(128)} %get-tuple-element.152, f32[12]{0:T(128)} %get-tuple-element.153, f32[12]{0:T(128)} %get-tuple-element.154, f32[12]{0:T(128)} %get-tuple-element.155, f32[12]{0:T(128)} %get-tuple-element.156, ...), kind=kLoop, calls=%fused_computation.33 | loop fusion | flops 18874368 | bytes 3933696 | tf_op jit(solution)/shard_map/jit(_where)/select_n | solution.py:482
  68.2 1.6 constant_dynamic-update-slice_fusion.1
  69.8 26.5 %collective-permute-done.1 = bf16[2,512,768]{2,1,0:T(8,128)(2,1)} collective-permute-done((bf16[2,512,768]{2,1,0:T(8,128)(2,1)}, bf16[2,512,768]{2,1,0:T(8,128)(2,1)}, u32[]{:S(2)}, u32[]{:S(2)}) %collective-permute-start.1) | collective-permute-done | bytes 1572896 | tf_op jit(solution)/shard_map/ppermute | solution.py:433
  96.3 2.7 constant_dynamic-update-slice_fusion
  100.8 1.7 copy.47.gain_ref
  103.2 11.7 %qkv.1 = (bf16[2048,768]{1,0:T(8,128)(2,1)}, bf16[2048,768]{1,0:T(8,128)(2,1)}, bf16[2048,768]{1,0:T(8,128)(2,1)}) custom-call(bf16[2048,768]{1,0:T(8,128)(2,1)} %bitcast.65, f32[1,768]{1,0:T(1,128)} %copy.47.gain_ref, bf16[768,2432]{1,0:T(8,128)(2,1)} %all-gather.3.cloned.1.call-done.w_ref), custom_call_target="tpu_custom_call" | custom-call | tf_op jit(solution)/shard_map/qkv/pallas_call | solution.py:68
  115.0 45.1 %attend.1 = (bf16[2048,768]{1,0:T(8,128)(2,1)}, f32[2,6,2,1024]{3,2,1,0:T(2,128)}) custom-call(s32[2]{0:T(128)} %fusion.18.len_ref, f32[12,2]{1,0:T(8,128)} %copy.48.far_ref, bf16[2048,768]{1,0:T(8,128)(2,1)} %get-tuple-element.52.q_ref, bf16[2048,768]{1,0:T(8,128)(2,1)} %get-tuple-element.53.k_ref, bf16[2048,768]{1,0:T(8,128)(2,1)} %get-tuple-element.54.v_ref, ...), custom_call_target="tpu_custom_call" | custom-call | tf_op jit(solution)/shard_map/attend/pallas_call | solution.py:125
  160.0 11.5 %all-gather.5.cloned.1.call-done.w_ref = bf16[768,6912]{1,0:T(8,128)(2,1)} async-done(((bf16[24,6912]{1,0:T(8,128)(2,1)}), bf16[768,6912]{1,0:T(8,128)(2,1)}) %all-gather.5.cloned.1.call-update) | async-done | bytes 10616848 | tf_op jit(solution)/shard_map/all_gather | solution.py:508
  171.5 84.0 %middle.1 = (bf16[2048,768]{1,0:T(8,128)(2,1)}, bf16[2048,768]{1,0:T(8,128)(2,1)}, bf16[2048,768]{1,0:T(8,128)(2,1)}, bf16[768,6912]{1,0:T(8,128)(2,1)}, f32[1,768]{1,0:T(1,128)}) custom-call(s32[2]{0:T(128)} %fusion.18.len_ref, bf16[2048,768]{1,0:T(8,128)(2,1)} %bitcast.66, bf16[2048,768]{1,0:T(8,128)(2,1)} %get-tuple-element.55.heads_ref.o_ref, ...), custom_call_target="tpu_custom_call" | custom-call | tf_op jit(solution)/shard_map/middle/pallas_call | solution.py:210
  255.6 78.2 %attend_back.1 = (bf16[2048,768]{1,0:T(8,128)(2,1)}, bf16[2048,768]{1,0:T(8,128)(2,1)}, bf16[2048,768]{1,0:T(8,128)(2,1)}, f32[12,3,128,128]{3,2,1,0:T(8,128)}, f32[12,2,8,128]{3,2,1,0:T(8,128)}) custom-call(s32[2]{0:T(128)} %fusion.18.len_ref, f32[12,2]{1,0:T(8,128)} %copy.48.far_ref, bf16[2048,768]{1,0:T(8,128)(2,1)} %get-tuple-element.52.q_ref, ...), custom_call_target="tpu_custom_call" | custom-call | tf_op jit(solution)/shard_map/attend_back/pallas_call | solution.py:324
  333.8 24.2 %last.1 = (bf16[2048,768]{1,0:T(8,128)(2,1)}, bf16[768,2432]{1,0:T(8,128)(2,1)}) custom-call(bf16[2048,768]{1,0:T(8,128)(2,1)} %bitcast.67, bf16[2048,768]{1,0:T(8,128)(2,1)} %get-tuple-element.59.dq_ref, bf16[2048,768]{1,0:T(8,128)(2,1)} %get-tuple-element.60.dk_ref, bf16[2048,768]{1,0:T(8,128)(2,1)} %get-tuple-element.61.dv_ref, ...), custom_call_target="tpu_custom_call" | custom-call | tf_op jit(solution)/shard_map/last/pallas_call | solution.py:405
  358.6 2.9 constant_dynamic-slice_fusion.1
  361.6 1.5 collective-permute-start.3
  365.3 5.8 select_reduce_fusion
  371.3 4.2 select_reduce_fusion.18
  375.9 99.1 %psum.7 = f32[32,12]{1,0:T(8,128)S(1)} all-reduce(f32[32,12]{1,0:T(8,128)S(1)} %scatter-add.9), channel_id=1, replica_groups=mesh['dp'=16,'blk'=2] {'dp','blk'}, use_global_device_ids=true, to_apply=%region_35.36 | all-reduce | flops 384 | bytes 3072 | tf_op jit(solution)/shard_map/psum | solution.py:553
  475.7 1.9 reshape.171.clone.1
  480.1 1.9 reshape.171.clone
  483.2 2.7 bitcast_dynamic-update-slice_fusion
  486.0 2.7 bitcast_dynamic-update-slice_fusion.2
  490.4 1.5 fusion.21
  491.9 120.0 %reduce-scatter.5.cloned.1.call-done = bf16[24,6912]{1,0:T(8,128)(2,1)} async-done(((bf16[768,6912]{1,0:T(8,128)(2,1)}), bf16[24,6912]{1,0:T(8,128)(2,1)}) %reduce-scatter.5.cloned.1.call-update) | async-done | bytes 331792 | tf_op jit(solution)/shard_map/reduce_scatter | solution.py:556
  611.8 1.8 fusion.20
  613.7 1.4 slice.254
  (268 shorter events, 20.5 us)
Async XLA Ops:
  7.2 30.2 %copy-start = (s32[4,1]{0,1:T(1,128)S(1)}, s32[4,1]{0,1:T(1,128)}, u32[]{:S(2)}) copy-start(s32[4,1]{0,1:T(1,128)} %param.17) | copy-start | bytes 52
  7.2 91.7 %all-gather.3.cloned.1.call-start = ((), (), s32[]{:S(2)}) async-start(), calls=%async_computation.2 | async-start | bytes 3852288 | tf_op jit(solution)/shard_map/all_gather | solution.py:505
  9.7 161.8 %all-gather.5.cloned.1.call-start = ((), (), s32[]{:S(2)}) async-start(), calls=%async_computation.3 | async-start | bytes 10948608 | tf_op jit(solution)/shard_map/all_gather | solution.py:508
  11.5 477.2 %reduce-scatter.7.cloned.1.call-start = ((), (), s32[]{:S(2)}) async-start(), calls=%async_computation.5 | async-start | bytes 3852288
  14.2 53.9 %collective-permute-start = (bf16[2,512,768]{2,1,0:T(8,128)(2,1)}, bf16[2,512,768]{2,1,0:T(8,128)(2,1)}, u32[]{:S(2)}, u32[]{:S(2)}) collective-permute-start(bf16[2,512,768]{2,1,0:T(8,128)(2,1)} %dynamic-slice_bitcast_fusion.1), channel_id=1, source_target_pairs={{0,1},{1,0},{2,3},{3,2},{4,5},{5,4},{6,7},{7,6},{8,9},{9,8},{10,11... | collective-permute-start | bytes 4718600 | tf_op jit(solution)/shard_map/ppermute | solution.py:433
  18.4 77.8 %collective-permute-start.1 = (bf16[2,512,768]{2,1,0:T(8,128)(2,1)}, bf16[2,512,768]{2,1,0:T(8,128)(2,1)}, u32[]{:S(2)}, u32[]{:S(2)}) collective-permute-start(bf16[2,512,768]{2,1,0:T(8,128)(2,1)} %dynamic-slice_bitcast_fusion), channel_id=1, source_target_pairs={{0,1},{1,0},{2,3},{3,2},{4,5},{5,4},{6,7},{7,6},{8,9},{9,8},{10,11... | collective-permute-start | bytes 4718600 | tf_op jit(solution)/shard_map/ppermute | solution.py:433
  19.4 16.9 %copy-start.98 = (f32[12]{0:T(128)}, f32[12]{0:T(128)S(1)}, u32[]{:S(2)}) copy-start(f32[12]{0:T(128)S(1)} %get-tuple-element.169) | copy-start | bytes 148
  19.4 16.9 %copy-start.100 = (f32[12]{0:T(128)}, f32[12]{0:T(128)S(1)}, u32[]{:S(2)}) copy-start(f32[12]{0:T(128)S(1)} %get-tuple-element.170) | copy-start | bytes 148
  19.4 16.9 %copy-start.102 = (f32[12]{0:T(128)}, f32[12]{0:T(128)S(1)}, u32[]{:S(2)}) copy-start(f32[12]{0:T(128)S(1)} %get-tuple-element.171) | copy-start | bytes 148
  19.4 16.9 %copy-start.104 = (f32[12]{0:T(128)}, f32[12]{0:T(128)S(1)}, u32[]{:S(2)}) copy-start(f32[12]{0:T(128)S(1)} %get-tuple-element.172) | copy-start | bytes 148
  19.4 16.9 %copy-start.106 = (f32[12]{0:T(128)}, f32[12]{0:T(128)S(1)}, u32[]{:S(2)}) copy-start(f32[12]{0:T(128)S(1)} %get-tuple-element.173) | copy-start | bytes 148
  19.4 16.9 %copy-start.108 = (f32[12]{0:T(128)}, f32[12]{0:T(128)S(1)}, u32[]{:S(2)}) copy-start(f32[12]{0:T(128)S(1)} %get-tuple-element.174) | copy-start | bytes 148
  19.4 16.9 %copy-start.110 = (f32[12]{0:T(128)}, f32[12]{0:T(128)S(1)}, u32[]{:S(2)}) copy-start(f32[12]{0:T(128)S(1)} %get-tuple-element.175) | copy-start | bytes 148
  24.0 12.3 %copy-start.10 = (pred[3,128,128]{2,1,0:T(8,128)(4,1)}, pred[3,128,128]{2,1,0:T(8,128)(4,1)S(1)}, u32[]{:S(2)}) copy-start(pred[3,128,128]{2,1,0:T(8,128)(4,1)S(1)} %get-tuple-element.207) | copy-start | bytes 147460
  24.0 12.3 %copy-start.12 = (pred[3,128,128]{2,1,0:T(8,128)(4,1)}, pred[3,128,128]{2,1,0:T(8,128)(4,1)S(1)}, u32[]{:S(2)}) copy-start(pred[3,128,128]{2,1,0:T(8,128)(4,1)S(1)} %get-tuple-element.208) | copy-start | bytes 147460
  24.0 12.3 %copy-start.14 = (pred[3,128,128]{2,1,0:T(8,128)(4,1)}, pred[3,128,128]{2,1,0:T(8,128)(4,1)S(1)}, u32[]{:S(2)}) copy-start(pred[3,128,128]{2,1,0:T(8,128)(4,1)S(1)} %get-tuple-element.209) | copy-start | bytes 147460
  24.0 12.3 %copy-start.16 = (pred[3,128,128]{2,1,0:T(8,128)(4,1)}, pred[3,128,128]{2,1,0:T(8,128)(4,1)S(1)}, u32[]{:S(2)}) copy-start(pred[3,128,128]{2,1,0:T(8,128)(4,1)S(1)} %get-tuple-element.210) | copy-start | bytes 147460
  24.0 12.3 %copy-start.18 = (pred[3,128,128]{2,1,0:T(8,128)(4,1)}, pred[3,128,128]{2,1,0:T(8,128)(4,1)S(1)}, u32[]{:S(2)}) copy-start(pred[3,128,128]{2,1,0:T(8,128)(4,1)S(1)} %get-tuple-element.211) | copy-start | bytes 147460
  24.1 12.3 %copy-start.20 = (pred[3,128,128]{2,1,0:T(8,128)(4,1)}, pred[3,128,128]{2,1,0:T(8,128)(4,1)S(1)}, u32[]{:S(2)}) copy-start(pred[3,128,128]{2,1,0:T(8,128)(4,1)S(1)} %get-tuple-element.212) | copy-start | bytes 147460
  24.1 12.3 %copy-start.22 = (pred[3,128,128]{2,1,0:T(8,128)(4,1)}, pred[3,128,128]{2,1,0:T(8,128)(4,1)S(1)}, u32[]{:S(2)}) copy-start(pred[3,128,128]{2,1,0:T(8,128)(4,1)S(1)} %get-tuple-element.213) | copy-start | bytes 147460
  24.1 12.3 %copy-start.24 = (pred[3,128,128]{2,1,0:T(8,128)(4,1)}, pred[3,128,128]{2,1,0:T(8,128)(4,1)S(1)}, u32[]{:S(2)}) copy-start(pred[3,128,128]{2,1,0:T(8,128)(4,1)S(1)} %get-tuple-element.214) | copy-start | bytes 147460
  24.1 12.3 %copy-start.26 = (pred[3,128,128]{2,1,0:T(8,128)(4,1)}, pred[3,128,128]{2,1,0:T(8,128)(4,1)S(1)}, u32[]{:S(2)}) copy-start(pred[3,128,128]{2,1,0:T(8,128)(4,1)S(1)} %get-tuple-element.215) | copy-start | bytes 147460
  24.1 12.3 %copy-start.28 = (pred[3,128,128]{2,1,0:T(8,128)(4,1)}, pred[3,128,128]{2,1,0:T(8,128)(4,1)S(1)}, u32[]{:S(2)}) copy-start(pred[3,128,128]{2,1,0:T(8,128)(4,1)S(1)} %get-tuple-element.216) | copy-start | bytes 147460
  24.1 12.3 %copy-start.30 = (pred[3,128,128]{2,1,0:T(8,128)(4,1)}, pred[3,128,128]{2,1,0:T(8,128)(4,1)S(1)}, u32[]{:S(2)}) copy-start(pred[3,128,128]{2,1,0:T(8,128)(4,1)S(1)} %get-tuple-element.217) | copy-start | bytes 147460
  24.1 12.3 %copy-start.32 = (pred[3,128,128]{2,1,0:T(8,128)(4,1)}, pred[3,128,128]{2,1,0:T(8,128)(4,1)S(1)}, u32[]{:S(2)}) copy-start(pred[3,128,128]{2,1,0:T(8,128)(4,1)S(1)} %get-tuple-element.218) | copy-start | bytes 147460
  24.1 12.3 %copy-start.34 = (pred[3,128,128]{2,1,0:T(8,128)(4,1)}, pred[3,128,128]{2,1,0:T(8,128)(4,1)S(1)}, u32[]{:S(2)}) copy-start(pred[3,128,128]{2,1,0:T(8,128)(4,1)S(1)} %get-tuple-element.219) | copy-start | bytes 147460
  24.1 12.3 %copy-start.36 = (pred[3,128,128]{2,1,0:T(8,128)(4,1)}, pred[3,128,128]{2,1,0:T(8,128)(4,1)S(1)}, u32[]{:S(2)}) copy-start(pred[3,128,128]{2,1,0:T(8,128)(4,1)S(1)} %get-tuple-element.188) | copy-start | bytes 147460
  69.7 31.0 %copy-start.2 = (bf16[2,1024,768]{2,1,0:T(8,128)(2,1)}, bf16[2,1024,768]{2,1,0:T(8,128)(2,1)S(1)}, u32[]{:S(2)}) copy-start(bf16[2,1024,768]{2,1,0:T(8,128)(2,1)S(1)} %constant_dynamic-update-slice_fusion.1) | copy-start | bytes 9437188
  358.0 253.8 %reduce-scatter.5.cloned.1.call-start = ((), (), s32[]{:S(2)}) async-start(), calls=%async_computation.4 | async-start | bytes 10948608 | tf_op jit(solution)/shard_map/reduce_scatter | solution.py:556
  361.6 121.6 %collective-permute-start.3 = (bf16[2,512,768]{2,1,0:T(8,128)(2,1)}, bf16[2,512,768]{2,1,0:T(8,128)(2,1)}, u32[]{:S(2)}, u32[]{:S(2)}) collective-permute-start(bf16[2,512,768]{2,1,0:T(8,128)(2,1)} %constant_dynamic-slice_fusion.1), channel_id=1, source_target_pairs={{0,1},{1,0},{2,3},{3,2},{4,5},{5,4},{6,7},{7,6},{8,9},{9,8},{10,11... | collective-permute-start | bytes 4718600 | tf_op jit(solution)/shard_map/ppermute | solution.py:453
  364.5 121.5 %collective-permute-start.2 = (bf16[2,512,768]{2,1,0:T(8,128)(2,1)}, bf16[2,512,768]{2,1,0:T(8,128)(2,1)}, u32[]{:S(2)}, u32[]{:S(2)}) collective-permute-start(bf16[2,512,768]{2,1,0:T(8,128)(2,1)} %constant_dynamic-slice_fusion), channel_id=1, source_target_pairs={{0,1},{1,0},{2,3},{3,2},{4,5},{5,4},{6,7},{7,6},{8,9},{9,8},{10,11... | collective-permute-start | bytes 4718600 | tf_op jit(solution)/shard_map/ppermute | solution.py:453
  483.2 131.8 %copy-start.1 = (s32[4,1]{0,1:T(1,128)S(1)}, s32[4,1]{0,1:T(1,128)}, u32[]{:S(2)}) copy-start(s32[4,1]{0,1:T(1,128)} %param.17) | copy-start | bytes 52
  (88 other events, 463.6 us)
Sparse Core Ops, SparseCore 0:
  11.5 70.3 all-gather.2
  84.8 86.7 all-gather.4
  358.1 106.8 reduce-scatter.6
  471.0 140.7 reduce-scatter.4

commit v2 on v1

--- a/solution.py
+++ b/solution.py
@@ -53,6 +53,27 @@
 SMEM = pl.BlockSpec(memory_space=pltpu.SMEM)
 
 
+def tile_buckets(apart, keys_dim):
+    keys = lax.broadcasted_iota(jnp.int32, (SUB, SUB), keys_dim)
+    queries = lax.broadcasted_iota(jnp.int32, (SUB, SUB), 1 - keys_dim)
+    return bucket_of(keys - queries + SUB * apart)
+
+
+def tile_range(apart):
+    return range(0 if apart <= 0 else 16, 16 if apart < 0 else 32)
+
+
+def fill_tiles(near, table_ref, pair, keys_dim):
+    for apart in (-1, 0, 1):
+        buckets = tile_buckets(apart, keys_dim)
+        masks = [(b, buckets == b) for b in tile_range(apart)]
+        for h in range(2):
+            tile = jnp.zeros((SUB, SUB), f32)
+            for b, mask in masks:
+                tile = jnp.where(mask, table_ref[2 * pair + h, b], tile)
+            near[h, apart + 1] = tile
+
+
 def qkv_kernel(x_ref, gain_ref, w_ref, q_ref, k_ref, v_ref):
     width = q_ref.shape[1]
     normed, _ = norm_rows(x_ref[...].astype(f32))
@@ -77,9 +98,14 @@
 
 
 def attend_kernel(
-    len_ref, far_ref, q_ref, k_ref, v_ref, near_ref, o_ref, lse_ref, *, rows
+    len_ref, table_ref, q_ref, k_ref, v_ref, o_ref, lse_ref, near_ref, *, rows
 ):
     pair, doc = pl.program_id(0), pl.program_id(1)
+
+    @pl.when(doc == 0)
+    def _():
+        fill_tiles(near_ref, table_ref, pair, 1)
+
     seq = q_ref.shape[0]
     subs = seq // SUB
     first = lax.broadcasted_iota(jnp.int32, (1, 128), 1) < 64
@@ -101,11 +127,11 @@
                 low, high = max(at - 1, 0), min(at + 2, subs)
                 parts = []
                 if low > 0:
-                    parts.append(strip[:, : low * SUB] + far_ref[2 * pair + h, 0])
+                    parts.append(strip[:, : low * SUB] + table_ref[2 * pair + h, 15])
                 for b in range(low, high):
                     parts.append(strip[:, b * SUB : (b + 1) * SUB] + near_ref[h, b - at + 1])
                 if high < subs:
-                    parts.append(strip[:, high * SUB :] + far_ref[2 * pair + h, 1])
+                    parts.append(strip[:, high * SUB :] + table_ref[2 * pair + h, 31])
                 strips.append(jnp.concatenate(parts, 1))
             scores = jnp.where(live, jnp.concatenate(strips, 0), NEG)
             top = jnp.max(scores, 1, keepdims=True)
@@ -118,7 +144,7 @@
         lse_ref[0, 0, 1:2, span] = log_total[64:65]
 
 
-def attend_call(lengths, far, q, k, v, near, rows=512):
+def attend_call(lengths, table, q, k, v, rows=512):
     docs, (total, width) = lengths.shape[0], q.shape
     seq, pairs = total // docs, width // 128
     slab = pl.BlockSpec((seq, 128), lambda p, d: (d, p))
@@ -131,13 +157,13 @@
             slab,
             slab,
             slab,
-            pl.BlockSpec((2, 3, SUB, SUB), lambda p, d: (p, 0, 0, 0)),
         ],
         out_specs=[slab, pl.BlockSpec((1, 1, 2, seq), lambda p, d: (d, p, 0, 0))],
         out_shape=[struct((total, width)), struct((docs, pairs, 2, seq), f32)],
+        scratch_shapes=[pltpu.VMEM((2, 3, SUB, SUB), f32)],
         compiler_params=params(),
         name="attend",
-    )(lengths, far, q, k, v, near)
+    )(lengths, table, q, k, v)
 
 
 def middle_kernel(
@@ -221,17 +247,18 @@
 
 def attend_back_kernel(
     len_ref,
-    far_ref,
+    table_ref,
     q_ref,
     k_ref,
     v_ref,
     grad_ref,
     o_ref,
     lse_ref,
-    near_ref,
     dq_ref,
     dk_ref,
     dv_ref,
+    table_sum,
+    near_ref,
     near_sum,
     far_sum,
     acc,
@@ -259,6 +286,7 @@
 
     @pl.when(doc == 0)
     def _():
+        fill_tiles(near_ref, table_ref, pair, 0)
         near_sum[...] = jnp.zeros_like(near_sum)
         far_sum[...] = jnp.zeros_like(far_sum)
 
@@ -277,7 +305,7 @@
                 scores = dot(k, q_one[h][span], NT)
                 prob_grad = dot(v, g_one[h][span], NT)
                 lse = lse_ref[0, 0, h : h + 1, span]
-                lse_side = (lse - far_ref[2 * pair + h, 0], lse - far_ref[2 * pair + h, 1])
+                lse_side = (lse - table_ref[2 * pair + h, 15], lse - table_ref[2 * pair + h, 31])
                 row_delta = delta[h : h + 1, span]
                 prob_rows, grad_rows = [], []
                 for a in range(keys // SUB):
@@ -314,13 +342,29 @@
         dk_ref[held, :] = (dk * (1 / LOG2E)).astype(low_type)
     dq_ref[...] = (acc[...] * 0.125).astype(low_type)
 
-
-def attend_back_call(lengths, far, q, k, v, grad, o, lse, near, keys=256, queries=1024):
+    @pl.when(doc == pl.num_programs(1) - 1)
+    def _():
+        sums = {}
+        for apart in (-1, 0, 1):
+            buckets = tile_buckets(apart, 0)
+            masks = [(b, buckets == b) for b in tile_range(apart)]
+            for h in range(2):
+                tile = near_sum[h, apart + 1]
+                for b, mask in masks:
+                    part = jnp.sum(jnp.where(mask, tile, 0.0), 0, keepdims=True)
+                    sums[h, b] = sums[h, b] + part if (h, b) in sums else part
+        for h in range(2):
+            for side, b in enumerate((15, 31)):
+                sums[h, b] = sums[h, b] + jnp.sum(far_sum[h, side], 0, keepdims=True)
+            for b in range(32):
+                table_sum[h, b : b + 1] = sums[h, b]
+
+
+def attend_back_call(lengths, table, q, k, v, grad, o, lse, keys=256, queries=1024):
     docs, (total, width) = lengths.shape[0], q.shape
     seq, pairs = total // docs, width // 128
     queries = min(queries, seq)
     slab = pl.BlockSpec((seq, 128), lambda p, d: (d, p))
-    tiles = pl.BlockSpec((2, 3, SUB, SUB), lambda p, d: (p, 0, 0, 0))
     return pl.pallas_call(
         functools.partial(attend_back_kernel, keys=keys, queries=queries),
         grid=(pairs, docs),
@@ -333,21 +377,18 @@
             slab,
             slab,
             pl.BlockSpec((1, 1, 2, seq), lambda p, d: (d, p, 0, 0)),
-            tiles,
         ],
-        out_specs=[
-            slab,
-            slab,
-            slab,
-            tiles,
-            pl.BlockSpec((2, 2, 8, SUB), lambda p, d: (p, 0, 0, 0)),
+        out_specs=[slab, slab, slab, pl.BlockSpec((2, 32, SUB), lambda p, d: (p, 0, 0))],
+        out_shape=[struct((total, width))] * 3 + [struct((2 * pairs, 32, SUB), f32)],
+        scratch_shapes=[
+            pltpu.VMEM((2, 3, SUB, SUB), f32),
+            pltpu.VMEM((2, 3, SUB, SUB), f32),
+            pltpu.VMEM((2, 2, 8, SUB), f32),
+            pltpu.VMEM((seq, 128), f32),
         ],
-        out_shape=[struct((total, width))] * 3
-        + [struct((2 * pairs, 3, SUB, SUB), f32), struct((2 * pairs, 2, 8, SUB), f32)],
-        scratch_shapes=[pltpu.VMEM((seq, 128), f32)],
         compiler_params=params(),
         name="attend_back",
-    )(lengths, far, q, k, v, grad, o, lse, near)
+    )(lengths, table, q, k, v, grad, o, lse)
 
 
 def last_kernel(
@@ -412,6 +453,424 @@
         compiler_params=params(),
         name="last",
     )(x, dq, dk, dv, mid, gain, w_first, gn_second)
+
+
+MESH_ID = pl.DeviceIdType.MESH
+ANY = pl.BlockSpec(memory_space=pl.ANY)
+VMEM_WHOLE = pl.BlockSpec(memory_space=pltpu.VMEM)
+SPARE = 128
+
+
+class Place:
+    def __init__(self):
+        self.dp, self.y = lax.axis_index("dp"), lax.axis_index("blk")
+        self.depth = lax.axis_size("dp") // 4
+        self.z = self.dp // 4
+        self.x = lax.rem(self.dp // 2, 2)
+        self.core = lax.rem(self.dp, 2)
+        self.has_left = self.z > 0
+        self.has_right = self.z < self.depth - 1
+
+    def unit(self, z, x, core):
+        return (z * 2 + x) * 2 + core
+
+    def left(self):
+        return (self.dp - 4, self.y)
+
+    def right(self):
+        return (self.dp + 4, self.y)
+
+    def over_x(self):
+        return (self.unit(self.z, 1 - self.x, self.core), self.y)
+
+    def over_core(self):
+        return (self.unit(self.z, self.x, 1 - self.core), self.y)
+
+    def over_y(self):
+        return (self.dp, 1 - self.y)
+
+    def greet(self):
+        barrier = pltpu.get_barrier_semaphore()
+        for target in (self.over_x(), self.over_core(), self.over_y()):
+            pl.semaphore_signal(barrier, device_id=target, device_id_type=MESH_ID)
+
+        @pl.when(self.has_left)
+        def _():
+            pl.semaphore_signal(barrier, device_id=self.left(), device_id_type=MESH_ID)
+
+        @pl.when(self.has_right)
+        def _():
+            pl.semaphore_signal(barrier, device_id=self.right(), device_id_type=MESH_ID)
+
+        ends = self.has_left.astype(jnp.int32) + self.has_right.astype(jnp.int32)
+        pl.semaphore_wait(barrier, 3 + ends)
+
+
+def remote(source, target, send, recv, device):
+    return pltpu.make_async_remote_copy(
+        src_ref=source,
+        dst_ref=target,
+        send_sem=send,
+        recv_sem=recv,
+        device_id=device,
+        device_id_type=MESH_ID,
+    )
+
+
+def head_kernel(
+    shard_ref, tokens_ref, w_ref, x_ref, other, pair, send_sem, recv_sem, swap_sem, local_sem
+):
+    place = Place()
+    depth, unit_rows = place.depth, pair.shape[0]
+    own_rows = unit_rows // 2
+    per, rows = x_ref.shape[0], tokens_ref.shape[1]
+    place.greet()
+
+    def unit_at(u):
+        return w_ref.at[pl.ds(pl.multiple_of(u * unit_rows, 16), unit_rows)]
+
+    meet = remote(shard_ref, other, swap_sem.at[0], swap_sem.at[1], place.over_y())
+    meet.start()
+    target = x_ref.at[:, pl.ds(pl.multiple_of(place.y * rows, 16), rows)]
+    swap = remote(
+        tokens_ref.at[pl.ds((1 - place.y) * per, per)],
+        target,
+        swap_sem.at[2],
+        swap_sem.at[3],
+        place.over_y(),
+    )
+    swap.start()
+    keep = pltpu.make_async_copy(tokens_ref.at[pl.ds(place.y * per, per)], target, local_sem.at[0])
+    keep.start()
+    meet.wait()
+    mine, theirs = shard_ref[:own_rows].astype(f32), other[:own_rows].astype(f32)
+    is_first = place.y == 0
+    pair[...] = jnp.concatenate(
+        [jnp.where(is_first, mine, theirs), jnp.where(is_first, theirs, mine)], 0
+    ).astype(low_type)
+    mine_at = place.unit(place.z, place.x, place.core)
+    put = pltpu.make_async_copy(pair, unit_at(mine_at), local_sem.at[1])
+    put.start()
+
+    def sends(u, source, kinds):
+        out = []
+        for kind in kinds:
+            device = (place.left, place.right, place.over_x, place.over_core)[kind]()
+            out.append(remote(source, unit_at(u), send_sem.at[kind, u], recv_sem.at[u], device))
+        return out
+
+    def arrival(u):
+        remote(
+            unit_at(u), unit_at(u), send_sem.at[3, u], recv_sem.at[u], place.over_core()
+        ).wait_recv()
+
+    for copy in sends(mine_at, pair, (2, 3)):
+        copy.start()
+    for kind, there in ((0, place.has_left), (1, place.has_right)):
+
+        @pl.when(there)
+        def _(kind=kind):
+            sends(mine_at, pair, (kind,))[0].start()
+
+    for step in range(1, depth):
+        for kind, z in ((1, place.z - step), (0, place.z + step)):
+            u = place.unit(z, place.x, place.core)
+            onward = place.has_right if kind == 1 else place.has_left
+
+            @pl.when((z >= 0) & (z < depth))
+            def _(u=u, kind=kind, onward=onward):
+                arrival(u)
+
+                @pl.when(onward)
+                def _():
+                    sends(u, unit_at(u), (kind,))[0].start()
+
+                for copy in sends(u, unit_at(u), (2, 3)):
+                    copy.start()
+
+    for z in range(depth):
+        u = place.unit(z, 1 - place.x, place.core)
+        arrival(u)
+        sends(u, unit_at(u), (3,))[0].start()
+    for z in range(depth):
+        for x in range(2):
+            arrival(place.unit(z, x, 1 - place.core))
+    put.wait()
+    keep.wait()
+    for z in range(depth):
+        u = place.unit(z, place.x, place.core)
+        for copy in sends(u, unit_at(u), (2, 3)):
+            copy.wait_send()
+
+        @pl.when((place.z >= z) & place.has_right)
+        def _(u=u):
+            sends(u, unit_at(u), (1,))[0].wait_send()
+
+        @pl.when((place.z <= z) & place.has_left)
+        def _(u=u):
+            sends(u, unit_at(u), (0,))[0].wait_send()
+
+        u = place.unit(z, 1 - place.x, place.core)
+        sends(u, unit_at(u), (3,))[0].wait_send()
+    swap.wait()
+
+
+def head_call(shard, tokens, ways):
+    units = lax.axis_size("dp")
+    count, rows, width = tokens.shape
+    own_rows, columns = shard.shape
+    padded = jnp.pad(shard, ((0, -own_rows % 16), (0, 0)))
+    return pl.pallas_call(
+        head_kernel,
+        in_specs=[VMEM_WHOLE, ANY],
+        out_specs=[ANY, ANY],
+        out_shape=[
+            struct((units * ways * own_rows, columns)),
+            struct((count // ways, rows * ways, width)),
+        ],
+        scratch_shapes=[
+            pltpu.VMEM(padded.shape, low_type),
+            pltpu.VMEM((ways * own_rows, columns), low_type),
+            pltpu.SemaphoreType.DMA((4, units)),
+            pltpu.SemaphoreType.DMA((units,)),
+            pltpu.SemaphoreType.DMA((4,)),
+            pltpu.SemaphoreType.DMA((2,)),
+        ],
+        compiler_params=pltpu.CompilerParams(
+            collective_id=1, has_side_effects=True, vmem_limit_bytes=VMEM
+        ),
+        name="head",
+    )(padded, tokens)
+
+
+def tail_kernel(
+    g_ref,
+    gt_ref,
+    table_ref,
+    gq_ref,
+    gk_ref,
+    gv_ref,
+    gain_ref,
+    out_ref,
+    table_out,
+    core_buf,
+    x_send,
+    x_buf,
+    z_send,
+    z_buf,
+    y_send,
+    y_buf,
+    table_send,
+    table_buf,
+    core_sem,
+    x_sem,
+    z_sem,
+    y_sem,
+    table_sem,
+    local_sem,
+):
+    place = Place()
+    depth, unit_rows = place.depth, core_buf.shape[2]
+    own_rows, width = unit_rows // 2, gq_ref.shape[1]
+    per, rows = gt_ref.shape[0], out_ref.shape[1]
+    place.greet()
+    target = out_ref.at[pl.ds(place.y * per, per)]
+    swap = remote(
+        gt_ref.at[:, pl.ds(pl.multiple_of((1 - place.y) * rows, 16), rows)],
+        target,
+        y_sem.at[2],
+        y_sem.at[3],
+        place.over_y(),
+    )
+    keep = pltpu.make_async_copy(
+        gt_ref.at[:, pl.ds(pl.multiple_of(place.y * rows, 16), rows)], target, local_sem
+    )
+    order = []
+    for at in range((depth + 1) // 2):
+        order += [depth - 1 - at] + ([at] if at != depth - 1 - at else [])
+
+    def unit_at(u):
+        return g_ref.at[pl.ds(pl.multiple_of(u * unit_rows, 16), unit_rows)]
+
+    def over_core(side, z):
+        x = place.x if side == 0 else 1 - place.x
+        return remote(
+            unit_at(place.unit(z, x, 1 - place.core)),
+            core_buf.at[side, z],
+            core_sem.at[0, side, z],
+            core_sem.at[1, side, z],
+            place.over_core(),
+        )
+
+    def over_x(z):
+        return remote(x_send.at[z], x_buf.at[z], x_sem.at[0, z], x_sem.at[1, z], place.over_x())
+
+    def along(kind, z):
+        device = place.right() if kind else place.left()
+        return remote(
+            z_send.at[z], z_buf.at[kind, z], z_sem.at[0, z], z_sem.at[1 + kind, z], device
+        )
+
+    for side in (1, 0):
+        for z in order:
+            over_core(side, z).start()
+    swap.start()
+    keep.start()
+
+    tables = (
+        place.over_core(),
+        place.over_x(),
+        place.over_y(),
+    )
+    span = 1
+    while span < depth:
+        flip = place.z + span - 2 * span * lax.rem(place.z // span, 2)
+        tables += ((place.unit(flip, place.x, place.core), place.y),)
+        span *= 2
+    reduced = table_ref[...]
+
+    def table_copy(at):
+        return remote(
+            table_send.at[at], table_buf.at[at], table_sem.at[0, at], table_sem.at[1, at], tables[at]
+        )
+
+    def table_start(at, value):
+        table_send[at] = value
+        table_copy(at).start()
+
+    def table_finish(at, value):
+        table_copy(at).wait()
+        return value + table_buf[at]
+
+    table_start(0, reduced)
+    for z in order:
+        over_core(1, z).wait_recv()
+        mine = unit_at(place.unit(z, 1 - place.x, place.core))
+        x_send[z] = (mine[...].astype(f32) + core_buf[1, z].astype(f32)).astype(low_type)
+        over_x(z).start()
+    reduced = table_finish(0, reduced)
+    table_start(1, reduced)
+    at = 1
+    for z in order:
+        over_core(0, z).wait_recv()
+        over_x(z).wait_recv()
+        mine = unit_at(place.unit(z, place.x, place.core))
+        part = mine[...].astype(f32) + core_buf[0, z].astype(f32) + x_buf[z].astype(f32)
+        z_send[z] = part.astype(low_type)
+
+        @pl.when(place.z < z)
+        def _(z=z):
+            @pl.when(place.has_left)
+            def _():
+                along(1, z).wait_recv()
+                z_send[z] = (z_send[z].astype(f32) + z_buf[1, z].astype(f32)).astype(low_type)
+
+            along(1, z).start()
+
+        @pl.when(place.z > z)
+        def _(z=z):
+            @pl.when(place.has_right)
+            def _():
+                along(0, z).wait_recv()
+                z_send[z] = (z_send[z].astype(f32) + z_buf[0, z].astype(f32)).astype(low_type)
+
+            along(0, z).start()
+
+        if at < len(tables):
+            reduced = table_finish(at, reduced)
+            at += 1
+            if at < len(tables):
+                table_start(at, reduced)
+
+    for z in range(depth):
+
+        @pl.when(place.z == z)
+        def _(z=z):
+            @pl.when(place.has_left)
+            def _():
+                along(1, z).wait_recv()
+                z_send[z] = (z_send[z].astype(f32) + z_buf[1, z].astype(f32)).astype(low_type)
+
+            @pl.when(place.has_right)
+            def _():
+                along(0, z).wait_recv()
+                z_send[z] = (z_send[z].astype(f32) + z_buf[0, z].astype(f32)).astype(low_type)
+
+    total = z_send[place.z].astype(f32)
+    upper, lower = total[:own_rows], total[own_rows:]
+    is_first = place.y == 0
+    y_send[:own_rows] = jnp.where(is_first, lower, upper)
+    meet = remote(y_send, y_buf, y_sem.at[0], y_sem.at[1], place.over_y())
+    meet.start()
+    while at < len(tables):
+        reduced = table_finish(at, reduced)
+        at += 1
+        if at < len(tables):
+            table_start(at, reduced)
+    table_out[...] = reduced
+    meet.wait()
+    final = jnp.where(is_first, upper, lower) + y_buf[:own_rows]
+    gq_ref[...] = final[:, :width]
+    gk_ref[...] = final[:, width : 2 * width]
+    gv_ref[...] = final[:, 2 * width : 3 * width]
+    gain_ref[...] = final[:, 3 * width :]
+    for z in range(depth):
+        for side in (1, 0):
+            over_core(side, z).wait_send()
+        over_x(z).wait_send()
+
+        @pl.when(place.z < z)
+        def _(z=z):
+            along(1, z).wait_send()
+
+        @pl.when(place.z > z)
+        def _(z=z):
+            along(0, z).wait_send()
+
+    keep.wait()
+    swap.wait()
+
+
+def tail_call(grads, gt, table, ways):
+    units = lax.axis_size("dp")
+    depth = units // 4
+    steps = 3 + (depth - 1).bit_length()
+    per, seq, width = gt.shape
+    columns = grads.shape[1]
+    unit = grads.shape[0] // units
+    own = unit // ways
+    return pl.pallas_call(
+        tail_kernel,
+        in_specs=[VMEM_WHOLE, ANY, VMEM_WHOLE],
+        out_specs=[VMEM_WHOLE] * 4 + [ANY, VMEM_WHOLE],
+        out_shape=[struct((own, width), f32)] * 3
+        + [
+            struct((own, columns - 3 * width), f32),
+            struct((per * ways, seq // ways, width)),
+            struct(table.shape, f32),
+        ],
+        scratch_shapes=[
+            pltpu.VMEM((2, depth, unit, columns), low_type),
+            pltpu.VMEM((depth, unit, columns), low_type),
+            pltpu.VMEM((depth, unit, columns), low_type),
+            pltpu.VMEM((depth, unit, columns), low_type),
+            pltpu.VMEM((2, depth, unit, columns), low_type),
+            pltpu.VMEM((own, columns), f32),
+            pltpu.VMEM((own, columns), f32),
+            pltpu.VMEM((steps,) + table.shape, f32),
+            pltpu.VMEM((steps,) + table.shape, f32),
+            pltpu.SemaphoreType.DMA((2, 2, depth)),
+            pltpu.SemaphoreType.DMA((2, depth)),
+            pltpu.SemaphoreType.DMA((3, depth)),
+            pltpu.SemaphoreType.DMA((4,)),
+            pltpu.SemaphoreType.DMA((2, steps)),
+            pltpu.SemaphoreType.DMA,
+        ],
+        compiler_params=pltpu.CompilerParams(
+            collective_id=2, has_side_effects=True, vmem_limit_bytes=VMEM
+        ),
+        name="tail",
+    )(grads, gt, table)
 
 
 def sharing(count):
@@ -474,15 +933,6 @@
     return lax.dynamic_slice_in_dim(y, at, size, axis)
 
 
-def bias_tiles(table):
-    offset = jnp.arange(SUB)[None, :] - jnp.arange(SUB)[:, None]
-    buckets = bucket_of(offset[None] + SUB * jnp.arange(-1, 2)[:, None, None])
-    tiles = jnp.zeros((table.shape[1],) + buckets.shape, f32)
-    for b in range(table.shape[0]):
-        tiles = jnp.where(buckets == b, table[b][:, None, None, None], tiles)
-    return tiles, buckets
-
-
 def body(
     tokens,
     lengths,
@@ -501,20 +951,26 @@
     count = micro * docs
     per, share = sharing(count)
     both = ("dp", "blk")
-    gains = jnp.pad(jnp.stack([norm1_gain, norm2_gain], 1), ((0, 0), (0, 126)))
-    w_first = lax.all_gather(
-        jnp.concatenate([w_query, w_key, w_value, gains], 1), both, axis=0, tiled=True
-    )
-    w_second = lax.all_gather(
-        jnp.concatenate([w_out, w_in, w_down], 1), both, axis=0, tiled=True
-    )
+    direct = lax.axis_size("blk") == 2 and per * 2 == count and lax.axis_size("dp") % 4 == 0
+    gains = jnp.pad(jnp.stack([norm1_gain, norm2_gain], 1), ((0, 0), (0, SPARE - 2)))
+    shard_first = jnp.concatenate([w_query, w_key, w_value, gains], 1)
+    shard_second = jnp.concatenate([w_out, w_in, w_down], 1)
+    w_second = lax.all_gather(shard_second, both, axis=0, tiled=True)
+    tokens_here = tokens.reshape(count, rows, width)
+    cot_here = cotangent.reshape(count, rows, width)
+    if direct:
+        w_first, x = head_call(shard_first, tokens_here, 2)
+        x = x.reshape(-1, width)
+        cot_here, x = lax.optimization_barrier((cot_here, x))
+    else:
+        w_first = lax.all_gather(shard_first, both, axis=0, tiled=True)
+        x = to_documents(tokens_here)
+    cot = to_documents(cot_here)
     gain_rows = w_first[:, 3 * width : 3 * width + 2].astype(f32).T
     gain_first, gain_second = gain_rows[:1], gain_rows[1:]
     own = lax.dynamic_slice_in_dim(
         lengths.reshape(count), lax.axis_index("blk") // share * per, per, 0
     )
-    x = to_documents(tokens.reshape(count, rows, width))
-    cot = to_documents(cotangent.reshape(count, rows, width))
     x_rows, cot_rows = my_share(x, share, 0), my_share(cot, share, 0)
     own_rows, w_heads = own, w_first
     if share > 1:
@@ -522,49 +978,53 @@
         w_heads = jnp.concatenate(
             [my_share(w_first[:, i * width : (i + 1) * width], share, 1) for i in range(3)], 1
         )
-
-    table = rel_table * LOG2E
-    near, buckets = bias_tiles(my_share(table, share, 1))
-    far = my_share(jnp.stack([table[15], table[31]], 1), share, 0)
+    table = my_share((rel_table * LOG2E).T, share, 0)
 
     q, k, v = qkv_call(x, gain_first, w_heads, width // share)
-    heads, lse = attend_call(own, far, q, k, v, near)
+    heads, lse = attend_call(own, table, q, k, v)
     mixed, heads_grad, mid, g_second, gn_second = middle_call(
         own_rows, x_rows, among(heads, share, 0, 1), cot_rows, gain_second, w_second
     )
-    dq, dk, dv, near_sum, far_sum = attend_back_call(
-        own, far, q, k, v, among(heads_grad, share, 1, 0), heads, lse, jnp.swapaxes(near, 2, 3)
+    mixed = from_documents(mixed, count)
+    g_second = lax.psum_scatter(g_second, both, scatter_dimension=0, tiled=True).astype(f32)
+    dq, dk, dv, table_sum = attend_back_call(
+        own, table, q, k, v, among(heads_grad, share, 1, 0), heads, lse
     )
     dq, dk, dv = (among(grad, share, 0, 1) for grad in (dq, dk, dv))
     grad_tokens, g_first = last_call(x_rows, dq, dk, dv, mid, gain_first, w_first, gn_second)
-
-    flipped = jnp.swapaxes(buckets, 1, 2)
-    rows_of = []
-    for b in range(rel_table.shape[0]):
-        rows_of.append(jnp.sum(jnp.where(flipped == b, near_sum, 0.0), (1, 2, 3)))
-    table_sum = jnp.stack(rows_of)
-    far_total = jnp.sum(far_sum, (2, 3))
-    table_sum = table_sum.at[15].add(far_total[:, 0]).at[31].add(far_total[:, 1])
-    if share > 1:
-        at = lax.rem(lax.axis_index("blk"), share) * table_sum.shape[1]
-        table_sum = lax.dynamic_update_slice_in_dim(
-            jnp.zeros(rel_table.shape, f32), table_sum, at, 1
+    table_sum = jnp.sum(table_sum, 2)
+    if direct:
+        head_count, bucket_count = table_sum.shape
+        table_sum = jnp.pad(
+            table_sum, ((0, -head_count % 8), (0, SUB - bucket_count))
         )
-    grad_table = lax.psum(table_sum, both)
-
-    g_first = lax.psum_scatter(g_first, both, scatter_dimension=0, tiled=True).astype(f32)
-    g_second = lax.psum_scatter(g_second, both, scatter_dimension=0, tiled=True).astype(f32)
+        grad_query, grad_key, grad_value, gains, grad_tokens, table_sum = tail_call(
+            g_first, grad_tokens.reshape(per, -1, width), table_sum, 2
+        )
+        grad_table = table_sum[:head_count, :bucket_count].T
+    else:
+        grad_tokens = from_documents(grad_tokens, count)
+        g_first = lax.psum_scatter(g_first, both, scatter_dimension=0, tiled=True).astype(f32)
+        grad_query, grad_key, grad_value, gains = jnp.split(
+            g_first, (width, 2 * width, 3 * width), 1
+        )
+        if share > 1:
+            at = lax.rem(lax.axis_index("blk"), share) * table_sum.shape[0]
+            table_sum = lax.dynamic_update_slice_in_dim(
+                jnp.zeros(rel_table.T.shape, f32), table_sum, at, 0
+            )
+        grad_table = lax.psum(table_sum, both).T
     hidden = w_in.shape[1]
     return (
-        from_documents(mixed, count).reshape(tokens.shape),
-        from_documents(grad_tokens, count).reshape(tokens.shape),
-        g_first[:, 3 * width],
-        g_first[:, :width],
-        g_first[:, width : 2 * width],
-        g_first[:, 2 * width : 3 * width],
+        mixed.reshape(tokens.shape),
+        grad_tokens.reshape(tokens.shape),
+        gains[:, 0],
+        grad_query,
+        grad_key,
+        grad_value,
         g_second[:, :width],
         grad_table,
-        g_first[:, 3 * width + 1],
+        gains[:, 1],
         g_second[:, width : width + hidden],
         g_second[:, width + hidden :],
     )

time: 631 us -> 432 us (0.68)
  waiting for transfers between devices: 159 us -> 0.04 us
  Pallas kernels: 243 us -> 372 us
  blocking collectives: 99.1 us -> 0 us
  other arithmetic: 54.7 us -> 5.61 us
  local copies, waits for them, and re-layouts: 45.3 us -> 32.6 us
    reduce_scatter x1, waiting for transfers between devices: 120 us -> 0.01 us  [body(): lax.psum_scatter(g_second, both, scatter_dimension=0, tiled=True)]
    pallas_call x0 -> x2, Pallas kernels: none -> 113 us  [the longest x1 59.9 us: tail_call(): pl.pallas_call(tail_kernel, in_specs=[VMEM_WHOLE, ANY, VMEM_WHOLE], out_s...]
    psum x1 -> x0, blocking collectives: 99.1 us -> none  [body(): grad_table = lax.psum(table_sum, both)]
    select_n x2 -> x0, other arithmetic: 35.2 us -> none  [bias_tiles(): tiles = jnp.where(buckets == b, table[b][:, None, None, None], tiles)]
    ppermute x2 -> x1, waiting for transfers between devices: 26.5 us -> 0.01 us  [to_documents(): lax.ppermute(piece, 'blk', [(i, (i + hop) % ways) for i in range(ways)])]
    all_gather x2 -> x1, waiting for transfers between devices: 11.5 us -> 0.01 us  [body(): w_second = lax.all_gather(shard_second, both, axis=0, tiled=True)]
    pallas_call x1, Pallas kernels: 78.2 us -> 89.2 us  [attend_back_call(): pl.pallas_call(functools.partial(attend_back_kernel, keys=keys, queries=q...]
    reduce_sum x3 -> x1, other arithmetic: 10.1 us -> 1.06 us  [body(): table_sum = jnp.sum(table_sum, 2)]
  transfers between devices with their start and end apart: 8 -> 4, of which waited for: 3 -> 0; matrix products, arithmetic and copies ran while one was open for 15% -> 6% of each run, Pallas kernels for 9% -> 67%
where the time goes in v2:
time: 432 us; the launch traced here: 426 us
  Pallas kernels  372 us (86%)
  local copies, waits for them, and re-layouts  32.6 us (8%)
  between operations  14.2 us (3%)
  other arithmetic  5.61 us (1%)
    pallas_call x1, Pallas kernels, attend_back_call(): pl.pallas_call(functools.partial(attend_back_kernel, keys=keys, queries=q...  89.2 us
    pallas_call x1, Pallas kernels, middle_call(): pl.pallas_call(functools.partial(middle_kernel, seq=total // lengths.shap...  84.2 us
    pallas_call x1, Pallas kernels, tail_call(): pl.pallas_call(tail_kernel, in_specs=[VMEM_WHOLE, ANY, VMEM_WHOLE], out_s...  59.9 us
    pallas_call x1, Pallas kernels, head_call(): pl.pallas_call(head_kernel, in_specs=[VMEM_WHOLE, ANY], out_specs=[ANY, A...  53.5 us
    pallas_call x1, Pallas kernels, attend_call(): pl.pallas_call(functools.partial(attend_kernel, rows=rows), grid=(pairs,...  49 us
    pallas_call x1, Pallas kernels, last_call(): pl.pallas_call(last_kernel, grid=(total // rows,), in_specs=[row] * 5 + [...  24.3 us
    pallas_call x1, Pallas kernels, qkv_call(): pl.pallas_call(qkv_kernel, grid=(total // rows,), in_specs=[row, whole((1...  11.8 us
  transfers between devices with their start and end apart: 4, of which 0 were waited for; matrix products, arithmetic and copies ran while one was open for 6% of the time, Pallas kernels for 67%

profile of v2, /device:TPU:0, one launch (start us, length us, event | category | flops | bytes accessed | tf_op | source)
XLA Modules:
  0.0 426.5 jit_solution(11676860061385484326)
XLA Ops:
  7.2 1.7 pad_maximum_fusion
  9.1 0.7 pad_maximum_fusion.1
  9.9 0.8 fusion.1
  10.7 0.7 pad.13.shard_ref
  11.4 53.5 %head.1 = (bf16[768,2432]{1,0:T(8,128)(2,1)}, bf16[2,1024,768]{2,1,0:T(8,128)(2,1)}) custom-call(bf16[32,2432]{1,0:T(8,128)(2,1)} %pad.13.shard_ref, bf16[4,512,768]{2,1,0:T(8,128)(2,1)} %bitcast.26), custom_call_target="tpu_custom_call" | custom-call | tf_op jit(solution)/shard_map/head/pallas_call | solution.py:623
  64.9 1.9 broadcast_in_dim.4
  66.8 1.1 copy-done.5
  67.9 1.9 constant_dynamic-slice_fusion
  69.7 1.6 collective-permute-start
  71.3 6.0 %copy.32 = bf16[768,2432]{0,1:T(8,128)(2,1)} copy(bf16[768,2432]{1,0:T(8,128)(2,1)} %get-tuple-element.39.w_ref) | data formatting | bytes 7471104 | tf_op jit(solution)/shard_map/head/pallas_call | solution.py:623
  77.3 0.7 convert_bitcast_fusion
  78.6 11.8 %qkv.1 = (bf16[2048,768]{1,0:T(8,128)(2,1)}, bf16[2048,768]{1,0:T(8,128)(2,1)}, bf16[2048,768]{1,0:T(8,128)(2,1)}) custom-call(bf16[2048,768]{1,0:T(8,128)(2,1)} %bitcast.23, f32[1,768]{1,0:T(1,128)} %get-tuple-element.103.gain_ref, bf16[768,2432]{1,0:T(8,128)(2,1)} %get-tuple-element.39.w_ref), custom_call_target="tpu_custom_call" | custom-call | tf_op jit(solution)/shard_map/qkv/pallas_call | solution.py:89
  91.6 49.0 %attend.1 = (bf16[2048,768]{1,0:T(8,128)(2,1)}, f32[2,6,2,1024]{3,2,1,0:T(2,128)}) custom-call(s32[2]{0:T(128)} %fusion.2.len_ref, f32[12,32]{1,0:T(8,128)} %multiply_bitcast_fusion.table_ref, bf16[2048,768]{1,0:T(8,128)(2,1)} %get-tuple-element.40.q_ref, bf16[2048,768]{1,0:T(8,128)(2,1)} %get-tuple-element.41.k_ref, bf16[2048,768]{1,0:T(8,128)(2,1)} %get-tuple-element.42.v_ref), custom_call_target="tpu_custom_call" | custom-call | tf_op jit(solution)/shard_map/attend/pallas_call | solution.py:151
  140.6 1.3 constant_dynamic-update-slice_fusion
  141.9 84.2 %middle.1 = (bf16[2048,768]{1,0:T(8,128)(2,1)}, bf16[2048,768]{1,0:T(8,128)(2,1)}, bf16[2048,768]{1,0:T(8,128)(2,1)}, bf16[768,6912]{1,0:T(8,128)(2,1)}, f32[1,768]{1,0:T(1,128)}) custom-call(s32[2]{0:T(128)} %fusion.2.len_ref, bf16[2048,768]{1,0:T(8,128)(2,1)} %bitcast.24, bf16[2048,768]{1,0:T(8,128)(2,1)} %get-tuple-element.43.heads_ref.o_ref, ...), custom_call_target="tpu_custom_call" | custom-call | tf_op jit(solution)/shard_map/middle/pallas_call | solution.py:236
  226.1 1.9 copy-done.3
  228.0 1.3 constant_dynamic-slice_fusion.1
  229.8 89.2 %attend_back.1 = (bf16[2048,768]{1,0:T(8,128)(2,1)}, bf16[2048,768]{1,0:T(8,128)(2,1)}, bf16[2048,768]{1,0:T(8,128)(2,1)}, f32[12,32,128]{2,1,0:T(8,128)}) custom-call(s32[2]{0:T(128)} %fusion.2.len_ref, f32[12,32]{1,0:T(8,128)} %multiply_bitcast_fusion.table_ref, bf16[2048,768]{1,0:T(8,128)(2,1)} %get-tuple-element.40.q_ref, ...), custom_call_target="tpu_custom_call" | custom-call | tf_op jit(solution)/shard_map/attend_back/pallas_call | solution.py:368
  319.0 1.1 reduce_sum.9
  320.1 0.6 pad.14.table_ref
  320.7 24.3 %last.1 = (bf16[2048,768]{1,0:T(8,128)(2,1)}, bf16[768,2432]{1,0:T(8,128)(2,1)}) custom-call(bf16[2048,768]{1,0:T(8,128)(2,1)} %bitcast.25, bf16[2048,768]{1,0:T(8,128)(2,1)} %get-tuple-element.48.dq_ref, bf16[2048,768]{1,0:T(8,128)(2,1)} %get-tuple-element.49.dk_ref, bf16[2048,768]{1,0:T(8,128)(2,1)} %get-tuple-element.50.dv_ref, ...), custom_call_target="tpu_custom_call" | custom-call | tf_op jit(solution)/shard_map/last/pallas_call | solution.py:446
  345.0 59.9 %tail.1 = (f32[24,768]{1,0:T(8,128)}, f32[24,768]{1,0:T(8,128)}, f32[24,768]{1,0:T(8,128)}, f32[24,128]{1,0:T(8,128)}, bf16[4,512,768]{2,1,0:T(8,128)(2,1)}, /*index=5*/f32[16,128]{1,0:T(8,128)}) custom-call(bf16[768,2432]{1,0:T(8,128)(2,1)} %get-tuple-element.53.g_ref, bf16[2,1024,768]{2,1,0:T(8,128)(2,1)} %bitcast.31, f32[16,128]{1,0:T(8,128)} %pad.14.table_ref), custom_call_target="tpu_custom_call" | custom-call | tf_op jit(solution)/shard_map/tail/pallas_call | solution.py:842
  404.8 1.6 slice_reduce_fusion
  406.4 1.9 reshape.56
  408.3 1.2 bitcast_dynamic-update-slice_fusion.1
  410.1 2.7 bitcast_dynamic-update-slice_fusion
  412.8 1.8 fusion.3
  414.6 1.4 slice.39
  416.1 1.7 copy.42
  417.7 0.6 copy.43
  418.4 0.6 copy.44
  419.0 0.6 copy.45
  (34 shorter events, 3.2 us)
Async XLA Ops:
  7.2 83.2 %copy-start = (s32[4,1]{0,1:T(1,128)S(1)}, s32[4,1]{0,1:T(1,128)}, u32[]{:S(2)}) copy-start(s32[4,1]{0,1:T(1,128)} %param.13) | copy-start | bytes 52
  7.2 134.7 %all-gather.2.cloned.1.call-start = ((), (), s32[]{:S(2)}) async-start(), calls=%async_computation.1 | async-start | bytes 10948608 | tf_op jit(solution)/shard_map/all_gather | solution.py:958
  9.0 403.8 %reduce-scatter.2.cloned.1.call-start = ((), (), s32[]{:S(2)}) async-start(), calls=%async_computation.2 | async-start | bytes 10948608 | tf_op jit(solution)/shard_map/reduce_scatter | solution.py:989
  64.8 3.0 copy-start.5
  69.7 70.8 %collective-permute-start = (bf16[2,512,768]{2,1,0:T(8,128)(2,1)}, bf16[2,512,768]{2,1,0:T(8,128)(2,1)S(1)}, u32[]{:S(2)}, u32[]{:S(2)}) collective-permute-start(bf16[2,512,768]{2,1,0:T(8,128)(2,1)} %get-tuple-element.98), channel_id=1, source_target_pairs={{0,1},{1,0},{2,3},{3,2},{4,5},{5,4},{6,7},{7,6},{8,9},{9,8},{10,11... | collective-permute-start | bytes 4718600 | tf_op jit(solution)/shard_map/ppermute | solution.py:892
  78.6 12.4 %copy-start.9 = (f32[32,12]{0,1:T(8,128)S(1)}, f32[32,12]{0,1:T(8,128)}, u32[]{:S(2)}) copy-start(f32[32,12]{0,1:T(8,128)} %param.19) | copy-start | bytes 4612
  226.1 1.9 copy-start.3
  229.2 180.9 %collective-permute-start.1 = (bf16[2,512,768]{2,1,0:T(8,128)(2,1)}, bf16[2,512,768]{2,1,0:T(8,128)(2,1)}, u32[]{:S(2)}, u32[]{:S(2)}) collective-permute-start(bf16[2,512,768]{2,1,0:T(8,128)(2,1)} %constant_dynamic-slice_fusion.1), channel_id=1, source_target_pairs={{0,1},{1,0},{2,3},{3,2},{4,5},{5,4},{6,7},{7,6},{8,9},{9,8},{10,11... | collective-permute-start | bytes 4718600 | tf_op jit(solution)/shard_map/ppermute | solution.py:912
  404.8 3.5 copy-start.4
  406.4 3.1 copy-start.10
  408.3 7.7 %copy-start.2 = (bf16[4,512,768]{2,1,0:T(8,128)(2,1)S(1)}, bf16[4,512,768]{2,1,0:T(8,128)(2,1)}, u32[]{:S(2)}) copy-start(bf16[4,512,768]{2,1,0:T(8,128)(2,1)} %get-tuple-element.56) | copy-start | bytes 9437188
  416.0 3.6 copy-start.1
  416.0 1.7 copy-start.8
  416.0 2.3 copy-start.7
  416.1 3.0 copy-start.6
Sparse Core Ops, SparseCore 0:
  10.9 118.1 all-gather.1
  226.3 143.9 reduce-scatter.1

commit v3 on v1

--- a/solution.py
+++ b/solution.py
@@ -53,6 +53,27 @@
 SMEM = pl.BlockSpec(memory_space=pltpu.SMEM)
 
 
+def tile_buckets(apart, keys_dim):
+    keys = lax.broadcasted_iota(jnp.int32, (SUB, SUB), keys_dim)
+    queries = lax.broadcasted_iota(jnp.int32, (SUB, SUB), 1 - keys_dim)
+    return bucket_of(keys - queries + SUB * apart)
+
+
+def tile_range(apart):
+    return range(0 if apart <= 0 else 16, 16 if apart < 0 else 32)
+
+
+def fill_tiles(near, table_ref, pair, keys_dim):
+    for apart in (-1, 0, 1):
+        buckets = tile_buckets(apart, keys_dim)
+        masks = [(b, buckets == b) for b in tile_range(apart)]
+        for h in range(2):
+            tile = jnp.zeros((SUB, SUB), f32)
+            for b, mask in masks:
+                tile = jnp.where(mask, table_ref[2 * pair + h, b], tile)
+            near[h, apart + 1] = tile
+
+
 def qkv_kernel(x_ref, gain_ref, w_ref, q_ref, k_ref, v_ref):
     width = q_ref.shape[1]
     normed, _ = norm_rows(x_ref[...].astype(f32))
@@ -77,9 +98,14 @@
 
 
 def attend_kernel(
-    len_ref, far_ref, q_ref, k_ref, v_ref, near_ref, o_ref, lse_ref, *, rows
+    len_ref, table_ref, q_ref, k_ref, v_ref, o_ref, lse_ref, near_ref, *, rows
 ):
     pair, doc = pl.program_id(0), pl.program_id(1)
+
+    @pl.when(doc == 0)
+    def _():
+        fill_tiles(near_ref, table_ref, pair, 1)
+
     seq = q_ref.shape[0]
     subs = seq // SUB
     first = lax.broadcasted_iota(jnp.int32, (1, 128), 1) < 64
@@ -101,11 +127,11 @@
                 low, high = max(at - 1, 0), min(at + 2, subs)
                 parts = []
                 if low > 0:
-                    parts.append(strip[:, : low * SUB] + far_ref[2 * pair + h, 0])
+                    parts.append(strip[:, : low * SUB] + table_ref[2 * pair + h, 15])
                 for b in range(low, high):
                     parts.append(strip[:, b * SUB : (b + 1) * SUB] + near_ref[h, b - at + 1])
                 if high < subs:
-                    parts.append(strip[:, high * SUB :] + far_ref[2 * pair + h, 1])
+                    parts.append(strip[:, high * SUB :] + table_ref[2 * pair + h, 31])
                 strips.append(jnp.concatenate(parts, 1))
             scores = jnp.where(live, jnp.concatenate(strips, 0), NEG)
             top = jnp.max(scores, 1, keepdims=True)
@@ -118,7 +144,7 @@
         lse_ref[0, 0, 1:2, span] = log_total[64:65]
 
 
-def attend_call(lengths, far, q, k, v, near, rows=512):
+def attend_call(lengths, table, q, k, v, rows=512):
     docs, (total, width) = lengths.shape[0], q.shape
     seq, pairs = total // docs, width // 128
     slab = pl.BlockSpec((seq, 128), lambda p, d: (d, p))
@@ -131,13 +157,13 @@
             slab,
             slab,
             slab,
-            pl.BlockSpec((2, 3, SUB, SUB), lambda p, d: (p, 0, 0, 0)),
         ],
         out_specs=[slab, pl.BlockSpec((1, 1, 2, seq), lambda p, d: (d, p, 0, 0))],
         out_shape=[struct((total, width)), struct((docs, pairs, 2, seq), f32)],
+        scratch_shapes=[pltpu.VMEM((2, 3, SUB, SUB), f32)],
         compiler_params=params(),
         name="attend",
-    )(lengths, far, q, k, v, near)
+    )(lengths, table, q, k, v)
 
 
 def middle_kernel(
@@ -221,17 +247,18 @@
 
 def attend_back_kernel(
     len_ref,
-    far_ref,
+    table_ref,
     q_ref,
     k_ref,
     v_ref,
     grad_ref,
     o_ref,
     lse_ref,
-    near_ref,
     dq_ref,
     dk_ref,
     dv_ref,
+    table_sum,
+    near_ref,
     near_sum,
     far_sum,
     acc,
@@ -259,6 +286,7 @@
 
     @pl.when(doc == 0)
     def _():
+        fill_tiles(near_ref, table_ref, pair, 0)
         near_sum[...] = jnp.zeros_like(near_sum)
         far_sum[...] = jnp.zeros_like(far_sum)
 
@@ -277,7 +305,7 @@
                 scores = dot(k, q_one[h][span], NT)
                 prob_grad = dot(v, g_one[h][span], NT)
                 lse = lse_ref[0, 0, h : h + 1, span]
-                lse_side = (lse - far_ref[2 * pair + h, 0], lse - far_ref[2 * pair + h, 1])
+                lse_side = (lse - table_ref[2 * pair + h, 15], lse - table_ref[2 * pair + h, 31])
                 row_delta = delta[h : h + 1, span]
                 prob_rows, grad_rows = [], []
                 for a in range(keys // SUB):
@@ -314,13 +342,29 @@
         dk_ref[held, :] = (dk * (1 / LOG2E)).astype(low_type)
     dq_ref[...] = (acc[...] * 0.125).astype(low_type)
 
-
-def attend_back_call(lengths, far, q, k, v, grad, o, lse, near, keys=256, queries=1024):
+    @pl.when(doc == pl.num_programs(1) - 1)
+    def _():
+        sums = {}
+        for apart in (-1, 0, 1):
+            buckets = tile_buckets(apart, 0)
+            masks = [(b, buckets == b) for b in tile_range(apart)]
+            for h in range(2):
+                tile = near_sum[h, apart + 1]
+                for b, mask in masks:
+                    part = jnp.sum(jnp.where(mask, tile, 0.0), 0, keepdims=True)
+                    sums[h, b] = sums[h, b] + part if (h, b) in sums else part
+        for h in range(2):
+            for side, b in enumerate((15, 31)):
+                sums[h, b] = sums[h, b] + jnp.sum(far_sum[h, side], 0, keepdims=True)
+            for b in range(32):
+                table_sum[h, b : b + 1] = sums[h, b]
+
+
+def attend_back_call(lengths, table, q, k, v, grad, o, lse, keys=256, queries=1024):
     docs, (total, width) = lengths.shape[0], q.shape
     seq, pairs = total // docs, width // 128
     queries = min(queries, seq)
     slab = pl.BlockSpec((seq, 128), lambda p, d: (d, p))
-    tiles = pl.BlockSpec((2, 3, SUB, SUB), lambda p, d: (p, 0, 0, 0))
     return pl.pallas_call(
         functools.partial(attend_back_kernel, keys=keys, queries=queries),
         grid=(pairs, docs),
@@ -333,21 +377,18 @@
             slab,
             slab,
             pl.BlockSpec((1, 1, 2, seq), lambda p, d: (d, p, 0, 0)),
-            tiles,
         ],
-        out_specs=[
-            slab,
-            slab,
-            slab,
-            tiles,
-            pl.BlockSpec((2, 2, 8, SUB), lambda p, d: (p, 0, 0, 0)),
+        out_specs=[slab, slab, slab, pl.BlockSpec((2, 32, SUB), lambda p, d: (p, 0, 0))],
+        out_shape=[struct((total, width))] * 3 + [struct((2 * pairs, 32, SUB), f32)],
+        scratch_shapes=[
+            pltpu.VMEM((2, 3, SUB, SUB), f32),
+            pltpu.VMEM((2, 3, SUB, SUB), f32),
+            pltpu.VMEM((2, 2, 8, SUB), f32),
+            pltpu.VMEM((seq, 128), f32),
         ],
-        out_shape=[struct((total, width))] * 3
-        + [struct((2 * pairs, 3, SUB, SUB), f32), struct((2 * pairs, 2, 8, SUB), f32)],
-        scratch_shapes=[pltpu.VMEM((seq, 128), f32)],
         compiler_params=params(),
         name="attend_back",
-    )(lengths, far, q, k, v, grad, o, lse, near)
+    )(lengths, table, q, k, v, grad, o, lse)
 
 
 def last_kernel(
@@ -358,9 +399,9 @@
     mid_ref,
     gain_ref,
     w_ref,
-    gn_second_ref,
     gt_ref,
     gw_ref,
+    gn_ref,
     acc,
     acc_gain,
 ):
@@ -389,29 +430,631 @@
 
     @pl.when(step == pl.num_programs(0) - 1)
     def _():
-        gw_ref[:, : 3 * width] = acc[...].astype(low_type)
-        pick = lax.broadcasted_iota(jnp.int32, (128, 1), 0)
-        gains = jnp.where(
-            pick == 0,
-            jnp.sum(acc_gain[...], 0, keepdims=True),
-            jnp.where(pick == 1, gn_second_ref[...], 0.0),
-        )
-        gw_ref[:, 3 * width :] = gains.T.astype(low_type)
-
-
-def last_call(x, dq, dk, dv, mid, gain, w_first, gn_second, rows=512):
+        gw_ref[...] = acc[...].astype(low_type)
+        gn_ref[...] = jnp.sum(acc_gain[...], 0, keepdims=True)
+
+
+def last_call(x, dq, dk, dv, mid, gain, w_first, rows=512):
     total, width = x.shape
     row = pl.BlockSpec((rows, width), lambda i: (i, 0))
+    grads = (width, 3 * width)
     return pl.pallas_call(
         last_kernel,
         grid=(total // rows,),
-        in_specs=[row] * 5 + [whole((1, width)), whole(w_first.shape), whole((1, width))],
-        out_specs=[row, whole(w_first.shape)],
-        out_shape=[struct((total, width)), struct(w_first.shape)],
-        scratch_shapes=[pltpu.VMEM((width, 3 * width), f32), pltpu.VMEM((8, width), f32)],
+        in_specs=[row] * 5 + [whole((1, width)), whole(w_first.shape)],
+        out_specs=[row, whole(grads), whole((1, width))],
+        out_shape=[struct((total, width)), struct(grads), struct((1, width), f32)],
+        scratch_shapes=[pltpu.VMEM(grads, f32), pltpu.VMEM((8, width), f32)],
         compiler_params=params(),
         name="last",
-    )(x, dq, dk, dv, mid, gain, w_first, gn_second)
+    )(x, dq, dk, dv, mid, gain, w_first)
+
+
+MESH_ID = pl.DeviceIdType.MESH
+ANY = pl.BlockSpec(memory_space=pl.ANY)
+VMEM_WHOLE = pl.BlockSpec(memory_space=pltpu.VMEM)
+DMA = pltpu.SemaphoreType.DMA
+SPARE = 128
+
+
+class Place:
+    def __init__(self):
+        self.dp, self.y = lax.axis_index("dp"), lax.axis_index("blk")
+        self.depth = lax.axis_size("dp") // 4
+        self.z = self.dp // 4
+        self.x = lax.rem(self.dp // 2, 2)
+        self.core = lax.rem(self.dp, 2)
+        self.hops = sorted(range(1, self.depth), key=lambda hop: min(hop, self.depth - hop))
+
+    def unit(self, z, x, core):
+        return (z * 2 + x) * 2 + core
+
+    def z_after(self, hop):
+        return lax.rem(self.z + hop, self.depth)
+
+    def z_before(self, hop):
+        return lax.rem(self.z + self.depth - hop, self.depth)
+
+    def along_z(self, hop):
+        return (self.unit(self.z_after(hop), self.x, self.core), self.y)
+
+    def over_x(self):
+        return (self.unit(self.z, 1 - self.x, self.core), self.y)
+
+    def over_core(self):
+        return (self.unit(self.z, self.x, 1 - self.core), self.y)
+
+    def over_y(self):
+        return (self.dp, 1 - self.y)
+
+    def greet(self):
+        barrier = pltpu.get_barrier_semaphore()
+        peers = [self.over_x(), self.over_core(), self.over_y()]
+        peers += [self.along_z(hop) for hop in self.hops]
+        for peer in peers:
+            pl.semaphore_signal(barrier, device_id=peer, device_id_type=MESH_ID)
+        pl.semaphore_wait(barrier, len(peers))
+
+
+def remote(source, target, send, recv, device):
+    return pltpu.make_async_remote_copy(
+        src_ref=source,
+        dst_ref=target,
+        send_sem=send,
+        recv_sem=recv,
+        device_id=device,
+        device_id_type=MESH_ID,
+    )
+
+
+class Gather:
+    def __init__(self, place, shard, other, pair, full, sems):
+        self.place, self.shard, self.other, self.pair, self.full = place, shard, other, pair, full
+        self.meet_sem, self.send_sem, self.recv_sem, self.put_sem = sems
+        self.rows = pair.shape[0]
+        self.mine = place.unit(place.z, place.x, place.core)
+
+    @staticmethod
+    def scratch(own_rows, columns, units):
+        return [
+            pltpu.VMEM((own_rows + -own_rows % 16, columns), low_type),
+            pltpu.VMEM((2 * own_rows, columns), low_type),
+            DMA((2,)),
+            DMA((units, 5)),
+            DMA((units,)),
+            DMA,
+        ]
+
+    def at(self, u):
+        return self.full.at[pl.ds(pl.multiple_of(u * self.rows, 16), self.rows)]
+
+    def meet(self):
+        return remote(
+            self.shard, self.other, self.meet_sem.at[0], self.meet_sem.at[1], self.place.over_y()
+        )
+
+    def send(self, u, kind, source=None):
+        device = {"x": self.place.over_x, "core": self.place.over_core}.get(kind)
+        device = device() if device else self.place.along_z(kind)
+        slot = {"x": 3, "core": 4}.get(kind, None)
+        slot = self.place.hops.index(kind) if slot is None else slot
+        source = self.at(u) if source is None else source
+        return remote(source, self.at(u), self.send_sem.at[u, slot], self.recv_sem.at[u], device)
+
+    def put(self):
+        return pltpu.make_async_copy(self.pair, self.at(self.mine), self.put_sem)
+
+    def start(self):
+        self.meet().start()
+
+    def spread(self):
+        place = self.place
+        self.meet().wait()
+        half = self.rows // 2
+        mine = self.shard[:half].astype(f32)
+        theirs = self.other[:half].astype(f32)
+        first = place.y == 0
+        self.pair[...] = jnp.concatenate(
+            [jnp.where(first, mine, theirs), jnp.where(first, theirs, mine)], 0
+        ).astype(low_type)
+        self.put().start()
+        for kind in place.hops + ["x", "core"]:
+            self.send(self.mine, kind, self.pair).start()
+
+    def from_z(self, hop):
+        u = self.place.unit(self.place.z_before(hop), self.place.x, self.place.core)
+        self.send(u, "core").wait_recv()
+        self.send(u, "x").start()
+        self.send(u, "core").start()
+
+    def from_x(self, hop):
+        u = self.place.unit(self.place.z_before(hop), 1 - self.place.x, self.place.core)
+        self.send(u, "core").wait_recv()
+        self.send(u, "core").start()
+
+    def from_core(self):
+        place = self.place
+        for z in range(place.depth):
+            for x in range(2):
+                self.send(place.unit(z, x, 1 - place.core), "core").wait_recv()
+        self.put().wait()
+
+    def stages(self):
+        out = [self.start, self.spread]
+        hops = self.place.hops
+        for at, hop in enumerate(hops):
+            out.append(lambda hop=hop: self.from_z(hop))
+            out.append(lambda hop=([0] + hops)[at]: self.from_x(hop))
+        out.append(lambda: self.from_x(hops[-1]))
+        out.append(self.from_core)
+        return out
+
+    def drain(self):
+        place = self.place
+        for kind in place.hops + ["x", "core"]:
+            self.send(self.mine, kind, self.pair).wait_send()
+        for hop in place.hops:
+            u = place.unit(place.z_before(hop), place.x, place.core)
+            self.send(u, "x").wait_send()
+            self.send(u, "core").wait_send()
+        for hop in [0] + place.hops:
+            u = place.unit(place.z_before(hop), 1 - place.x, place.core)
+            self.send(u, "core").wait_send()
+
+
+class Scatter:
+    def __init__(self, place, full, bufs, sems):
+        self.place, self.full = place, full
+        self.core_buf, self.x_send, self.x_buf, self.z_send, self.z_buf, self.y_send, self.y_buf = bufs
+        self.core_sem, self.x_sem, self.z_sem, self.y_sem = sems
+        self.rows = self.x_send.shape[1]
+        self.order = place.hops + [0]
+
+    @staticmethod
+    def scratch(own_rows, columns, units):
+        depth, unit = units // 4, (2 * own_rows, columns)
+        return [
+            pltpu.VMEM((2, depth) + unit, low_type),
+            pltpu.VMEM((depth,) + unit, low_type),
+            pltpu.VMEM((depth,) + unit, low_type),
+            pltpu.VMEM((depth,) + unit, low_type),
+            pltpu.VMEM((depth,) + unit, low_type),
+            pltpu.VMEM((own_rows, columns), f32),
+            pltpu.VMEM((own_rows, columns), f32),
+            DMA((2, 2, depth)),
+            DMA((2, depth)),
+            DMA((2, depth)),
+            DMA((2,)),
+        ]
+
+    def at(self, z, x, core):
+        u = self.place.unit(z, x, core)
+        return self.full.at[pl.ds(pl.multiple_of(u * self.rows, 16), self.rows)]
+
+    def x_of(self, side):
+        return self.place.x if side == 0 else 1 - self.place.x
+
+    def to_core(self, side, hop):
+        place = self.place
+        return remote(
+            self.at(place.z_after(hop), self.x_of(side), 1 - place.core),
+            self.core_buf.at[side, hop],
+            self.core_sem.at[0, side, hop],
+            self.core_sem.at[1, side, hop],
+            place.over_core(),
+        )
+
+    def to_x(self, hop):
+        return remote(
+            self.x_send.at[hop],
+            self.x_buf.at[hop],
+            self.x_sem.at[0, hop],
+            self.x_sem.at[1, hop],
+            self.place.over_x(),
+        )
+
+    def to_z(self, hop):
+        return remote(
+            self.z_send.at[hop],
+            self.z_buf.at[hop],
+            self.z_sem.at[0, hop],
+            self.z_sem.at[1, hop],
+            self.place.along_z(hop),
+        )
+
+    def to_y(self):
+        return remote(
+            self.y_send, self.y_buf, self.y_sem.at[0], self.y_sem.at[1], self.place.over_y()
+        )
+
+    def start(self):
+        for side in (1, 0):
+            for hop in self.order:
+                self.to_core(side, hop).start()
+
+    def mine(self, side, hop):
+        place = self.place
+        self.to_core(side, hop).wait_recv()
+        own = self.at(place.z_after(hop), self.x_of(side), place.core)
+        return own[...].astype(f32) + self.core_buf[side, hop].astype(f32)
+
+    def stage_x(self, hop):
+        self.x_send[hop] = self.mine(1, hop).astype(low_type)
+        self.to_x(hop).start()
+
+    def stage_z(self, hop):
+        part = self.mine(0, hop)
+        self.to_x(hop).wait_recv()
+        part = part + self.x_buf[hop].astype(f32)
+        self.z_send[hop] = part.astype(low_type)
+        if hop:
+            self.to_z(hop).start()
+
+    def stage_y(self):
+        total = self.z_send[0].astype(f32)
+        for hop in self.place.hops:
+            self.to_z(hop).wait_recv()
+            total = total + self.z_buf[hop].astype(f32)
+        half = self.rows // 2
+        first = self.place.y == 0
+        self.y_send[...] = jnp.where(first, total[half:], total[:half])
+        self.to_y().start()
+        return jnp.where(first, total[:half], total[half:])
+
+    def finish(self, kept):
+        self.to_y().wait()
+        return kept + self.y_buf[...]
+
+    def drain(self):
+        for hop in self.order:
+            for side in (1, 0):
+                self.to_core(side, hop).wait_send()
+            self.to_x(hop).wait_send()
+            if hop:
+                self.to_z(hop).wait_send()
+
+
+class Exchange:
+    def __init__(self, place, send, recv, sem):
+        self.send, self.recv, self.sem = send, recv, sem
+        self.targets = [place.over_core(), place.over_x(), place.over_y()]
+        span = 1
+        while span < place.depth:
+            flip = place.z + span - 2 * span * lax.rem(place.z // span, 2)
+            self.targets.append((place.unit(flip, place.x, place.core), place.y))
+            span *= 2
+
+    @staticmethod
+    def rounds(units):
+        return 3 + (units // 4 - 1).bit_length()
+
+    @staticmethod
+    def scratch(shape, units):
+        rounds = Exchange.rounds(units)
+        return [
+            pltpu.VMEM((rounds,) + shape, f32),
+            pltpu.VMEM((rounds,) + shape, f32),
+            DMA((2, rounds)),
+        ]
+
+    def copy(self, at):
+        return remote(
+            self.send.at[at], self.recv.at[at], self.sem.at[0, at], self.sem.at[1, at], self.targets[at]
+        )
+
+    def start(self, at, value):
+        self.send[at] = value
+        self.copy(at).start()
+
+    def finish(self, at):
+        self.copy(at).wait()
+        return self.send[at] + self.recv[at]
+
+
+def comm_params(collective):
+    return pltpu.CompilerParams(
+        collective_id=collective, has_side_effects=True, vmem_limit_bytes=VMEM
+    )
+
+
+def first_kernel(
+    shard_ref,
+    tokens_ref,
+    q_ref,
+    k_ref,
+    v_ref,
+    x_ref,
+    w_ref,
+    gain_ref,
+    w_all,
+    x_in,
+    stage,
+    other,
+    pair,
+    meet_sem,
+    send_sem,
+    recv_sem,
+    put_sem,
+    swap_sem,
+    load_sem,
+    save_sem,
+    stage_sem,
+    w_sem,
+):
+    place = Place()
+    per, seq, width = x_ref.shape
+    rows = tokens_ref.shape[1]
+    gather = Gather(
+        place, shard_ref, other, pair, w_all, (meet_sem, send_sem, recv_sem, put_sem)
+    )
+    place.greet()
+
+    def swap(doc):
+        return remote(
+            tokens_ref.at[(1 - place.y) * per + doc],
+            x_in.at[per + doc],
+            swap_sem.at[0, doc],
+            swap_sem.at[1, doc],
+            place.over_y(),
+        )
+
+    def load(doc):
+        return pltpu.make_async_copy(
+            tokens_ref.at[place.y * per + doc], x_in.at[doc], load_sem.at[doc]
+        )
+
+    def start_of(block):
+        y = place.y if block < per else 1 - place.y
+        return pl.multiple_of(y * rows, 16)
+
+    def save(block):
+        return pltpu.make_async_copy(
+            x_in.at[block], x_ref.at[block % per, pl.ds(start_of(block), rows)], save_sem.at[block]
+        )
+
+    def store(block, index):
+        target = (q_ref, k_ref, v_ref)[index]
+        begin = pl.multiple_of(block % per * seq + start_of(block), 16)
+        return pltpu.make_async_copy(
+            stage.at[block % 2, index], target.at[pl.ds(begin, rows)], stage_sem.at[block % 2, index]
+        )
+
+    stages = gather.stages()
+    stages[0]()
+    for doc in range(per):
+        load(doc).start()
+        swap(doc).start()
+    for step in stages[1:]:
+        step()
+    keep = pltpu.make_async_copy(w_all, w_ref, w_sem)
+    keep.start()
+    gains = w_all[:, 3 * width :].astype(f32).T
+    gain_ref[...] = gains[: gain_ref.shape[0]]
+    gain = gains[0:1]
+    for block in range(2 * per):
+        if block < per:
+            load(block).wait()
+        else:
+            swap(block - per).wait_recv()
+        save(block).start()
+        normed, _ = norm_rows(x_in[block].astype(f32))
+        low = (normed * gain).astype(low_type)
+        for index in range(3):
+            part = dot(low, w_all[:, index * width : (index + 1) * width])
+            if index == 0:
+                part = part * (0.125 * LOG2E)
+            if block >= 2:
+                store(block - 2, index).wait()
+            stage[block % 2, index] = part.astype(low_type)
+            store(block, index).start()
+    for block in range(2 * per):
+        save(block).wait()
+        if block >= 2 * per - 2:
+            for index in range(3):
+                store(block, index).wait()
+    keep.wait()
+    gather.drain()
+    for doc in range(per):
+        swap(doc).wait_send()
+
+
+def first_call(shard, tokens, ways):
+    units = lax.axis_size("dp")
+    count, rows, width = tokens.shape
+    own_rows, columns = shard.shape
+    per = count // ways
+    padded = jnp.pad(shard, ((0, -own_rows % 16), (0, 0)))
+    total = per * rows * ways
+    return pl.pallas_call(
+        first_kernel,
+        in_specs=[VMEM_WHOLE, ANY],
+        out_specs=[ANY] * 5 + [VMEM_WHOLE],
+        out_shape=[struct((total, width))] * 3
+        + [
+            struct((per, rows * ways, width)),
+            struct((units * ways * own_rows, columns)),
+            struct((8, width), f32),
+        ],
+        scratch_shapes=[
+            pltpu.VMEM((units * ways * own_rows, columns), low_type),
+            pltpu.VMEM((2 * per, rows, width), low_type),
+            pltpu.VMEM((2, 3, rows, width), low_type),
+        ]
+        + Gather.scratch(own_rows, columns, units)
+        + [DMA((2, per)), DMA((per,)), DMA((2 * per,)), DMA((2, 3)), DMA],
+        compiler_params=comm_params(1),
+        name="first",
+    )(padded, tokens)
+
+
+def end_kernel(
+    x_ref,
+    dq_ref,
+    dk_ref,
+    dv_ref,
+    mid_ref,
+    w_ref,
+    gain_ref,
+    gn_second_ref,
+    table_ref,
+    gw_ref,
+    gt_ref,
+    small_ref,
+    rows_in,
+    acc,
+    grads,
+    gt,
+    core_buf,
+    x_send,
+    x_buf,
+    z_send,
+    z_buf,
+    y_send,
+    y_buf,
+    core_sem,
+    x_sem,
+    z_sem,
+    y_sem,
+    small_send,
+    small_recv,
+    small_sem,
+    load_sem,
+    gt_sem,
+):
+    place = Place()
+    count, rows, width = gt_ref.shape
+    per = count // 2
+    seq = 2 * rows
+    scatter = Scatter(
+        place,
+        grads,
+        (core_buf, x_send, x_buf, z_send, z_buf, y_send, y_buf),
+        (core_sem, x_sem, z_sem, y_sem),
+    )
+    exchange = Exchange(place, small_send, small_recv, small_sem)
+    sources = (x_ref, dq_ref, dk_ref, dv_ref, mid_ref)
+
+    def load(block, index):
+        y = 1 - place.y if block < per else place.y
+        begin = pl.multiple_of(block % per * seq + y * rows, 16)
+        return pltpu.make_async_copy(
+            sources[index].at[pl.ds(begin, rows)], rows_in.at[block, index], load_sem.at[block, index]
+        )
+
+    def give(block):
+        target = gt_ref.at[place.y * per + block % per]
+        if block < per:
+            return remote(
+                gt.at[block], target, gt_sem.at[0, block], gt_sem.at[1, block], place.over_y()
+            )
+        return pltpu.make_async_copy(gt.at[block], target, gt_sem.at[0, block])
+
+    for block in range(2 * per):
+        for index in range(5):
+            load(block, index).start()
+    place.greet()
+    gain = gain_ref[0:1]
+    gain_sum = []
+
+    def normed_of(block):
+        return norm_rows(rows_in[block, 0].astype(f32))
+
+    def rows_back(block):
+        normed, inverse = normed_of(block)
+        normed_grad = None
+        for index in range(3):
+            part = dot(
+                rows_in[block, 1 + index], w_ref[:, index * width : (index + 1) * width], NT
+            )
+            normed_grad = part if normed_grad is None else normed_grad + part
+        gain_sum.append(jnp.sum((normed_grad * normed).reshape(rows // 8, 8, width), 0))
+        scaled = normed_grad * gain
+        inner = jnp.mean(scaled * normed, -1, keepdims=True)
+        mid = rows_in[block, 4].astype(f32)
+        gt[block] = (mid + inverse * (scaled - normed * inner)).astype(low_type)
+        give(block).start()
+
+    def weights_back(block, last):
+        normed, _ = normed_of(block)
+        low = (normed * gain).astype(low_type)
+        for index in range(3):
+            span = slice(index * width, (index + 1) * width)
+            part = dot(low, rows_in[block, 1 + index], TN)
+            if block:
+                part = part + acc[:, span]
+            if last:
+                grads[:, span] = part.astype(low_type)
+            else:
+                acc[:, span] = part
+
+    for block in range(2 * per):
+        for index in range(5):
+            load(block, index).wait()
+        if block < per:
+            rows_back(block)
+        weights_back(block, block == 2 * per - 1)
+    scatter.start()
+    rows_back(per)
+    order = scatter.order
+    for hop in order[:2]:
+        scatter.stage_x(hop)
+    for block in range(per + 1, 2 * per):
+        rows_back(block)
+    for hop in order[2:]:
+        scatter.stage_x(hop)
+    gain_row = jnp.sum(sum(gain_sum[1:], gain_sum[0]), 0, keepdims=True)
+    lines = [table_ref[...]]
+    for row in (gain_row, gn_second_ref[...]):
+        lines += [row[:, at : at + 128] for at in range(0, width, 128)]
+    gap = small_ref.shape[0] - sum(line.shape[0] for line in lines)
+    if gap:
+        lines.append(jnp.zeros((gap, 128), f32))
+    exchange.start(0, jnp.concatenate(lines, 0))
+    rounds = len(exchange.targets)
+    at = 0
+    for hop in order:
+        scatter.stage_z(hop)
+        if at < rounds - 1:
+            exchange.start(at + 1, exchange.finish(at))
+            at += 1
+    kept = scatter.stage_y()
+    while at < rounds - 1:
+        exchange.start(at + 1, exchange.finish(at))
+        at += 1
+    small_ref[...] = exchange.finish(at)
+    gw_ref[...] = scatter.finish(kept)
+    scatter.drain()
+    for block in range(2 * per):
+        give(block).wait()
+
+
+def end_call(x, dq, dk, dv, mid, w_first, gains, gn_second, table, docs, ways):
+    units = lax.axis_size("dp")
+    total, width = x.shape
+    own = width // (units * ways)
+    rows = total // (docs * ways)
+    small = (table.shape[0] + -(-2 * (width // 128) // 8) * 8, 128)
+    return pl.pallas_call(
+        end_kernel,
+        in_specs=[ANY] * 5 + [VMEM_WHOLE] * 4,
+        out_specs=[VMEM_WHOLE, ANY, VMEM_WHOLE],
+        out_shape=[
+            struct((own, 3 * width), f32),
+            struct((docs * ways, rows, width)),
+            struct(small, f32),
+        ],
+        scratch_shapes=[
+            pltpu.VMEM((docs * ways, 5, rows, width), low_type),
+            pltpu.VMEM((width, 3 * width), f32),
+            pltpu.VMEM((width, 3 * width), low_type),
+            pltpu.VMEM((docs * ways, rows, width), low_type),
+        ]
+        + Scatter.scratch(own, 3 * width, units)
+        + Exchange.scratch(small, units)
+        + [DMA((docs * ways, 5)), DMA((2, docs * ways))],
+        compiler_params=comm_params(2),
+        name="end",
+    )(x, dq, dk, dv, mid, w_first, gains, gn_second, table)
 
 
 def sharing(count):
@@ -474,15 +1117,6 @@
     return lax.dynamic_slice_in_dim(y, at, size, axis)
 
 
-def bias_tiles(table):
-    offset = jnp.arange(SUB)[None, :] - jnp.arange(SUB)[:, None]
-    buckets = bucket_of(offset[None] + SUB * jnp.arange(-1, 2)[:, None, None])
-    tiles = jnp.zeros((table.shape[1],) + buckets.shape, f32)
-    for b in range(table.shape[0]):
-        tiles = jnp.where(buckets == b, table[b][:, None, None, None], tiles)
-    return tiles, buckets
-
-
 def body(
     tokens,
     lengths,
@@ -501,20 +1135,26 @@
     count = micro * docs
     per, share = sharing(count)
     both = ("dp", "blk")
-    gains = jnp.pad(jnp.stack([norm1_gain, norm2_gain], 1), ((0, 0), (0, 126)))
-    w_first = lax.all_gather(
-        jnp.concatenate([w_query, w_key, w_value, gains], 1), both, axis=0, tiled=True
-    )
-    w_second = lax.all_gather(
-        jnp.concatenate([w_out, w_in, w_down], 1), both, axis=0, tiled=True
-    )
-    gain_rows = w_first[:, 3 * width : 3 * width + 2].astype(f32).T
-    gain_first, gain_second = gain_rows[:1], gain_rows[1:]
+    direct = lax.axis_size("blk") == 2 and per * 2 == count and lax.axis_size("dp") % 4 == 0
+    gains = jnp.pad(jnp.stack([norm1_gain, norm2_gain], 1), ((0, 0), (0, SPARE - 2)))
+    shard_first = jnp.concatenate([w_query, w_key, w_value, gains], 1)
+    shard_second = jnp.concatenate([w_out, w_in, w_down], 1)
+    w_second = lax.all_gather(shard_second, both, axis=0, tiled=True)
+    tokens_here = tokens.reshape(count, rows, width)
+    cot_here = cotangent.reshape(count, rows, width)
+    if direct:
+        q, k, v, x, w_first, gain_rows = first_call(shard_first, tokens_here, 2)
+        x = x.reshape(-1, width)
+        cot_here, x = lax.optimization_barrier((cot_here, x))
+    else:
+        w_first = lax.all_gather(shard_first, both, axis=0, tiled=True)
+        x = to_documents(tokens_here)
+        gain_rows = w_first[:, 3 * width : 3 * width + 2].astype(f32).T
+    cot = to_documents(cot_here)
+    gain_first, gain_second = gain_rows[:1], gain_rows[1:2]
     own = lax.dynamic_slice_in_dim(
         lengths.reshape(count), lax.axis_index("blk") // share * per, per, 0
     )
-    x = to_documents(tokens.reshape(count, rows, width))
-    cot = to_documents(cotangent.reshape(count, rows, width))
     x_rows, cot_rows = my_share(x, share, 0), my_share(cot, share, 0)
     own_rows, w_heads = own, w_first
     if share > 1:
@@ -522,49 +1162,61 @@
         w_heads = jnp.concatenate(
             [my_share(w_first[:, i * width : (i + 1) * width], share, 1) for i in range(3)], 1
         )
-
-    table = rel_table * LOG2E
-    near, buckets = bias_tiles(my_share(table, share, 1))
-    far = my_share(jnp.stack([table[15], table[31]], 1), share, 0)
-
-    q, k, v = qkv_call(x, gain_first, w_heads, width // share)
-    heads, lse = attend_call(own, far, q, k, v, near)
+    table = my_share((rel_table * LOG2E).T, share, 0)
+
+    if not direct:
+        q, k, v = qkv_call(x, gain_first, w_heads, width // share)
+    heads, lse = attend_call(own, table, q, k, v)
     mixed, heads_grad, mid, g_second, gn_second = middle_call(
         own_rows, x_rows, among(heads, share, 0, 1), cot_rows, gain_second, w_second
     )
-    dq, dk, dv, near_sum, far_sum = attend_back_call(
-        own, far, q, k, v, among(heads_grad, share, 1, 0), heads, lse, jnp.swapaxes(near, 2, 3)
+    mixed = from_documents(mixed, count)
+    g_second = lax.psum_scatter(g_second, both, scatter_dimension=0, tiled=True).astype(f32)
+    dq, dk, dv, table_sum = attend_back_call(
+        own, table, q, k, v, among(heads_grad, share, 1, 0), heads, lse
     )
     dq, dk, dv = (among(grad, share, 0, 1) for grad in (dq, dk, dv))
-    grad_tokens, g_first = last_call(x_rows, dq, dk, dv, mid, gain_first, w_first, gn_second)
-
-    flipped = jnp.swapaxes(buckets, 1, 2)
-    rows_of = []
-    for b in range(rel_table.shape[0]):
-        rows_of.append(jnp.sum(jnp.where(flipped == b, near_sum, 0.0), (1, 2, 3)))
-    table_sum = jnp.stack(rows_of)
-    far_total = jnp.sum(far_sum, (2, 3))
-    table_sum = table_sum.at[15].add(far_total[:, 0]).at[31].add(far_total[:, 1])
-    if share > 1:
-        at = lax.rem(lax.axis_index("blk"), share) * table_sum.shape[1]
-        table_sum = lax.dynamic_update_slice_in_dim(
-            jnp.zeros(rel_table.shape, f32), table_sum, at, 1
-        )
-    grad_table = lax.psum(table_sum, both)
-
-    g_first = lax.psum_scatter(g_first, both, scatter_dimension=0, tiled=True).astype(f32)
-    g_second = lax.psum_scatter(g_second, both, scatter_dimension=0, tiled=True).astype(f32)
+    table_sum = jnp.sum(table_sum, 2)
+    head_count, bucket_count = rel_table.shape[1], rel_table.shape[0]
+    index = lax.axis_index("dp") * lax.axis_size("blk") + lax.axis_index("blk")
+    own_gain = norm1_gain.shape[0]
+    if direct:
+        table_sum = jnp.pad(table_sum, ((0, -head_count % 8), (0, SUB - bucket_count)))
+        g_first, grad_tokens, small = end_call(
+            x, dq, dk, dv, mid, w_first, gain_rows, gn_second, table_sum, per, 2
+        )
+        grad_table = small[:head_count, :bucket_count].T
+        gains = small[table_sum.shape[0] :][: 2 * (width // 128)].reshape(2, width)
+        gains = lax.dynamic_slice_in_dim(gains, index * own_gain, own_gain, 1)
+    else:
+        grad_tokens, g_first, gn_first = last_call(
+            x_rows, dq, dk, dv, mid, gain_first, w_first
+        )
+        grad_tokens = from_documents(grad_tokens, count)
+        g_first = lax.psum_scatter(g_first, both, scatter_dimension=0, tiled=True).astype(f32)
+        gains = lax.psum_scatter(
+            jnp.concatenate([gn_first, gn_second], 0), both, scatter_dimension=1, tiled=True
+        )
+        if share > 1:
+            at = lax.rem(lax.axis_index("blk"), share) * table_sum.shape[0]
+            table_sum = lax.dynamic_update_slice_in_dim(
+                jnp.zeros(rel_table.T.shape, f32), table_sum, at, 0
+            )
+        grad_table = lax.psum(table_sum, both).T
+    grad_query, grad_key, grad_value = (
+        g_first[:, i * width : (i + 1) * width] for i in range(3)
+    )
     hidden = w_in.shape[1]
     return (
-        from_documents(mixed, count).reshape(tokens.shape),
-        from_documents(grad_tokens, count).reshape(tokens.shape),
-        g_first[:, 3 * width],
-        g_first[:, :width],
-        g_first[:, width : 2 * width],
-        g_first[:, 2 * width : 3 * width],
+        mixed.reshape(tokens.shape),
+        grad_tokens.reshape(tokens.shape),
+        gains[0],
+        grad_query,
+        grad_key,
+        grad_value,
         g_second[:, :width],
         grad_table,
-        g_first[:, 3 * width + 1],
+        gains[1],
         g_second[:, width : width + hidden],
         g_second[:, width + hidden :],
     )

time: 631 us -> 416 us (0.66)
  waiting for transfers between devices: 159 us -> 0.04 us
  Pallas kernels: 243 us -> 361 us
  blocking collectives: 99.1 us -> 0 us
  other arithmetic: 54.7 us -> 4.91 us
  local copies, waits for them, and re-layouts: 45.3 us -> 26.3 us
    reduce_scatter x1, waiting for transfers between devices: 120 us -> 0.01 us  [body(): lax.psum_scatter(g_second, both, scatter_dimension=0, tiled=True)]
    pallas_call x2, Pallas kernels: 35.9 us -> 138 us  [the longest x1 74.3 us: end_call(): pl.pallas_call(end_kernel, in_specs=[ANY] * 5 + [VMEM_WHOLE] * 4, out_spe...]
    psum x1 -> x0, blocking collectives: 99.1 us -> none  [body(): grad_table = lax.psum(table_sum, both)]
    select_n x2 -> x0, other arithmetic: 35.2 us -> none  [bias_tiles(): tiles = jnp.where(buckets == b, table[b][:, None, None, None], tiles)]
    ppermute x2 -> x1, waiting for transfers between devices: 26.5 us -> 0.01 us  [to_documents(): lax.ppermute(piece, 'blk', [(i, (i + hop) % ways) for i in range(ways)])]
    all_gather x2 -> x1, waiting for transfers between devices: 11.5 us -> 0.01 us  [body(): w_second = lax.all_gather(shard_second, both, axis=0, tiled=True)]
    pallas_call x1, Pallas kernels: 78.2 us -> 89.3 us  [attend_back_call(): pl.pallas_call(functools.partial(attend_back_kernel, keys=keys, queries=q...]
    reduce_sum x3 -> x1, other arithmetic: 10.1 us -> 1.06 us  [body(): table_sum = jnp.sum(table_sum, 2)]
  transfers between devices with their start and end apart: 8 -> 4, of which waited for: 3 -> 0; matrix products, arithmetic and copies ran while one was open for 15% -> 5% of each run, Pallas kernels for 9% -> 68%
where the time goes in v3:
time: 416 us; the launch traced here: 409 us
  Pallas kernels  361 us (87%)
  local copies, waits for them, and re-layouts  26.3 us (6%)
  between operations  14.6 us (4%)
  other arithmetic  4.91 us (1%)
    pallas_call x1, Pallas kernels, attend_back_call(): pl.pallas_call(functools.partial(attend_back_kernel, keys=keys, queries=q...  89.3 us
    pallas_call x1, Pallas kernels, middle_call(): pl.pallas_call(functools.partial(middle_kernel, seq=total // lengths.shap...  84 us
    pallas_call x1, Pallas kernels, end_call(): pl.pallas_call(end_kernel, in_specs=[ANY] * 5 + [VMEM_WHOLE] * 4, out_spe...  74.3 us
    pallas_call x1, Pallas kernels, first_call(): pl.pallas_call(first_kernel, in_specs=[VMEM_WHOLE, ANY], out_specs=[ANY]...  63.7 us
    pallas_call x1, Pallas kernels, attend_call(): pl.pallas_call(functools.partial(attend_kernel, rows=rows), grid=(pairs,...  49.4 us
  transfers between devices with their start and end apart: 4, of which 0 were waited for; matrix products, arithmetic and copies ran while one was open for 5% of the time, Pallas kernels for 68%

profile of v3, /device:TPU:0, one launch (start us, length us, event | category | flops | bytes accessed | tf_op | source)
XLA Modules:
  0.0 408.6 jit_solution(563834853212288845)
XLA Ops:
  7.2 1.8 pad_maximum_fusion
  9.1 0.7 pad_maximum_fusion.1
  9.8 0.1 copy.26
  9.9 0.8 fusion.1
  10.7 0.7 pad.13.shard_ref
  11.4 63.7 %first.1 = (bf16[2048,768]{1,0:T(8,128)(2,1)}, bf16[2048,768]{1,0:T(8,128)(2,1)}, bf16[2048,768]{1,0:T(8,128)(2,1)}, bf16[2,1024,768]{2,1,0:T(8,128)(2,1)}, bf16[768,2432]{1,0:T(8,128)(2,1)}, /*index=5*/f32[8,768]{1,0:T(8,128)}) custom-call(bf16[32,2432]{1,0:T(8,128)(2,1)} %pad.13.shard_ref, bf16[4,512,768]{2,1,0:T(8,128)(2,1)} %bitcast.26), custom_call_target="tpu_custom_call" | custom-call | tf_op jit(solution)/shard_map/first/pallas_call | solution.py:868
  75.1 1.9 broadcast_in_dim.4
  76.9 1.4 copy-done.5
  78.3 1.9 constant_dynamic-slice_fusion.2
  80.2 1.3 slice.35.gain_ref
  81.5 0.6 fusion.2.len_ref
  82.1 0.6 multiply_bitcast_fusion.table_ref
  82.7 49.4 %attend.1 = (bf16[2048,768]{1,0:T(8,128)(2,1)}, f32[2,6,2,1024]{3,2,1,0:T(2,128)}) custom-call(s32[2]{0:T(128)} %fusion.2.len_ref, f32[12,32]{1,0:T(8,128)} %multiply_bitcast_fusion.table_ref, bf16[2048,768]{1,0:T(8,128)(2,1)} %get-tuple-element.35.q_ref, bf16[2048,768]{1,0:T(8,128)(2,1)} %get-tuple-element.36.k_ref, bf16[2048,768]{1,0:T(8,128)(2,1)} %get-tuple-element.37.v_ref), custom_call_target="tpu_custom_call" | custom-call | tf_op jit(solution)/shard_map/attend/pallas_call | solution.py:151
  132.2 1.3 constant_dynamic-update-slice_fusion
  133.4 84.0 %middle.1 = (bf16[2048,768]{1,0:T(8,128)(2,1)}, bf16[2048,768]{1,0:T(8,128)(2,1)}, bf16[2048,768]{1,0:T(8,128)(2,1)}, bf16[768,6912]{1,0:T(8,128)(2,1)}, f32[1,768]{1,0:T(1,128)}) custom-call(s32[2]{0:T(128)} %fusion.2.len_ref, bf16[2048,768]{1,0:T(8,128)(2,1)} %bitcast.24, bf16[2048,768]{1,0:T(8,128)(2,1)} %get-tuple-element.38.heads_ref.o_ref, ...), custom_call_target="tpu_custom_call" | custom-call | tf_op jit(solution)/shard_map/middle/pallas_call | solution.py:236
  217.5 1.9 copy-done.3
  219.3 1.3 constant_dynamic-slice_fusion
  220.6 2.0 collective-permute-start.1
  222.6 89.3 %attend_back.1 = (bf16[2048,768]{1,0:T(8,128)(2,1)}, bf16[2048,768]{1,0:T(8,128)(2,1)}, bf16[2048,768]{1,0:T(8,128)(2,1)}, f32[12,32,128]{2,1,0:T(8,128)}) custom-call(s32[2]{0:T(128)} %fusion.2.len_ref, f32[12,32]{1,0:T(8,128)} %multiply_bitcast_fusion.table_ref, bf16[2048,768]{1,0:T(8,128)(2,1)} %get-tuple-element.35.q_ref, ...), custom_call_target="tpu_custom_call" | custom-call | tf_op jit(solution)/shard_map/attend_back/pallas_call | solution.py:368
  311.9 1.1 reduce_sum.9
  313.0 0.6 pad.14.table_ref
  313.6 74.3 %end.1 = (f32[24,2304]{1,0:T(8,128)}, bf16[4,512,768]{2,1,0:T(8,128)(2,1)}, f32[32,128]{1,0:T(8,128)}) custom-call(bf16[2048,768]{1,0:T(8,128)(2,1)} %bitcast.25, bf16[2048,768]{1,0:T(8,128)(2,1)} %get-tuple-element.44.dq_ref, bf16[2048,768]{1,0:T(8,128)(2,1)} %get-tuple-element.45.dk_ref, bf16[2048,768]{1,0:T(8,128)(2,1)} %get-tuple-element.46.dv_ref, ...), custom_call_target="tpu_custom_call" | custom-call | tf_op jit(solution)/shard_map/end/pallas_call | solution.py:1037
  387.9 0.8 slice.36
  388.8 1.9 reshape.56
  390.7 1.2 bitcast_dynamic-update-slice_fusion.1
  391.9 0.5 slice_bitcast_fusion.1
  392.5 0.6 slice_bitcast_fusion
  393.1 0.7 fusion.4
  393.7 2.7 bitcast_dynamic-update-slice_fusion
  396.4 1.8 fusion.3
  398.2 1.4 slice.46
  399.6 1.7 copy.33
  (27 shorter events, 0.2 us)
Async XLA Ops:
  7.2 74.4 %copy-start = (s32[4,1]{0,1:T(1,128)S(1)}, s32[4,1]{0,1:T(1,128)}, u32[]{:S(2)}) copy-start(s32[4,1]{0,1:T(1,128)} %param.13) | copy-start | bytes 52
  7.2 126.2 %all-gather.2.cloned.1.call-start = ((), (), s32[]{:S(2)}) async-start(), calls=%async_computation.1 | async-start | bytes 10948608 | tf_op jit(solution)/shard_map/all_gather | solution.py:1142
  9.0 387.4 %reduce-scatter.2.cloned.1.call-start = ((), (), s32[]{:S(2)}) async-start(), calls=%async_computation.2 | async-start | bytes 10948608 | tf_op jit(solution)/shard_map/reduce_scatter | solution.py:1174
  75.0 3.3 copy-start.5
  78.3 3.8 copy-start.8
  80.2 51.9 %collective-permute-start = (bf16[2,512,768]{2,1,0:T(8,128)(2,1)}, bf16[2,512,768]{2,1,0:T(8,128)(2,1)S(1)}, u32[]{:S(2)}, u32[]{:S(2)}) collective-permute-start(bf16[2,512,768]{2,1,0:T(8,128)(2,1)} %get-tuple-element.77), channel_id=1, source_target_pairs={{0,1},{1,0},{2,3},{3,2},{4,5},{5,4},{6,7},{7,6},{8,9},{9,8},{10,11... | collective-permute-start | bytes 4718600 | tf_op jit(solution)/shard_map/ppermute | solution.py:1076
  217.5 1.9 copy-start.3
  220.6 173.1 %collective-permute-start.1 = (bf16[2,512,768]{2,1,0:T(8,128)(2,1)}, bf16[2,512,768]{2,1,0:T(8,128)(2,1)}, u32[]{:S(2)}, u32[]{:S(2)}) collective-permute-start(bf16[2,512,768]{2,1,0:T(8,128)(2,1)} %constant_dynamic-slice_fusion), channel_id=1, source_target_pairs={{0,1},{1,0},{2,3},{3,2},{4,5},{5,4},{6,7},{7,6},{8,9},{9,8},{10,11... | collective-permute-start | bytes 4718600 | tf_op jit(solution)/shard_map/ppermute | solution.py:1096
  387.9 2.8 copy-start.4
  388.8 3.6 copy-start.7
  388.8 4.2 %copy-start.6 = (f32[24,2304]{1,0:T(8,128)S(1)}, f32[24,2304]{1,0:T(8,128)}, u32[]{:S(2)}) copy-start(f32[24,2304]{1,0:T(8,128)} %get-tuple-element.53) | copy-start | bytes 663556
  391.9 7.7 %copy-start.2 = (bf16[4,512,768]{2,1,0:T(8,128)(2,1)S(1)}, bf16[4,512,768]{2,1,0:T(8,128)(2,1)}, u32[]{:S(2)}) copy-start(bf16[4,512,768]{2,1,0:T(8,128)(2,1)} %get-tuple-element.51) | copy-start | bytes 9437188
  399.6 1.7 copy-start.1
Sparse Core Ops, SparseCore 0:
  10.9 116.1 all-gather.1
  217.6 160.1 reduce-scatter.1

commit v4 on v3

--- a/solution.py
+++ b/solution.py
@@ -166,83 +166,270 @@
     )(lengths, table, q, k, v)
 
 
+CHUNKS = 4
+AHEAD = 2
+
+
+def second_pieces(w_out, w_in, w_down):
+    chunk = w_in.shape[1] // CHUNKS
+    parts = [w_out]
+    for at in range(0, CHUNKS * chunk, chunk):
+        parts += [w_in[:, at : at + chunk], w_down[:, at : at + chunk]]
+    return jnp.concatenate(parts, 1)
+
+
+def split_hidden(grads):
+    chunk = grads.shape[1] // (2 * CHUNKS)
+    parts = [grads[:, at * chunk : (at + 1) * chunk] for at in range(2 * CHUNKS)]
+    return jnp.concatenate(parts[0::2], 1), jnp.concatenate(parts[1::2], 1)
+
+
 def middle_kernel(
     len_ref,
     x_ref,
     heads_ref,
     cot_ref,
     gain_ref,
-    w_ref,
+    w_out,
+    w_hbm,
     mixed_ref,
     hgrad_ref,
     mid_ref,
-    gw_ref,
+    g_out,
+    g_ref,
     gn_ref,
-    acc,
-    acc_gain,
+    scratch,
     *,
     seq,
-    chunk,
+    before_chunk,
 ):
+    low_all, grad_all, normed_all, inverse_all, mixed_all, back_all = scratch[:6]
+    act_all, up_all, g_buf, acc_gain, g_sem, w_all, w_sem = scratch[6:]
     step = pl.program_id(0)
     rows, width = x_ref.shape
-    hidden = (w_ref.shape[1] - width) // 2
+    total = low_all.shape[0]
+    chunk = w_all.shape[1] // (2 * CHUNKS)
+    fine, block = total // rows, MIDDLE_BLOCK
+    coarse = total // block
+    begin = fine
+    finish = fine + CHUNKS * coarse
+
+    @pl.when(step < begin)
+    def _():
+        span = pl.ds(pl.multiple_of(step * rows, rows), rows)
+        per = seq // rows
+        place = lax.rem(step, per) * rows + lax.broadcasted_iota(jnp.int32, (rows, 1), 0)
+        residual = x_ref[...].astype(f32) + dot(heads_ref[...], w_out[...])
+        normed, inverse = norm_rows(residual)
+        mixed_all[span, :] = residual
+        back_all[span, :] = jnp.zeros_like(residual)
+        normed_all[span, :] = normed.astype(low_type)
+        inverse_all[span, :] = jnp.broadcast_to(inverse, (rows, 128))
+        low_all[span, :] = (normed * gain_ref[...]).astype(low_type)
+        grad_all[span, :] = jnp.where(
+            place < len_ref[jnp.minimum(step // per, len_ref.shape[0] - 1)],
+            cot_ref[...],
+            jnp.zeros((), low_type),
+        )
+
+    def store(at):
+        begins = pl.multiple_of(at * (2 * chunk), 128)
+        slot = lax.rem(at, 2)
+        return pltpu.make_async_copy(
+            g_buf.at[slot], g_ref.at[:, pl.ds(begins, 2 * chunk)], g_sem.at[slot]
+        )
+
+    ready = w_hbm.shape[1] - width
+    take = pltpu.make_async_copy(w_hbm.at[:, width:], w_all.at[:, :ready], w_sem)
 
     @pl.when(step == 0)
     def _():
-        acc[...] = jnp.zeros_like(acc)
-        acc_gain[...] = jnp.zeros_like(acc_gain)
-
-    per = seq // rows
-    place = (step % per) * rows + lax.broadcasted_iota(jnp.int32, (rows, 1), 0)
-    heads, gain = heads_ref[...], gain_ref[...]
-    residual = x_ref[...].astype(f32) + dot(heads, w_ref[:, :width])
-    normed, inverse = norm_rows(residual)
-    low = (normed * gain).astype(low_type)
-    out_grad = jnp.where(place < len_ref[step // per], cot_ref[...], jnp.zeros((), low_type))
-    mixed, normed_grad = residual, jnp.zeros((rows, width), f32)
-    for at in range(0, hidden, chunk):
-        up = slice(width + at, width + at + chunk)
-        down = slice(width + hidden + at, width + hidden + at + chunk)
-        u = dot(low, w_ref[:, up])
+        take.start()
+
+    at = jnp.maximum(step - begin, 0) // coarse
+
+    @pl.when(step == begin)
+    def _():
+        take.wait()
+
+    for index in range(CHUNKS):
+
+        @pl.when(step == begin + index * coarse)
+        def _(index=index):
+            before_chunk(index)
+
+    @pl.when((step >= begin) & (step < finish))
+    def _():
+        span = pl.ds(pl.multiple_of((step - begin - at * coarse) * block, block), block)
+        w_up = w_all[:, pl.ds(pl.multiple_of(at * (2 * chunk), 128), chunk)]
+        w_down = w_all[:, pl.ds(pl.multiple_of(at * (2 * chunk) + chunk, 128), chunk)]
+        u = dot(low_all[span, :], w_up)
         square = u * u
         bend = jnp.tanh(u * (GELU_A + GELU_A * GELU_B * square))
         half = 0.5 + 0.5 * bend
         act = (u * half).astype(low_type)
         slope = half + (0.5 * u) * (1 - bend * bend) * (GELU_A + 3 * GELU_A * GELU_B * square)
-        up_grad = (dot(out_grad, w_ref[:, down]) * slope).astype(low_type)
-        mixed = mixed + dot(act, w_ref[:, down], NT)
-        normed_grad = normed_grad + dot(up_grad, w_ref[:, up], NT)
-        acc[:, down] += dot(out_grad, act, TN)
-        acc[:, up] += dot(low, up_grad, TN)
-    mixed_ref[...] = mixed.astype(low_type)
-    scaled = normed_grad * gain
-    inner = jnp.mean(scaled * normed, -1, keepdims=True)
-    mid = (out_grad.astype(f32) + inverse * (scaled - normed * inner)).astype(low_type)
-    acc_gain[...] += jnp.sum((normed_grad * normed).reshape(rows // 8, 8, width), 0)
-    mid_ref[...] = mid
-    acc[:, :width] += dot(heads, mid, TN)
-    hgrad_ref[...] = dot(mid, w_ref[:, :width], NT).astype(low_type)
+        up_grad = (dot(grad_all[span, :], w_down) * slope).astype(low_type)
+        act_all[span, :] = act
+        up_all[span, :] = up_grad
+        mixed_all[span, :] += dot(act, w_down, NT)
+        back_all[span, :] += dot(up_grad, w_up, NT)
+
+    @pl.when((step >= begin) & (step < finish) & (step - begin == at * coarse + coarse - 1))
+    def _():
+        slot = lax.rem(at, 2)
+
+        @pl.when(at >= 2)
+        def _():
+            store(at - 2).wait()
+
+        g_buf[slot, :, :chunk] = dot(low_all[...], up_all[...], TN).astype(low_type)
+        g_buf[slot, :, chunk:] = dot(grad_all[...], act_all[...], TN).astype(low_type)
+        store(at).start()
+
+    @pl.when(step >= finish)
+    def _():
+        span = pl.ds(pl.multiple_of((step - finish) * rows, rows), rows)
+        mixed_ref[...] = mixed_all[span, :].astype(low_type)
+        normed, back = normed_all[span, :].astype(f32), back_all[span, :]
+        scaled = back * gain_ref[...]
+        inner = jnp.mean(scaled * normed, -1, keepdims=True)
+        inverse = inverse_all[span, :][:, :1]
+        mid = grad_all[span, :].astype(f32) + inverse * (scaled - normed * inner)
+        mid = mid.astype(low_type)
+        part = jnp.sum((back * normed).reshape(rows // 8, 8, width), 0)
+        acc_gain[...] = jnp.where(step == finish, part, acc_gain[...] + part)
+        mid_ref[...] = mid
+        act_all[span, :width] = mid
+        up_all[span, :width] = heads_ref[...]
+        hgrad_ref[...] = dot(mid, w_out[...], NT).astype(low_type)
 
     @pl.when(step == pl.num_programs(0) - 1)
     def _():
-        gw_ref[...] = acc[...].astype(low_type)
+        g_out[...] = dot(up_all[:, :width], act_all[:, :width], TN).astype(low_type)
         gn_ref[...] = jnp.sum(acc_gain[...], 0, keepdims=True)
-
-
-def middle_call(lengths, x, heads, cot, gain, w_second, rows=256, chunk=1024):
+        for at in range(CHUNKS - 2, CHUNKS):
+            store(at).wait()
+
+
+MIDDLE_BLOCK = 512
+
+
+def middle_plain_kernel(*refs, seq):
+    w_ref, w_hbm, rest = refs[5], refs[6], refs[7:]
+    middle_kernel(
+        *refs[:5],
+        w_ref,
+        w_hbm,
+        *rest[:6],
+        rest[6:],
+        seq=seq,
+        before_chunk=lambda at: None,
+    )
+
+
+def middle_send_kernel(*refs, seq):
+    w_ref, w_hbm, pair_ref, rest = refs[5], refs[6], refs[7], refs[8:]
+    w_all, sems = rest[17], rest[19:]
+    place = Place()
+    ahead = w_hbm.shape[1]
+    late = w_all.at[:, ahead - refs[1].shape[1] :]
+    gathers = gather_parts(place, pair_ref.at[:, ahead:], late, sems)
+    stages = [gather.stages() for gather in gathers]
+    planned = {(part, index) for _, part, index in MIDDLE_PLAN}
+    step = pl.program_id(0)
+
+    @pl.when(step == 0)
+    def _():
+        place.greet()
+
+    for when, part, index in MIDDLE_PLAN:
+
+        @pl.when(step == when)
+        def _(part=part, index=index):
+            stages[part][index]()
+
+    def before_chunk(at):
+        part = (at - AHEAD) * PARTS // (CHUNKS - AHEAD)
+        if at >= AHEAD and part * (CHUNKS - AHEAD) == (at - AHEAD) * PARTS:
+            for index in range(len(stages[part])):
+                if (part, index) not in planned:
+                    stages[part][index]()
+
+    middle_kernel(
+        *refs[:5],
+        w_ref,
+        w_hbm,
+        *rest[:6],
+        rest[6:19],
+        seq=seq,
+        before_chunk=before_chunk,
+    )
+
+    @pl.when(step == pl.num_programs(0) - 1)
+    def _():
+        for gather in gathers:
+            gather.drain()
+
+
+MIDDLE_PLAN = (
+    (0, 0, 0), (4, 1, 0), (5, 0, 1), (6, 1, 1), (7, 0, 2), (8, 1, 2),
+    (9, 0, 3), (10, 1, 3), (11, 0, 4), (13, 1, 4),
+)
+
+
+def middle_call(lengths, x, heads, cot, gain, w_second, pair=None, rows=512):
     total, width = x.shape
-    row = pl.BlockSpec((rows, width), lambda i: (i, 0))
+    columns = w_second.shape[1] if pair is None else pair.shape[1]
+    chunk = (columns - width) // (2 * CHUNKS)
+    fine = total // rows
+    steps = 2 * fine + CHUNKS * (total // MIDDLE_BLOCK)
+    early = pl.BlockSpec((rows, width), lambda i: (jnp.minimum(i, fine - 1), 0))
+    late = pl.BlockSpec((rows, width), lambda i: (jnp.maximum(i - (steps - fine), 0), 0))
+    ends = pl.BlockSpec(
+        (rows, width),
+        lambda i: (jnp.where(i < steps - fine, jnp.minimum(i, fine - 1), i - (steps - fine)), 0),
+    )
+    square = (width, 2 * chunk)
+    scratch = [
+        pltpu.VMEM((total, width), low_type),
+        pltpu.VMEM((total, width), low_type),
+        pltpu.VMEM((total, width), low_type),
+        pltpu.VMEM((total, 128), f32),
+        pltpu.VMEM((total, width), f32),
+        pltpu.VMEM((total, width), f32),
+        pltpu.VMEM((total, max(chunk, width)), low_type),
+        pltpu.VMEM((total, max(chunk, width)), low_type),
+        pltpu.VMEM((2,) + square, low_type),
+        pltpu.VMEM((8, width), f32),
+        DMA((2,)),
+        pltpu.VMEM((width, columns - width), low_type),
+        DMA,
+    ]
+    kernel, compiler, operands = middle_plain_kernel, params(), []
+    if pair is not None:
+        kernel, compiler, operands = middle_send_kernel, comm_params(5), [pair]
+        scratch += PARTS * Gather.scratch(lax.axis_size("dp"))
+    square_out = (width, width)
+    first_block = pl.BlockSpec(
+        square_out, lambda i: (0, 0), pipeline_mode=pl.Buffered(1)
+    )
     return pl.pallas_call(
-        functools.partial(middle_kernel, seq=total // lengths.shape[0], chunk=chunk),
-        grid=(total // rows,),
-        in_specs=[SMEM, row, row, row, whole((1, width)), whole(w_second.shape)],
-        out_specs=[row, row, row, whole(w_second.shape), whole((1, width))],
-        out_shape=[struct((total, width))] * 3 + [struct(w_second.shape), struct((1, width), f32)],
-        scratch_shapes=[pltpu.VMEM(w_second.shape, f32), pltpu.VMEM((8, width), f32)],
-        compiler_params=params(),
+        functools.partial(kernel, seq=total // lengths.shape[0]),
+        grid=(steps,),
+        in_specs=[SMEM, early, ends, early, whole((1, width)), first_block, ANY]
+        + [whole(operand.shape) for operand in operands],
+        out_specs=[late, late, late, whole(square_out), ANY, whole((1, width))],
+        out_shape=[struct((total, width))] * 3
+        + [
+            struct(square_out),
+            struct((width, CHUNKS * 2 * chunk)),
+            struct((1, width), f32),
+        ],
+        scratch_shapes=scratch,
+        compiler_params=compiler,
         name="middle",
-    )(lengths, x, heads, cot, gain, w_second)
+    )(lengths, x, heads, cot, gain, w_second, w_second, *operands)
 
 
 def attend_back_kernel(
@@ -507,70 +694,106 @@
     )
 
 
+class Meet:
+    def __init__(self, place, shard, other, sem):
+        self.place, self.shard, self.other, self.sem = place, shard, other, sem
+
+    @staticmethod
+    def scratch(own_rows, columns):
+        block = (own_rows + -own_rows % 16, columns)
+        return [pltpu.VMEM(block, low_type), pltpu.VMEM(block, low_type), DMA((2,))]
+
+    def copy(self):
+        return remote(self.shard, self.other, self.sem.at[0], self.sem.at[1], self.place.over_y())
+
+    def start(self, parts):
+        at = 0
+        for ref in parts:
+            rows, columns = ref.shape
+            self.shard[:rows, at : at + columns] = ref[...]
+            at += columns
+        self.copy().start()
+
+    def finish(self, pair):
+        self.copy().wait()
+        half = pair.shape[0] // 2
+        mine = self.shard[:half].astype(f32)
+        theirs = self.other[:half].astype(f32)
+        first = self.place.y == 0
+        pair[...] = jnp.concatenate(
+            [jnp.where(first, mine, theirs), jnp.where(first, theirs, mine)], 0
+        ).astype(low_type)
+
+
 class Gather:
-    def __init__(self, place, shard, other, pair, full, sems):
-        self.place, self.shard, self.other, self.pair, self.full = place, shard, other, pair, full
-        self.meet_sem, self.send_sem, self.recv_sem, self.put_sem = sems
+    def __init__(self, place, pair, full, sems):
+        self.place, self.pair, self.full = place, pair, full
+        self.send_sem, self.recv_sem, self.put_sem = sems
         self.rows = pair.shape[0]
         self.mine = place.unit(place.z, place.x, place.core)
+        self.has_left, self.has_right = place.z > 0, place.z < place.depth - 1
 
     @staticmethod
-    def scratch(own_rows, columns, units):
-        return [
-            pltpu.VMEM((own_rows + -own_rows % 16, columns), low_type),
-            pltpu.VMEM((2 * own_rows, columns), low_type),
-            DMA((2,)),
-            DMA((units, 5)),
-            DMA((units,)),
-            DMA,
-        ]
+    def scratch(units):
+        return [DMA((units, 4)), DMA((units,)), DMA]
 
     def at(self, u):
         return self.full.at[pl.ds(pl.multiple_of(u * self.rows, 16), self.rows)]
 
-    def meet(self):
-        return remote(
-            self.shard, self.other, self.meet_sem.at[0], self.meet_sem.at[1], self.place.over_y()
-        )
-
     def send(self, u, kind, source=None):
-        device = {"x": self.place.over_x, "core": self.place.over_core}.get(kind)
-        device = device() if device else self.place.along_z(kind)
-        slot = {"x": 3, "core": 4}.get(kind, None)
-        slot = self.place.hops.index(kind) if slot is None else slot
+        place = self.place
+        device = {
+            "left": (place.dp - 4, place.y),
+            "right": (place.dp + 4, place.y),
+            "x": place.over_x(),
+            "core": place.over_core(),
+        }[kind]
+        slot = ("left", "right", "x", "core").index(kind)
         source = self.at(u) if source is None else source
         return remote(source, self.at(u), self.send_sem.at[u, slot], self.recv_sem.at[u], device)
 
     def put(self):
         return pltpu.make_async_copy(self.pair, self.at(self.mine), self.put_sem)
 
-    def start(self):
-        self.meet().start()
-
     def spread(self):
+        for kind, there in (("right", self.has_right), ("left", self.has_left)):
+
+            @pl.when(there)
+            def _(kind=kind):
+                self.send(self.mine, kind, self.pair).start()
+
+        self.send(self.mine, "x", self.pair).start()
+        self.send(self.mine, "core", self.pair).start()
+        self.put().start()
+
+    def from_z(self, hop):
         place = self.place
-        self.meet().wait()
-        half = self.rows // 2
-        mine = self.shard[:half].astype(f32)
-        theirs = self.other[:half].astype(f32)
-        first = place.y == 0
-        self.pair[...] = jnp.concatenate(
-            [jnp.where(first, mine, theirs), jnp.where(first, theirs, mine)], 0
-        ).astype(low_type)
-        self.put().start()
-        for kind in place.hops + ["x", "core"]:
-            self.send(self.mine, kind, self.pair).start()
-
-    def from_z(self, hop):
-        u = self.place.unit(self.place.z_before(hop), self.place.x, self.place.core)
-        self.send(u, "core").wait_recv()
-        self.send(u, "x").start()
-        self.send(u, "core").start()
+        for kind, z, onward in (
+            ("right", place.z - hop, self.has_right),
+            ("left", place.z + hop, self.has_left),
+        ):
+
+            @pl.when((z >= 0) & (z < place.depth))
+            def _(kind=kind, z=z, onward=onward):
+                u = place.unit(z, place.x, place.core)
+                self.send(u, "core").wait_recv()
+
+                @pl.when(onward)
+                def _():
+                    self.send(u, kind).start()
+
+                self.send(u, "x").start()
+                self.send(u, "core").start()
 
     def from_x(self, hop):
-        u = self.place.unit(self.place.z_before(hop), 1 - self.place.x, self.place.core)
-        self.send(u, "core").wait_recv()
-        self.send(u, "core").start()
+        place = self.place
+        for z in (place.z - hop, place.z + hop)[: 1 + min(hop, 1)]:
+
+            @pl.when((z >= 0) & (z < place.depth))
+            def _(z=z):
+                u = place.unit(z, 1 - place.x, place.core)
+                self.send(u, "core").wait_recv()
+                self.send(u, "core").start()
 
     def from_core(self):
         place = self.place
@@ -580,56 +803,76 @@
         self.put().wait()
 
     def stages(self):
-        out = [self.start, self.spread]
-        hops = self.place.hops
-        for at, hop in enumerate(hops):
-            out.append(lambda hop=hop: self.from_z(hop))
-            out.append(lambda hop=([0] + hops)[at]: self.from_x(hop))
-        out.append(lambda: self.from_x(hops[-1]))
-        out.append(self.from_core)
-        return out
+        def at_hop(hop):
+            if hop < self.place.depth:
+                self.from_z(hop)
+            self.from_x(hop - 1)
+
+        out = [self.spread]
+        out += [lambda hop=hop: at_hop(hop) for hop in range(1, self.place.depth + 1)]
+        return out + [self.from_core]
 
     def drain(self):
         place = self.place
-        for kind in place.hops + ["x", "core"]:
-            self.send(self.mine, kind, self.pair).wait_send()
-        for hop in place.hops:
-            u = place.unit(place.z_before(hop), place.x, place.core)
+        for z in range(place.depth):
+            u = place.unit(z, place.x, place.core)
             self.send(u, "x").wait_send()
             self.send(u, "core").wait_send()
-        for hop in [0] + place.hops:
-            u = place.unit(place.z_before(hop), 1 - place.x, place.core)
-            self.send(u, "core").wait_send()
+
+            @pl.when((place.z >= z) & self.has_right)
+            def _(u=u):
+                self.send(u, "right").wait_send()
+
+            @pl.when((place.z <= z) & self.has_left)
+            def _(u=u):
+                self.send(u, "left").wait_send()
+
+            self.send(place.unit(z, 1 - place.x, place.core), "core").wait_send()
+
+
+PARTS = 2
+
+
+def gather_parts(place, pair, full, sems):
+    size = full.shape[1] // PARTS
+    out = []
+    for at in range(PARTS):
+        span = slice(at * size, (at + 1) * size)
+        out.append(Gather(place, pair.at[:, span], full.at[:, span], sems[3 * at : 3 * at + 3]))
+    return out
 
 
 class Scatter:
-    def __init__(self, place, full, bufs, sems):
+    def __init__(self, place, full, scratch, source=None):
         self.place, self.full = place, full
-        self.core_buf, self.x_send, self.x_buf, self.z_send, self.z_buf, self.y_send, self.y_buf = bufs
-        self.core_sem, self.x_sem, self.z_sem, self.y_sem = sems
+        self.source = full if source is None else source
+        self.core_buf, self.x_send, self.x_buf, self.z_send, self.z_buf = scratch[:5]
+        self.y_send, self.y_buf = scratch[5:7]
+        self.core_sem, self.x_sem, self.z_sem, self.y_sem = scratch[7:]
         self.rows = self.x_send.shape[1]
         self.order = place.hops + [0]
 
     @staticmethod
-    def scratch(own_rows, columns, units):
+    def scratch(own_rows, columns, units, lead=()):
         depth, unit = units // 4, (2 * own_rows, columns)
+        edge = lead + (own_rows + -own_rows % 16, columns)
         return [
-            pltpu.VMEM((2, depth) + unit, low_type),
-            pltpu.VMEM((depth,) + unit, low_type),
-            pltpu.VMEM((depth,) + unit, low_type),
-            pltpu.VMEM((depth,) + unit, low_type),
-            pltpu.VMEM((depth,) + unit, low_type),
-            pltpu.VMEM((own_rows, columns), f32),
-            pltpu.VMEM((own_rows, columns), f32),
-            DMA((2, 2, depth)),
-            DMA((2, depth)),
-            DMA((2, depth)),
-            DMA((2,)),
+            pltpu.VMEM(lead + (2, depth) + unit, low_type),
+            pltpu.VMEM(lead + (depth,) + unit, low_type),
+            pltpu.VMEM(lead + (depth,) + unit, low_type),
+            pltpu.VMEM(lead + (depth,) + unit, low_type),
+            pltpu.VMEM(lead + (depth,) + unit, low_type),
+            pltpu.VMEM(edge, low_type),
+            pltpu.VMEM(edge, low_type),
+            DMA(lead + (2, 2, depth)),
+            DMA(lead + (2, depth)),
+            DMA(lead + (2, depth)),
+            DMA(lead + (2,)),
         ]
 
-    def at(self, z, x, core):
+    def at(self, ref, z, x, core):
         u = self.place.unit(z, x, core)
-        return self.full.at[pl.ds(pl.multiple_of(u * self.rows, 16), self.rows)]
+        return ref.at[pl.ds(pl.multiple_of(u * self.rows, 16), self.rows)]
 
     def x_of(self, side):
         return self.place.x if side == 0 else 1 - self.place.x
@@ -637,7 +880,7 @@
     def to_core(self, side, hop):
         place = self.place
         return remote(
-            self.at(place.z_after(hop), self.x_of(side), 1 - place.core),
+            self.at(self.source, place.z_after(hop), self.x_of(side), 1 - place.core),
             self.core_buf.at[side, hop],
             self.core_sem.at[0, side, hop],
             self.core_sem.at[1, side, hop],
@@ -675,7 +918,7 @@
     def mine(self, side, hop):
         place = self.place
         self.to_core(side, hop).wait_recv()
-        own = self.at(place.z_after(hop), self.x_of(side), place.core)
+        own = self.at(self.full, place.z_after(hop), self.x_of(side), place.core)
         return own[...].astype(f32) + self.core_buf[side, hop].astype(f32)
 
     def stage_x(self, hop):
@@ -697,13 +940,13 @@
             total = total + self.z_buf[hop].astype(f32)
         half = self.rows // 2
         first = self.place.y == 0
-        self.y_send[...] = jnp.where(first, total[half:], total[:half])
+        self.y_send[:half] = jnp.where(first, total[half:], total[:half]).astype(low_type)
         self.to_y().start()
         return jnp.where(first, total[:half], total[half:])
 
     def finish(self, kept):
         self.to_y().wait()
-        return kept + self.y_buf[...]
+        return kept + self.y_buf[: kept.shape[0]].astype(f32)
 
     def drain(self):
         for hop in self.order:
@@ -758,7 +1001,11 @@
 
 
 def first_kernel(
-    shard_ref,
+    wq_ref,
+    wk_ref,
+    wv_ref,
+    gains_ref,
+    second_refs,
     tokens_ref,
     q_ref,
     k_ref,
@@ -766,27 +1013,19 @@
     x_ref,
     w_ref,
     gain_ref,
+    second_pair,
     w_all,
     x_in,
     stage,
-    other,
     pair,
-    meet_sem,
-    send_sem,
-    recv_sem,
-    put_sem,
-    swap_sem,
-    load_sem,
-    save_sem,
-    stage_sem,
-    w_sem,
+    *rest,
 ):
+    swap_sem, load_sem, save_sem, stage_sem, w_sem = rest[9:]
     place = Place()
     per, seq, width = x_ref.shape
     rows = tokens_ref.shape[1]
-    gather = Gather(
-        place, shard_ref, other, pair, w_all, (meet_sem, send_sem, recv_sem, put_sem)
-    )
+    gather = Gather(place, pair, w_all, rest[6:9])
+    meet, second_meet = Meet(place, *rest[:3]), Meet(place, *rest[3:6])
     place.greet()
 
     def swap(doc):
@@ -804,26 +1043,38 @@
         )
 
     def start_of(block):
-        y = place.y if block < per else 1 - place.y
+        y = jnp.where(block < per, place.y, 1 - place.y)
         return pl.multiple_of(y * rows, 16)
 
     def save(block):
         return pltpu.make_async_copy(
-            x_in.at[block], x_ref.at[block % per, pl.ds(start_of(block), rows)], save_sem.at[block]
+            x_in.at[block],
+            x_ref.at[lax.rem(block, per), pl.ds(start_of(block), rows)],
+            save_sem.at[block],
         )
 
     def store(block, index):
         target = (q_ref, k_ref, v_ref)[index]
-        begin = pl.multiple_of(block % per * seq + start_of(block), 16)
+        begin = pl.multiple_of(lax.rem(block, per) * seq + start_of(block), 16)
+        slot = lax.rem(block, 2)
         return pltpu.make_async_copy(
-            stage.at[block % 2, index], target.at[pl.ds(begin, rows)], stage_sem.at[block % 2, index]
-        )
-
-    stages = gather.stages()
-    stages[0]()
+            stage.at[slot, index], target.at[pl.ds(begin, rows)], stage_sem.at[slot, index]
+        )
+
+    meet.start((wq_ref, wk_ref, wv_ref, gains_ref))
     for doc in range(per):
         load(doc).start()
         swap(doc).start()
+    meet.finish(pair)
+    stages = gather.stages()
+    stages[0]()
+    out_ref, in_ref, down_ref = second_refs
+    chunk = in_ref.shape[1] // CHUNKS
+    parts = [out_ref]
+    for at in range(CHUNKS):
+        span = slice(at * chunk, (at + 1) * chunk)
+        parts += [in_ref.at[:, span], down_ref.at[:, span]]
+    second_meet.start(parts)
     for step in stages[1:]:
         step()
     keep = pltpu.make_async_copy(w_all, w_ref, w_sem)
@@ -831,22 +1082,35 @@
     gains = w_all[:, 3 * width :].astype(f32).T
     gain_ref[...] = gains[: gain_ref.shape[0]]
     gain = gains[0:1]
-    for block in range(2 * per):
-        if block < per:
+
+    def project(block, _):
+        @pl.when(block < per)
+        def _():
             load(block).wait()
-        else:
+
+        @pl.when(block >= per)
+        def _():
             swap(block - per).wait_recv()
+
         save(block).start()
         normed, _ = norm_rows(x_in[block].astype(f32))
         low = (normed * gain).astype(low_type)
+        slot = lax.rem(block, 2)
         for index in range(3):
             part = dot(low, w_all[:, index * width : (index + 1) * width])
             if index == 0:
                 part = part * (0.125 * LOG2E)
-            if block >= 2:
+
+            @pl.when(block >= 2)
+            def _(index=index):
                 store(block - 2, index).wait()
-            stage[block % 2, index] = part.astype(low_type)
+
+            stage[slot, index] = part.astype(low_type)
             store(block, index).start()
+        return 0
+
+    lax.fori_loop(0, 2 * per, project, 0)
+    second_meet.finish(second_pair)
     for block in range(2 * per):
         save(block).wait()
         if block >= 2 * per - 2:
@@ -858,33 +1122,358 @@
         swap(doc).wait_send()
 
 
-def first_call(shard, tokens, ways):
+def first_call(firsts, gains, seconds, tokens, ways):
     units = lax.axis_size("dp")
     count, rows, width = tokens.shape
-    own_rows, columns = shard.shape
+    own_rows = gains.shape[0]
+    columns = sum(w.shape[1] for w in firsts) + gains.shape[1]
+    second_columns = sum(w.shape[1] for w in seconds)
     per = count // ways
-    padded = jnp.pad(shard, ((0, -own_rows % 16), (0, 0)))
     total = per * rows * ways
+
+    def kernel(*refs):
+        begin = len(firsts) + 1
+        end = begin + len(seconds)
+        first_kernel(*refs[:begin], refs[begin:end], *refs[end:])
+
     return pl.pallas_call(
-        first_kernel,
-        in_specs=[VMEM_WHOLE, ANY],
-        out_specs=[ANY] * 5 + [VMEM_WHOLE],
+        kernel,
+        in_specs=[VMEM_WHOLE] * (len(firsts) + 1 + len(seconds)) + [ANY],
+        out_specs=[ANY] * 5 + [VMEM_WHOLE] * 2,
         out_shape=[struct((total, width))] * 3
         + [
             struct((per, rows * ways, width)),
             struct((units * ways * own_rows, columns)),
             struct((8, width), f32),
+            struct((ways * own_rows, second_columns)),
         ],
         scratch_shapes=[
             pltpu.VMEM((units * ways * own_rows, columns), low_type),
             pltpu.VMEM((2 * per, rows, width), low_type),
             pltpu.VMEM((2, 3, rows, width), low_type),
+            pltpu.VMEM((ways * own_rows, columns), low_type),
         ]
-        + Gather.scratch(own_rows, columns, units)
+        + Meet.scratch(own_rows, columns)
+        + Meet.scratch(own_rows, second_columns)
+        + Gather.scratch(units)
         + [DMA((2, per)), DMA((per,)), DMA((2 * per,)), DMA((2, 3)), DMA],
         compiler_params=comm_params(1),
         name="first",
-    )(padded, tokens)
+    )(*firsts, gains, *seconds, tokens)
+
+
+def attend_send_kernel(
+    len_ref,
+    table_ref,
+    q_ref,
+    k_ref,
+    v_ref,
+    pair_ref,
+    cot_ref,
+    o_ref,
+    lse_ref,
+    w_ref,
+    cot_doc,
+    near_ref,
+    cot_in,
+    *rest,
+    rows,
+):
+    place = Place()
+    gathers = gather_parts(place, pair_ref.at[:, : w_ref.shape[1]], w_ref, rest[:-2])
+    swap_sem, load_sem = rest[-2:]
+    per, part = cot_doc.shape[0], cot_ref.shape[1]
+    step = pl.program_id(0) * pl.num_programs(1) + pl.program_id(1)
+    last = pl.num_programs(0) * pl.num_programs(1) - 1
+    stages = [gather.stages() for gather in gathers]
+
+    def swap(doc):
+        return remote(
+            cot_ref.at[(1 - place.y) * per + doc],
+            cot_doc.at[doc, pl.ds(pl.multiple_of(place.y * part, 16), part)],
+            swap_sem.at[0, doc],
+            swap_sem.at[1, doc],
+            place.over_y(),
+        )
+
+    def load(doc):
+        return pltpu.make_async_copy(
+            cot_ref.at[place.y * per + doc], cot_in.at[doc], load_sem.at[0, doc]
+        )
+
+    def save(doc):
+        return pltpu.make_async_copy(
+            cot_in.at[doc],
+            cot_doc.at[doc, pl.ds(pl.multiple_of(place.y * part, 16), part)],
+            load_sem.at[1, doc],
+        )
+
+    @pl.when(step == 0)
+    def _():
+        place.greet()
+        for doc in range(per):
+            load(doc).start()
+
+    for at, piece, index in SEND_PLAN:
+
+        @pl.when(step == at)
+        def _(piece=piece, index=index):
+            stages[piece][index]()
+
+    @pl.when(step == 1)
+    def _():
+        for doc in range(per):
+            swap(doc).start()
+            load(doc).wait()
+            save(doc).start()
+
+    attend_kernel(len_ref, table_ref, q_ref, k_ref, v_ref, o_ref, lse_ref, near_ref, rows=rows)
+
+    @pl.when(step == last)
+    def _():
+        done = {(piece, index) for _, piece, index in SEND_PLAN}
+        for index in range(len(stages[0])):
+            for piece in range(PARTS):
+                if (piece, index) not in done:
+                    stages[piece][index]()
+        for gather in gathers:
+            gather.drain()
+        for doc in range(per):
+            save(doc).wait()
+            swap(doc).wait()
+
+
+SEND_PLAN = (
+    (0, 0, 0), (1, 1, 0), (3, 0, 1), (4, 1, 1), (5, 0, 2), (6, 1, 2),
+    (7, 0, 3), (8, 1, 3), (9, 0, 4), (10, 1, 4), (11, 0, 5),
+)
+
+
+def attend_send_call(lengths, table, q, k, v, pair, columns, cot, rows=512):
+    units = lax.axis_size("dp")
+    docs, (total, width) = lengths.shape[0], q.shape
+    seq, pairs = total // docs, width // 128
+    slab = pl.BlockSpec((seq, 128), lambda p, d: (d, p))
+    return pl.pallas_call(
+        functools.partial(attend_send_kernel, rows=rows),
+        grid=(pairs, docs),
+        in_specs=[SMEM, SMEM, slab, slab, slab, whole(pair.shape), ANY],
+        out_specs=[slab, pl.BlockSpec((1, 1, 2, seq), lambda p, d: (d, p, 0, 0)), ANY, ANY],
+        out_shape=[
+            struct((total, width)),
+            struct((docs, pairs, 2, seq), f32),
+            struct((units * pair.shape[0], columns)),
+            struct((docs, seq, width)),
+        ],
+        scratch_shapes=[
+            pltpu.VMEM((2, 3, SUB, SUB), f32),
+            pltpu.VMEM((docs, cot.shape[1], width), low_type),
+        ]
+        + PARTS * Gather.scratch(units)
+        + [DMA((2, docs)), DMA((2, docs))],
+        compiler_params=comm_params(3),
+        name="attend",
+    )(lengths, table, q, k, v, pair, cot)
+
+
+def back_send_kernel(
+    len_ref,
+    table_ref,
+    q_ref,
+    k_ref,
+    v_ref,
+    grad_ref,
+    o_ref,
+    lse_ref,
+    g_ref,
+    mixed_ref,
+    dq_ref,
+    dk_ref,
+    dv_ref,
+    table_sum,
+    gw_ref,
+    mixed_out,
+    near_ref,
+    near_sum,
+    far_sum,
+    acc,
+    grads,
+    mixed_in,
+    kept,
+    *rest,
+    keys,
+    queries,
+    steps,
+):
+    place = Place()
+    size = grads.shape[1] // CHUNKS
+    grads_sem, swap_sem, load_sem = rest[11:]
+
+    def scatter(at):
+        span = pl.ds(pl.multiple_of(at * size, 128), size)
+        return Scatter(
+            place, grads.at[:, span], [ref.at[at] for ref in rest[:11]], g_ref.at[:, span]
+        )
+
+    per, part = mixed_ref.shape[0], mixed_out.shape[1]
+    step = pl.program_id(0) * pl.num_programs(1) + pl.program_id(1)
+    last = pl.num_programs(0) * pl.num_programs(1) - 1
+
+    def swap(doc):
+        return remote(
+            mixed_ref.at[doc, pl.ds(pl.multiple_of((1 - place.y) * part, 16), part)],
+            mixed_out.at[place.y * per + doc],
+            swap_sem.at[0, doc],
+            swap_sem.at[1, doc],
+            place.over_y(),
+        )
+
+    def load(doc):
+        return pltpu.make_async_copy(
+            mixed_ref.at[doc, pl.ds(pl.multiple_of(place.y * part, 16), part)],
+            mixed_in.at[doc],
+            load_sem.at[0, doc],
+        )
+
+    def save(doc):
+        return pltpu.make_async_copy(
+            mixed_in.at[doc], mixed_out.at[place.y * per + doc], load_sem.at[1, doc]
+        )
+
+    take = pltpu.make_async_copy(g_ref, grads, grads_sem)
+
+    @pl.when(step == 0)
+    def _():
+        place.greet()
+        for at in range(CHUNKS):
+            scatter(at).start()
+        take.start()
+        for doc in range(per):
+            load(doc).start()
+            swap(doc).start()
+
+    @pl.when(step == 1)
+    def _():
+        take.wait()
+
+    def every_other(first, work):
+        at = (step - first) // 2
+
+        @pl.when((step >= first) & (at < CHUNKS) & (step == first + 2 * at))
+        def _():
+            work(at)
+
+    def x_stages(at):
+        for hop in place.hops + [0]:
+            scatter(at).stage_x(hop)
+
+    def z_stages(at):
+        for hop in place.hops + [0]:
+            scatter(at).stage_z(hop)
+
+    def y_stage(at):
+        kept[at] = scatter(at).stage_y()
+
+    def finish(at):
+        gw_ref[:, pl.ds(pl.multiple_of(at * size, 128), size)] = scatter(at).finish(kept[at])
+
+    every_other(1, x_stages)
+    every_other(3, z_stages)
+    every_other(5, y_stage)
+    every_other(6, finish)
+
+    @pl.when(step == 3)
+    def _():
+        for doc in range(per):
+            load(doc).wait()
+            save(doc).start()
+
+    attend_back_kernel(
+        len_ref,
+        table_ref,
+        q_ref,
+        k_ref,
+        v_ref,
+        grad_ref,
+        o_ref,
+        lse_ref,
+        dq_ref,
+        dk_ref,
+        dv_ref,
+        table_sum,
+        near_ref,
+        near_sum,
+        far_sum,
+        acc,
+        keys=keys,
+        queries=queries,
+    )
+
+    @pl.when(step == last)
+    def _():
+        for at in range(CHUNKS):
+            for first, work in ((1, x_stages), (3, z_stages), (5, y_stage), (6, finish)):
+                if first + 2 * at >= steps:
+                    work(at)
+        for at in range(CHUNKS):
+            scatter(at).drain()
+        for doc in range(per):
+            save(doc).wait()
+            swap(doc).wait()
+
+
+def back_send_call(lengths, table, q, k, v, grad, o, lse, g, mixed, keys=256, queries=1024):
+    units = lax.axis_size("dp")
+    docs, (total, width) = lengths.shape[0], q.shape
+    seq, pairs = total // docs, width // 128
+    columns = g.shape[1]
+    own = g.shape[0] // (2 * units)
+    slab = pl.BlockSpec((seq, 128), lambda p, d: (d, p))
+    return pl.pallas_call(
+        functools.partial(
+            back_send_kernel, keys=keys, queries=min(queries, seq), steps=pairs * docs
+        ),
+        grid=(pairs, docs),
+        in_specs=[
+            SMEM,
+            SMEM,
+            slab,
+            slab,
+            slab,
+            slab,
+            slab,
+            pl.BlockSpec((1, 1, 2, seq), lambda p, d: (d, p, 0, 0)),
+            ANY,
+            ANY,
+        ],
+        out_specs=[
+            slab,
+            slab,
+            slab,
+            pl.BlockSpec((2, 32, SUB), lambda p, d: (p, 0, 0)),
+            whole((own, columns)),
+            ANY,
+        ],
+        out_shape=[struct((total, width))] * 3
+        + [
+            struct((2 * pairs, 32, SUB), f32),
+            struct((own, columns), f32),
+            struct((2 * docs, seq // 2, width)),
+        ],
+        scratch_shapes=[
+            pltpu.VMEM((2, 3, SUB, SUB), f32),
+            pltpu.VMEM((2, 3, SUB, SUB), f32),
+            pltpu.VMEM((2, 2, 8, SUB), f32),
+            pltpu.VMEM((seq, 128), f32),
+            pltpu.VMEM(g.shape, low_type),
+            pltpu.VMEM((docs, seq // 2, width), low_type),
+            pltpu.VMEM((CHUNKS, own, columns // CHUNKS), f32),
+        ]
+        + Scatter.scratch(own, columns // CHUNKS, units, (CHUNKS,))
+        + [DMA, DMA((2, docs)), DMA((2, docs))],
+        compiler_params=comm_params(4),
+        name="attend_back",
+    )(lengths, table, q, k, v, grad, o, lse, g, mixed.reshape(docs, seq, width))
 
 
 def end_kernel(
@@ -895,166 +1484,227 @@
     mid_ref,
     w_ref,
     gain_ref,
-    gn_second_ref,
     table_ref,
+    wq_ref,
+    wk_ref,
+    wv_ref,
+    w_in_ref,
+    g_hidden_ref,
+    g_out,
     gw_ref,
     gt_ref,
     small_ref,
+    gains_ref,
     rows_in,
-    acc,
+    low_all,
     grads,
     gt,
-    core_buf,
-    x_send,
-    x_buf,
-    z_send,
-    z_buf,
-    y_send,
-    y_buf,
-    core_sem,
-    x_sem,
-    z_sem,
-    y_sem,
-    small_send,
-    small_recv,
-    small_sem,
-    load_sem,
-    gt_sem,
+    *rest,
 ):
     place = Place()
     count, rows, width = gt_ref.shape
     per = count // 2
     seq = 2 * rows
-    scatter = Scatter(
-        place,
-        grads,
-        (core_buf, x_send, x_buf, z_send, z_buf, y_send, y_buf),
-        (core_sem, x_sem, z_sem, y_sem),
-    )
+    scatter_refs, kept = rest[:11], rest[11]
+    small_send, small_recv, small_sem, load_sem, gt_sem = rest[12:]
     exchange = Exchange(place, small_send, small_recv, small_sem)
     sources = (x_ref, dq_ref, dk_ref, dv_ref, mid_ref)
 
+    def scatter(at):
+        return Scatter(place, grads.at[at], [ref.at[at] for ref in scatter_refs])
+
     def load(block, index):
-        y = 1 - place.y if block < per else place.y
-        begin = pl.multiple_of(block % per * seq + y * rows, 16)
+        y = jnp.where(block < per, 1 - place.y, place.y)
+        begin = pl.multiple_of(lax.rem(block, per) * seq + y * rows, 16)
         return pltpu.make_async_copy(
-            sources[index].at[pl.ds(begin, rows)], rows_in.at[block, index], load_sem.at[block, index]
-        )
-
-    def give(block):
-        target = gt_ref.at[place.y * per + block % per]
-        if block < per:
-            return remote(
-                gt.at[block], target, gt_sem.at[0, block], gt_sem.at[1, block], place.over_y()
-            )
-        return pltpu.make_async_copy(gt.at[block], target, gt_sem.at[0, block])
-
-    for block in range(2 * per):
-        for index in range(5):
+            sources[index].at[pl.ds(begin, rows)],
+            rows_in.at[index, block],
+            load_sem.at[block, index],
+        )
+
+    def give_away(block):
+        return remote(
+            gt.at[block],
+            gt_ref.at[place.y * per + block],
+            gt_sem.at[0, block],
+            gt_sem.at[1, block],
+            place.over_y(),
+        )
+
+    def give_home(block):
+        return pltpu.make_async_copy(
+            gt.at[block], gt_ref.at[place.y * per + block - per], gt_sem.at[0, block]
+        )
+
+    take = pltpu.make_async_copy(g_out, grads.at[0], load_sem.at[2 * per, 0])
+    for index in range(5):
+        load(0, index).start()
+    take.start()
+    for index in range(5):
+        for block in range(1, 2 * per):
             load(block, index).start()
     place.greet()
     gain = gain_ref[0:1]
-    gain_sum = []
-
-    def normed_of(block):
-        return norm_rows(rows_in[block, 0].astype(f32))
+    take.wait()
+    scatter(0).start()
+    heads, buckets = table_ref.shape[:2]
+    small_send[0] = jnp.zeros(small_ref.shape, f32)
+    small_send[0, :heads, :buckets] = jnp.sum(table_ref[...], 2)
+    exchange.copy(0).start()
+    chunk = g_hidden_ref.shape[1] // (2 * CHUNKS)
+    sum_second = jnp.zeros((gains_ref.shape[0], chunk), f32)
+    for at in range(CHUNKS):
+        sum_second += (
+            g_hidden_ref[:, 2 * at * chunk : (2 * at + 1) * chunk]
+            * w_in_ref[:, at * chunk : (at + 1) * chunk].astype(f32)
+        )
+    rounds = len(exchange.targets)
+
+    def exchange_round(at):
+        value = exchange.finish(at)
+        if at < rounds - 1:
+            exchange.start(at + 1, value)
+        else:
+            small_ref[...] = value
+
+    def low_rows(block, _):
+        @pl.when(block > 0)
+        def _():
+            load(block, 0).wait()
+
+        normed, _ = norm_rows(rows_in[0, block].astype(f32))
+        low_all[block] = (normed * gain).astype(low_type)
+        return 0
 
     def rows_back(block):
-        normed, inverse = normed_of(block)
+        normed, inverse = norm_rows(rows_in[0, block].astype(f32))
         normed_grad = None
         for index in range(3):
             part = dot(
-                rows_in[block, 1 + index], w_ref[:, index * width : (index + 1) * width], NT
+                rows_in[1 + index, block], w_ref[:, index * width : (index + 1) * width], NT
             )
             normed_grad = part if normed_grad is None else normed_grad + part
-        gain_sum.append(jnp.sum((normed_grad * normed).reshape(rows // 8, 8, width), 0))
         scaled = normed_grad * gain
         inner = jnp.mean(scaled * normed, -1, keepdims=True)
-        mid = rows_in[block, 4].astype(f32)
+        mid = rows_in[4, block].astype(f32)
         gt[block] = (mid + inverse * (scaled - normed * inner)).astype(low_type)
-        give(block).start()
-
-    def weights_back(block, last):
-        normed, _ = normed_of(block)
-        low = (normed * gain).astype(low_type)
-        for index in range(3):
-            span = slice(index * width, (index + 1) * width)
-            part = dot(low, rows_in[block, 1 + index], TN)
-            if block:
-                part = part + acc[:, span]
-            if last:
-                grads[:, span] = part.astype(low_type)
-            else:
-                acc[:, span] = part
-
-    for block in range(2 * per):
-        for index in range(5):
+
+        @pl.when(block < per)
+        def _():
+            give_away(block).start()
+
+        @pl.when(block >= per)
+        def _():
+            give_home(block).start()
+
+    def weights_back(at):
+        grads[at] = dot(
+            low_all[...].reshape(2 * per * rows, width),
+            rows_in[at].reshape(2 * per * rows, width),
+            TN,
+        ).astype(low_type)
+        scatter(at).start()
+
+    def during(at, first, last, work):
+        @pl.when((at >= first) & (at <= last))
+        def _():
+            work(at)
+
+    def x_stages(at):
+        for hop in place.hops + [0]:
+            scatter(at).stage_x(hop)
+
+    def z_stages(at):
+        for hop in place.hops + [0]:
+            scatter(at).stage_z(hop)
+
+    def y_stage(at):
+        kept[at] = scatter(at).stage_y()
+
+    def finish(at):
+        gw_ref[at] = scatter(at).finish(kept[at])
+
+    def project_step(at, _):
+        weights_back(at)
+        x_stages(at - 1)
+        for index in range(2):
+            during(at, index + 2, index + 2, lambda _, index=index: exchange_round(index))
+        return 0
+
+    def rows_step(block, _):
+        rows_back(block)
+        during(block, 1, 1, lambda _: x_stages(3))
+        during(block, 1, 1, lambda _: z_stages(0))
+        during(block, 1, 3, z_stages)
+        during(block - 2, 0, 0, y_stage)
+        during(block - 1, 1, 2, y_stage)
+        during(block - 3, 0, 0, finish)
+        for index in range(2, rounds):
+            during(block, index - 1, index - 1, lambda _, index=index: exchange_round(index))
+        return 0
+
+    for index in range(5):
+        load(0, index).wait()
+    rows_back(0)
+    lax.fori_loop(0, 2 * per, low_rows, 0)
+    for index in range(1, 5):
+        for block in range(1, 2 * per):
             load(block, index).wait()
-        if block < per:
-            rows_back(block)
-        weights_back(block, block == 2 * per - 1)
-    scatter.start()
-    rows_back(per)
-    order = scatter.order
-    for hop in order[:2]:
-        scatter.stage_x(hop)
-    for block in range(per + 1, 2 * per):
-        rows_back(block)
-    for hop in order[2:]:
-        scatter.stage_x(hop)
-    gain_row = jnp.sum(sum(gain_sum[1:], gain_sum[0]), 0, keepdims=True)
-    lines = [table_ref[...]]
-    for row in (gain_row, gn_second_ref[...]):
-        lines += [row[:, at : at + 128] for at in range(0, width, 128)]
-    gap = small_ref.shape[0] - sum(line.shape[0] for line in lines)
-    if gap:
-        lines.append(jnp.zeros((gap, 128), f32))
-    exchange.start(0, jnp.concatenate(lines, 0))
-    rounds = len(exchange.targets)
-    at = 0
-    for hop in order:
-        scatter.stage_z(hop)
-        if at < rounds - 1:
-            exchange.start(at + 1, exchange.finish(at))
-            at += 1
-    kept = scatter.stage_y()
-    while at < rounds - 1:
-        exchange.start(at + 1, exchange.finish(at))
-        at += 1
-    small_ref[...] = exchange.finish(at)
-    gw_ref[...] = scatter.finish(kept)
-    scatter.drain()
-    for block in range(2 * per):
-        give(block).wait()
-
-
-def end_call(x, dq, dk, dv, mid, w_first, gains, gn_second, table, docs, ways):
+    lax.fori_loop(1, 4, project_step, 0)
+    lax.fori_loop(1, 2 * per, rows_step, 0)
+    y_stage(3)
+    finish(1)
+    finish(2)
+    finish(3)
+    sum_first = jnp.zeros((gains_ref.shape[0], width), f32)
+    for at, ref in enumerate((wq_ref, wk_ref, wv_ref)):
+        sum_first += gw_ref[1 + at] * ref[...].astype(f32)
+    lane = lax.broadcasted_iota(jnp.int32, (1, 128), 1)
+    gains_ref[...] = jnp.where(
+        lane == 0,
+        jnp.sum(sum_first, 1, keepdims=True),
+        jnp.sum(sum_second, 1, keepdims=True),
+    )
+
+    def drain(at, _):
+        scatter(at).drain()
+        return 0
+
+    lax.fori_loop(0, 4, drain, 0)
+    for block in range(per):
+        give_away(block).wait()
+        give_home(per + block).wait()
+
+
+def end_call(x, dq, dk, dv, mid, w_first, gains, table, own_weights, g_hidden, g_out, docs, ways):
     units = lax.axis_size("dp")
     total, width = x.shape
     own = width // (units * ways)
     rows = total // (docs * ways)
-    small = (table.shape[0] + -(-2 * (width // 128) // 8) * 8, 128)
+    small = (table.shape[0] + -table.shape[0] % 8, 128)
     return pl.pallas_call(
         end_kernel,
-        in_specs=[ANY] * 5 + [VMEM_WHOLE] * 4,
-        out_specs=[VMEM_WHOLE, ANY, VMEM_WHOLE],
+        in_specs=[ANY] * 5 + [VMEM_WHOLE] * 8 + [ANY],
+        out_specs=[VMEM_WHOLE, ANY, VMEM_WHOLE, VMEM_WHOLE],
         out_shape=[
-            struct((own, 3 * width), f32),
+            struct((4, own, width), f32),
             struct((docs * ways, rows, width)),
             struct(small, f32),
+            struct((own, 128), f32),
         ],
         scratch_shapes=[
-            pltpu.VMEM((docs * ways, 5, rows, width), low_type),
-            pltpu.VMEM((width, 3 * width), f32),
-            pltpu.VMEM((width, 3 * width), low_type),
+            pltpu.VMEM((5, docs * ways, rows, width), low_type),
+            pltpu.VMEM((docs * ways, rows, width), low_type),
+            pltpu.VMEM((4, width, width), low_type),
             pltpu.VMEM((docs * ways, rows, width), low_type),
         ]
-        + Scatter.scratch(own, 3 * width, units)
+        + Scatter.scratch(own, width, units, (4,))
+        + [pltpu.VMEM((4, own, width), f32)]
         + Exchange.scratch(small, units)
-        + [DMA((docs * ways, 5)), DMA((2, docs * ways))],
+        + [DMA((docs * ways + 1, 5)), DMA((2, docs * ways))],
         compiler_params=comm_params(2),
         name="end",
-    )(x, dq, dk, dv, mid, w_first, gains, gn_second, table)
+    )(x, dq, dk, dv, mid, w_first, gains, table, *own_weights, g_hidden, g_out)
 
 
 def sharing(count):
@@ -1137,25 +1787,27 @@
     both = ("dp", "blk")
     direct = lax.axis_size("blk") == 2 and per * 2 == count and lax.axis_size("dp") % 4 == 0
     gains = jnp.pad(jnp.stack([norm1_gain, norm2_gain], 1), ((0, 0), (0, SPARE - 2)))
-    shard_first = jnp.concatenate([w_query, w_key, w_value, gains], 1)
-    shard_second = jnp.concatenate([w_out, w_in, w_down], 1)
-    w_second = lax.all_gather(shard_second, both, axis=0, tiled=True)
+    firsts, seconds = (w_query, w_key, w_value), (w_out, w_in, w_down)
     tokens_here = tokens.reshape(count, rows, width)
     cot_here = cotangent.reshape(count, rows, width)
     if direct:
-        q, k, v, x, w_first, gain_rows = first_call(shard_first, tokens_here, 2)
+        q, k, v, x, w_first, gain_rows, pair = first_call(
+            firsts, gains, seconds, tokens_here, 2
+        )
         x = x.reshape(-1, width)
-        cot_here, x = lax.optimization_barrier((cot_here, x))
     else:
-        w_first = lax.all_gather(shard_first, both, axis=0, tiled=True)
+        pair = None
+        w_second = lax.all_gather(second_pieces(*seconds), both, axis=0, tiled=True)
+        w_first = lax.all_gather(
+            jnp.concatenate(firsts + (gains,), 1), both, axis=0, tiled=True
+        )
         x = to_documents(tokens_here)
         gain_rows = w_first[:, 3 * width : 3 * width + 2].astype(f32).T
-    cot = to_documents(cot_here)
     gain_first, gain_second = gain_rows[:1], gain_rows[1:2]
     own = lax.dynamic_slice_in_dim(
         lengths.reshape(count), lax.axis_index("blk") // share * per, per, 0
     )
-    x_rows, cot_rows = my_share(x, share, 0), my_share(cot, share, 0)
+    x_rows = my_share(x, share, 0)
     own_rows, w_heads = own, w_first
     if share > 1:
         own_rows = own - lax.rem(lax.axis_index("blk"), share) * x_rows.shape[0]
@@ -1164,30 +1816,50 @@
         )
     table = my_share((rel_table * LOG2E).T, share, 0)
 
-    if not direct:
+    if direct:
+        ahead = width + AHEAD * 2 * (w_in.shape[1] // CHUNKS)
+        heads, lse, w_second, cot = attend_send_call(
+            own, table, q, k, v, pair, ahead, cot_here
+        )
+        cot = cot.reshape(-1, width)
+    else:
         q, k, v = qkv_call(x, gain_first, w_heads, width // share)
-    heads, lse = attend_call(own, table, q, k, v)
-    mixed, heads_grad, mid, g_second, gn_second = middle_call(
-        own_rows, x_rows, among(heads, share, 0, 1), cot_rows, gain_second, w_second
+        heads, lse = attend_call(own, table, q, k, v)
+        cot = my_share(to_documents(cot_here), share, 0)
+    mixed, heads_grad, mid, g_out, g_hidden, gn_second = middle_call(
+        own_rows, x_rows, among(heads, share, 0, 1), cot, gain_second, w_second, pair if AHEAD < CHUNKS else None
     )
-    mixed = from_documents(mixed, count)
-    g_second = lax.psum_scatter(g_second, both, scatter_dimension=0, tiled=True).astype(f32)
-    dq, dk, dv, table_sum = attend_back_call(
-        own, table, q, k, v, among(heads_grad, share, 1, 0), heads, lse
-    )
+    if direct:
+        dq, dk, dv, table_sum, g_hidden, mixed = back_send_call(
+            own, table, q, k, v, heads_grad, heads, lse, g_hidden, mixed
+        )
+    else:
+        dq, dk, dv, table_sum = attend_back_call(
+            own, table, q, k, v, among(heads_grad, share, 1, 0), heads, lse
+        )
+        mixed = from_documents(mixed, count)
+        g_out = lax.psum_scatter(g_out, both, scatter_dimension=0, tiled=True).astype(f32)
+        g_hidden = lax.psum_scatter(g_hidden, both, scatter_dimension=0, tiled=True).astype(f32)
     dq, dk, dv = (among(grad, share, 0, 1) for grad in (dq, dk, dv))
-    table_sum = jnp.sum(table_sum, 2)
     head_count, bucket_count = rel_table.shape[1], rel_table.shape[0]
-    index = lax.axis_index("dp") * lax.axis_size("blk") + lax.axis_index("blk")
-    own_gain = norm1_gain.shape[0]
     if direct:
-        table_sum = jnp.pad(table_sum, ((0, -head_count % 8), (0, SUB - bucket_count)))
-        g_first, grad_tokens, small = end_call(
-            x, dq, dk, dv, mid, w_first, gain_rows, gn_second, table_sum, per, 2
+        g_first, grad_tokens, small, gains = end_call(
+            x,
+            dq,
+            dk,
+            dv,
+            mid,
+            w_first,
+            gain_rows,
+            table_sum,
+            firsts + (w_in,),
+            g_hidden,
+            g_out,
+            per,
+            2,
         )
         grad_table = small[:head_count, :bucket_count].T
-        gains = small[table_sum.shape[0] :][: 2 * (width // 128)].reshape(2, width)
-        gains = lax.dynamic_slice_in_dim(gains, index * own_gain, own_gain, 1)
+        gains = (gains[:, 0] / norm1_gain.astype(f32), gains[:, 1] / norm2_gain.astype(f32))
     else:
         grad_tokens, g_first, gn_first = last_call(
             x_rows, dq, dk, dv, mid, gain_first, w_first
@@ -1197,16 +1869,20 @@
         gains = lax.psum_scatter(
             jnp.concatenate([gn_first, gn_second], 0), both, scatter_dimension=1, tiled=True
         )
+        table_sum = jnp.sum(table_sum, 2)
         if share > 1:
             at = lax.rem(lax.axis_index("blk"), share) * table_sum.shape[0]
             table_sum = lax.dynamic_update_slice_in_dim(
                 jnp.zeros(rel_table.T.shape, f32), table_sum, at, 0
             )
         grad_table = lax.psum(table_sum, both).T
-    grad_query, grad_key, grad_value = (
-        g_first[:, i * width : (i + 1) * width] for i in range(3)
-    )
-    hidden = w_in.shape[1]
+    if direct:
+        g_out, grad_query, grad_key, grad_value = g_first
+    else:
+        grad_query, grad_key, grad_value = (
+            g_first[:, i * width : (i + 1) * width] for i in range(3)
+        )
+    grad_in, grad_down = split_hidden(g_hidden)
     return (
         mixed.reshape(tokens.shape),
         grad_tokens.reshape(tokens.shape),
@@ -1214,11 +1890,11 @@
         grad_query,
         grad_key,
         grad_value,
-        g_second[:, :width],
+        g_out,
         grad_table,
         gains[1],
-        g_second[:, width : width + hidden],
-        g_second[:, width + hidden :],
+        grad_in,
+        grad_down,
     )
 
 

time: 416 us -> 394 us (0.947)
  local copies, waits for them, and re-layouts: 26.3 us -> 12.8 us
  between operations: 14.6 us -> 1.19 us
  Pallas kernels: 361 us -> 369 us
    pallas_call x5, Pallas kernels: 361 us -> 369 us  [the longest x1 100 us: middle_call(): pl.pallas_call(functools.partial(kernel, seq=total // lengths.shape[0]),...]
    dynamic_update_slice x3 -> x0, local copies, waits for them, and re-layouts: 5.15 us -> none  [the longest x2 3.9 us: from_documents(): out = lax.dynamic_update_slice_in_dim(out, piece, source * per, 0)]
  transfers between devices with their start and end apart: 4 -> 0, of which waited for: 0 -> 0; matrix products, arithmetic and copies ran while one was open for 5% -> 0% of each run, Pallas kernels for 68% -> 0%
where the time goes in v4:
time: 394 us; the launch traced here: 387 us
  Pallas kernels  369 us (94%)
  local copies, waits for them, and re-layouts  12.8 us (3%)
    pallas_call x1, Pallas kernels, middle_call(): pl.pallas_call(functools.partial(kernel, seq=total // lengths.shape[0]),...  100 us
    pallas_call x1, Pallas kernels, back_send_call(): pl.pallas_call(functools.partial(back_send_kernel, keys=keys, queries=min...  97.7 us
    pallas_call x1, Pallas kernels, end_call(): pl.pallas_call(end_kernel, in_specs=[ANY] * 5 + [VMEM_WHOLE] * 8 + [ANY],...  60.3 us
    pallas_call x1, Pallas kernels, first_call(): pl.pallas_call(kernel, in_specs=[VMEM_WHOLE] * (len(firsts) + 1 + len(sec...  56.5 us
    pallas_call x1, Pallas kernels, attend_send_call(): pl.pallas_call(functools.partial(attend_send_kernel, rows=rows), grid=(pa...  54.6 us

profile of v4, /device:TPU:0, one launch (start us, length us, event | category | flops | bytes accessed | tf_op | source)
XLA Modules:
  0.0 386.7 jit_solution(15050552370539003705)
XLA Ops:
  0.6 0.0 copy-start
  0.7 0.6 copy-done
  1.3 0.6 dynamic-slice_bitcast_fusion.len_ref.refs_0_
  1.9 0.7 pad_maximum_fusion.2
  2.6 0.1 copy.31
  2.7 0.6 pad.4.refs_3_
  3.3 1.3 multiply_bitcast_fusion.table_ref
  4.6 56.5 %first.1 = (bf16[2048,768]{1,0:T(8,128)(2,1)}, bf16[2048,768]{1,0:T(8,128)(2,1)}, bf16[2048,768]{1,0:T(8,128)(2,1)}, bf16[2,1024,768]{2,1,0:T(8,128)(2,1)}, bf16...) custom-call(bf16[24,768]{1,0:T(8,128)(2,1)} %wq_ref.1, bf16[24,768]{1,0:T(8,128)(2,1)} %wk_ref.1, ...), custom_call_target="tpu_custom_call" | custom-call | tf_op jit(solution)/shard_map/first/pallas_call | solution.py:1139
  61.1 1.3 slice.36.refs_4_
  62.4 54.6 %attend.1 = (bf16[2048,768]{1,0:T(8,128)(2,1)}, f32[2,6,2,1024]{3,2,1,0:T(2,128)}, bf16[768,3840]{1,0:T(8,128)(2,1)}, bf16[2,1024,768]{2,1,0:T(8,128)(2,1)}) custom-call(s32[2]{0:T(128)} %dynamic-slice_bitcast_fusion.len_ref.refs_0_, f32[12,32]{1,0:T(8,128)} %multiply_bitcast_fusion.table_ref, bf16[2048,768]{1,0:T(8,128)(2,1)} %get-tuple-element.37.q_ref, ...), custom_call_target="tpu_custom_call" | custom-call | tf_op jit(solution)/shard_map/attend/pallas_call | solution.py:1257
  117.1 100.1 %middle.1 = (bf16[2048,768]{1,0:T(8,128)(2,1)}, bf16[2048,768]{1,0:T(8,128)(2,1)}, bf16[2048,768]{1,0:T(8,128)(2,1)}, bf16[768,768]{1,0:T(8,128)(2,1)}, bf16[768,6144]{1,0:T(8,128)(2,1)}, /*index=5*/f32[1,768]{1,0:T(1,128)}) custom-call(s32[2]{0:T(128)} %dynamic-slice_bitcast_fusion.len_ref.refs_0_, bf16[2048,768]{1,0:T(8,128)(2,1)} %bitcast.27, ...), custom_call_target="tpu_custom_call" | custom-call | tf_op jit(solution)/shard_map/middle/pallas_call | solution.py:417
  217.1 97.7 %attend_back.1 = (bf16[2048,768]{1,0:T(8,128)(2,1)}, bf16[2048,768]{1,0:T(8,128)(2,1)}, bf16[2048,768]{1,0:T(8,128)(2,1)}, f32[12,32,128]{2,1,0:T(8,128)}, f32[2...) custom-call(s32[2]{0:T(128)} %dynamic-slice_bitcast_fusion.len_ref.refs_0_, f32[12,32]{1,0:T(8,128)} %multiply_bitcast_fusion.table_ref, ...), custom_call_target="tpu_custom_call" | custom-call | tf_op jit(solution)/shard_map/attend_back/pallas_call | solution.py:1432
  314.9 0.0 copy-start.4
  314.9 0.0 copy-start.5
  314.9 0.0 copy-start.3
  314.9 60.3 %end.1 = (f32[4,24,768]{2,1,0:T(8,128)}, bf16[4,512,768]{2,1,0:T(8,128)(2,1)}, f32[16,128]{1,0:T(8,128)}, f32[24,128]{1,0:T(8,128)}) custom-call(bf16[2048,768]{1,0:T(8,128)(2,1)} %bitcast.28, bf16[2048,768]{1,0:T(8,128)(2,1)} %get-tuple-element.51.dq_ref, bf16[2048,768]{1,0:T(8,128)(2,1)} %get-tuple-element.52.dk_ref, ...), custom_call_target="tpu_custom_call" | custom-call | tf_op jit(solution)/shard_map/end/pallas_call | solution.py:1685
  375.2 1.0 slice_reduce_fusion
  376.2 0.0 copy-done.4
  376.2 0.0 copy-done.5
  376.2 0.5 convert_divide_fusion
  376.7 1.3 slice_bitcast_fusion.4
  378.0 1.7 slice_bitcast_fusion
  379.7 0.0 copy-done.3
  379.8 0.9 pad_maximum_fusion
  380.6 0.0 copy-start.2
  380.6 0.0 copy-start.1
  380.6 3.9 %copy.36 = bf16[4,1,512,768]{3,2,1,0:T(8,128)(2,1)} copy(bf16[4,1,512,768]{3,2,1,0:T(8,128)(2,1)} %bitcast.31) | data formatting | bytes 6291456
  384.5 0.0 copy-done.2
  384.5 1.7 copy.37
  386.2 0.0 copy-done.1
  (1 shorter events, 0.0 us)
Async XLA Ops:
  0.6 0.7 copy-start
  314.9 61.3 %copy-start.4 = (bf16[24]{0:T(256)(128)(2,1)S(1)}, bf16[24]{0:T(256)(128)(2,1)}, u32[]{:S(2)}) copy-start(bf16[24]{0:T(256)(128)(2,1)} %param.20) | copy-start | bytes 148
  314.9 61.3 %copy-start.5 = (bf16[24]{0:T(256)(128)(2,1)S(1)}, bf16[24]{0:T(256)(128)(2,1)}, u32[]{:S(2)}) copy-start(bf16[24]{0:T(256)(128)(2,1)} %param.14) | copy-start | bytes 148
  314.9 64.8 %copy-start.3 = (f32[24,6144]{1,0:T(8,128)S(1)}, f32[24,6144]{1,0:T(8,128)}, u32[]{:S(2)}) copy-start(f32[24,6144]{1,0:T(8,128)} %get-tuple-element.57.g_hidden_ref) | copy-start | bytes 1769476
  380.6 3.9 %copy-start.2 = (bf16[4,512,768]{2,1,0:T(8,128)(2,1)S(1)}, bf16[4,512,768]{2,1,0:T(8,128)(2,1)}, u32[]{:S(2)}) copy-start(bf16[4,512,768]{2,1,0:T(8,128)(2,1)} %get-tuple-element.59) | copy-start | bytes 9437188
  380.6 5.6 %copy-start.1 = (s32[4,1]{0,1:T(1,128)S(1)}, s32[4,1]{0,1:T(1,128)}, u32[]{:S(2)}) copy-start(s32[4,1]{0,1:T(1,128)} %param.13) | copy-start | bytes 52
